TPU v7x, 32 devices: a whole 2x2x4 slice. The times are simulated.
32 devices in a mesh: dp: 8 (over z, y), tensor: 4 (over x, core).
Axes of the slice: x: 2, y: 2, z: 4, core: 2. Of those that a mesh axis runs over, the one named last changes fastest.
Arguments:
- h_in: bfloat16 [8192, 768], P(('dp', 'tensor')), may hold values from -6 to 6
- g_in: bfloat16 [8192, 768], P(('dp', 'tensor')), may hold values from -6 to 6
- lengths: int32 [16, 4], P('dp'), may hold values from 1 to 384, 512 in all within a row
- order: int32 [16, 512], P('dp'), may hold values from 0 to 511, each once within a row
- predicted: int32 [16, 512], P('dp'), may hold values 0 or 1
- w_query: bfloat16 [2, 768, 768], P(None, 'dp', 'tensor'), may hold values from -0.21875 to 0.21875
- w_key: bfloat16 [2, 768, 768], P(None, 'dp', 'tensor'), may hold values from -0.21875 to 0.21875
- w_value: bfloat16 [2, 768, 768], P(None, 'dp', 'tensor'), may hold values from -0.21875 to 0.21875
- w_out: bfloat16 [2, 768, 768], P(None, 'tensor', 'dp'), may hold values from -0.625 to 0.625
- w_up: bfloat16 [2, 768, 3072], P(None, 'dp', 'tensor'), may hold values from -0.21875 to 0.21875
- w_down: bfloat16 [2, 3072, 768], P(None, 'tensor', 'dp'), may hold values from -0.109375 to 0.109375
- q_bias: float32 [2, 768], P(None, 'tensor'), may hold values from -3 to 3
- v_bias: float32 [2, 768], P(None, 'tensor'), may hold values from -3 to 3
- up_bias: float32 [2, 3072], P(None, 'tensor'), may hold values from -3 to 3
- rel_table: float32 [2, 12, 32], P(None, 'tensor'), may hold values from -4 to 4
- norm_gain: float32 [2, 2, 768], replicated, may hold values from 0.5 to 1.5
- norm_shift: float32 [2, 2, 768], replicated, may hold values from -2 to 2
- out_bias: float32 [2, 2, 768], replicated, may hold values from -2 to 2
- h_cot: bfloat16 [8192, 768], P(('dp', 'tensor')), may hold values from -6 to 6
- g_cot: bfloat16 [8192, 768], P(('dp', 'tensor')), may hold values from -6 to 6
Outputs:
- h_out: bfloat16 [8192, 768], P(('dp', 'tensor'))
- g_out: bfloat16 [8192, 768], P(('dp', 'tensor'))
- h_grad: bfloat16 [8192, 768], P(('dp', 'tensor'))
- g_grad: bfloat16 [8192, 768], P(('dp', 'tensor'))
- w_query_grad: float32 [2, 768, 768], P(None, 'dp', 'tensor')
- w_key_grad: float32 [2, 768, 768], P(None, 'dp', 'tensor')
- w_value_grad: float32 [2, 768, 768], P(None, 'dp', 'tensor')
- w_out_grad: float32 [2, 768, 768], P(None, 'tensor', 'dp')
- w_up_grad: float32 [2, 768, 3072], P(None, 'dp', 'tensor')
- w_down_grad: float32 [2, 3072, 768], P(None, 'tensor', 'dp')
- q_bias_grad: float32 [2, 768], P(None, 'tensor')
- v_bias_grad: float32 [2, 768], P(None, 'tensor')
- up_bias_grad: float32 [2, 3072], P(None, 'tensor')
- rel_table_grad: float32 [2, 12, 32], P(None, 'tensor')
- norm_gain_grad: float32 [2, 2, 768], replicated
- norm_shift_grad: float32 [2, 2, 768], replicated
- out_bias_grad: float32 [2, 2, 768], replicated
Inputs may be any that keep to these rules, and one draw needn't show every extreme that they name: Row s lists the lengths of the 3 documents of slot s in order and, last, the slot's padding; each row sums to 512. `order`: each row is a permutation of 0 to 511.
All inputs are finite; a program needn't handle non-finite values. No bound on the sum of `predicted` on one device may be relied on, other than what follows from the above.
Results may differ from a plain program's by a relative error of at most 0.03.
Values may be sent and summed in bfloat16 or wider, within the bound.
No kernel may reach another device: no remote copies, remote signals or barrier semaphores. Data moves between devices by JAX's collectives and lax.ppermute only.
A program may use at most 192 MiB of HBM per device.

v0:
```python
import jax
import jax.numpy as jnp
from jax import lax
from jax.sharding import PartitionSpec as P

HEAD = 64
BUCKETS = 32
LAYERS = 2
SEQ = 512


epsilon = 1e-05
limits = (12, 16, 23, 32, 46, 64, 91)
highest = lax.Precision.HIGHEST
contract_rows = (((0,), (0,)), ((), ()))
contract_cols = (((1,), (1,)), ((), ()))
contract_plain = (((1,), (0,)), ((), ()))


def matmul(left, right):
    return jnp.dot(left, right, preferred_element_type=jnp.float32)


def over_rows(left, right):
    return lax.dot_general(left, right, contract_rows, preferred_element_type=jnp.float32)


def over_cols(left, right):
    return lax.dot_general(left, right, contract_cols, preferred_element_type=jnp.float32)


def bucket_of(offset):
    distance = jnp.abs(offset)
    farther = 8 + sum(((distance >= border).astype(jnp.int32) for border in limits))
    return jnp.where(distance < 8, distance, farther) + 16 * (offset > 0).astype(jnp.int32)


def slot_masks(piece_lengths, ranks, chosen):
    places = jnp.arange(SEQ, dtype=jnp.int32)
    borders = jnp.cumsum(piece_lengths)[:-1]
    segment = jnp.sum((places[:, None] >= borders[None, :]).astype(jnp.int32), axis=1)
    starts = jnp.concatenate([jnp.zeros((1,), jnp.int32), borders])
    pieces = jnp.arange(starts.shape[0], dtype=jnp.int32)
    leading = jnp.sum(jnp.where(segment[:, None] == pieces[None, :], starts[None, :], 0), axis=1)
    same_doc = segment[:, None] == segment[None, :]
    visible = chosen[None, :] == 0
    content_mask = same_doc & (visible | (ranks[None, :] <= ranks[:, None]))
    query_mask = same_doc & (
        (places[None, :] == leading[:, None])
        | visible & (places[None, :] != places[:, None])
        | (ranks[None, :] < ranks[:, None])
    )
    return (content_mask, query_mask)


def norm_rows(rows, gain, shift):
    center = rows - jnp.mean(rows, axis=-1, keepdims=True)
    spread = jnp.mean(center * center, axis=-1, keepdims=True)
    return center * lax.rsqrt(spread + epsilon) * gain + shift


def norm_back(rows, gain, shift, grad):
    unused, pull = jax.vjp(norm_rows, rows, gain, shift)
    return pull(grad)


def smooth(inner):
    return jax.nn.gelu(inner, approximate=True)


def smooth_back(inner, grad):
    unused, pull = jax.vjp(smooth, inner)
    return pull(grad)[0]


def masked_scores(queries, keys, allowed, bias):
    scores = (
        jnp.einsum("qhe,khe->hqk", queries, keys, preferred_element_type=jnp.float32) * 0.125 + bias
    )
    return jnp.where(allowed[None], scores, -1e30)


def attend(queries, keys, values, allowed, bias):
    scores = masked_scores(queries, keys, allowed, bias)
    maxima = jnp.max(scores, axis=-1, keepdims=True)
    raised = jnp.exp(scores - maxima)
    total = jnp.sum(raised, axis=-1, keepdims=True)
    probs = (raised / total).astype(jnp.bfloat16)
    result = jnp.einsum("hqk,khe->qhe", probs, values, preferred_element_type=jnp.float32)
    return (result.astype(jnp.bfloat16), (maxima + jnp.log(total))[..., 0])


def attend_back(queries, keys, values, allowed, bias, logsum, grad_out):
    scores = masked_scores(queries, keys, allowed, bias)
    probs = jnp.where(allowed[None], jnp.exp(scores - logsum[..., None]), 0.0)
    grad_probs = jnp.einsum("qhe,khe->hqk", grad_out, values, preferred_element_type=jnp.float32)
    inner = jnp.sum(probs * grad_probs, axis=-1, keepdims=True)
    grad_scores = (probs * (grad_probs - inner)).astype(jnp.bfloat16)
    grad_query = (
        jnp.einsum("hqk,khe->qhe", grad_scores, keys, preferred_element_type=jnp.float32) * 0.125
    )
    grad_keys = (
        jnp.einsum("hqk,qhe->khe", grad_scores, queries, preferred_element_type=jnp.float32) * 0.125
    )
    grad_values = jnp.einsum(
        "hqk,qhe->khe", probs.astype(jnp.bfloat16), grad_out, preferred_element_type=jnp.float32
    )
    return (grad_query, grad_keys, grad_values, grad_scores)


def fetch_weights(query_w, key_w, value_w, up_w, out_w, down_w):
    return (
        lax.all_gather(query_w, "dp", axis=0, tiled=True),
        lax.all_gather(key_w, "dp", axis=0, tiled=True),
        lax.all_gather(value_w, "dp", axis=0, tiled=True),
        lax.all_gather(up_w, "dp", axis=0, tiled=True),
        lax.all_gather(out_w, "dp", axis=1, tiled=True),
        lax.all_gather(down_w, "dp", axis=1, tiled=True),
    )


def fetch_again(query_w, key_w, value_w, up_w, out_w, down_w):
    return (
        lax.all_gather(query_w, "dp", axis=0, tiled=True),
        lax.all_gather(key_w, "dp", axis=0, tiled=True),
        lax.all_gather(value_w, "dp", axis=0, tiled=True),
        lax.all_gather(up_w, "dp", axis=0, tiled=True),
        lax.all_gather(out_w, "dp", axis=1, tiled=True),
        lax.all_gather(down_w, "dp", axis=1, tiled=True),
    )


def share_rows(first, second):
    return (
        lax.all_gather(first, "tensor", axis=0, tiled=True),
        lax.all_gather(second, "tensor", axis=0, tiled=True),
    )


def share_grads(first, second):
    return (
        lax.all_gather(first, "tensor", axis=0, tiled=True),
        lax.all_gather(second, "tensor", axis=0, tiled=True),
    )


def row_term(left_h, right_h, left_g, right_g, numbers):
    first = lax.dot_general(left_h, right_h, numbers, preferred_element_type=jnp.float32)
    second = lax.dot_general(left_g, right_g, numbers, preferred_element_type=jnp.float32)
    return jnp.concatenate([first, second], axis=1)


def sum_forward(left_h, right_h, left_g, right_g):
    joined = lax.psum_scatter(
        row_term(left_h, right_h, left_g, right_g, contract_plain).astype(jnp.bfloat16),
        "tensor",
        scatter_dimension=0,
        tiled=True,
    ).astype(jnp.float32)
    width = right_h.shape[1]
    return (joined[:, :width], joined[:, width:])


def sum_backward(left_h, right_h, left_g, right_g):
    joined = lax.psum_scatter(
        row_term(left_h, right_h, left_g, right_g, contract_cols).astype(jnp.bfloat16),
        "tensor",
        scatter_dimension=0,
        tiled=True,
    ).astype(jnp.float32)
    width = right_h.shape[0]
    return (joined[:, :width], joined[:, width:])


def local(
    h_in,
    g_in,
    lengths,
    order,
    predicted,
    w_query,
    w_key,
    w_value,
    w_out,
    w_up,
    w_down,
    q_bias,
    v_bias,
    up_bias,
    rel_table,
    norm_gain,
    norm_shift,
    out_bias,
    h_cot,
    g_cot,
):
    content_masks, query_masks = jax.vmap(slot_masks)(lengths, order, predicted)
    slots = lengths.shape[0]
    heads_local = w_query.shape[2] // HEAD
    width_local = w_query.shape[2]
    places = jnp.arange(SEQ, dtype=jnp.int32)
    buckets = bucket_of(places[None, :] - places[:, None])
    onehot = (jnp.arange(BUCKETS, dtype=jnp.int32)[:, None, None] == buckets[None]).astype(
        jnp.float32
    )

    def to_heads(block):
        return block.reshape(slots, SEQ, heads_local, HEAD)

    current_h = h_in.astype(jnp.float32)
    current_g = g_in.astype(jnp.float32)
    fetched = []
    kept = []
    for layer in range(LAYERS):
        weights = fetch_weights(
            w_query[layer], w_key[layer], w_value[layer], w_up[layer], w_out[layer], w_down[layer]
        )
        query_full, key_full, value_full, up_full, out_full, down_full = weights
        fetched.append(weights)
        sent_h, sent_g = share_rows(current_h.astype(jnp.bfloat16), current_g.astype(jnp.bfloat16))
        query_h = (matmul(sent_h, query_full) + q_bias[layer]).astype(jnp.bfloat16)
        query_g = (matmul(sent_g, query_full) + q_bias[layer]).astype(jnp.bfloat16)
        keys = matmul(sent_h, key_full).astype(jnp.bfloat16)
        values = (matmul(sent_h, value_full) + v_bias[layer]).astype(jnp.bfloat16)
        bias = jnp.einsum("bij,hb->hij", onehot, rel_table[layer], precision=highest)

        def slot_forward(items, bias=bias):
            slot_qh, slot_qg, slot_keys, slot_values, content_mask, query_mask = items
            mixed_one, logsum_one = attend(slot_qh, slot_keys, slot_values, content_mask, bias)
            mixed_two, logsum_two = attend(slot_qg, slot_keys, slot_values, query_mask, bias)
            return (mixed_one, mixed_two, logsum_one, logsum_two)

        mixed_h, mixed_g, logsum_h, logsum_g = lax.map(
            slot_forward,
            (
                to_heads(query_h),
                to_heads(query_g),
                to_heads(keys),
                to_heads(values),
                content_masks,
                query_masks,
            ),
        )
        mixed_h = mixed_h.reshape(-1, width_local)
        mixed_g = mixed_g.reshape(-1, width_local)
        attn_h, attn_g = sum_forward(mixed_h, out_full, mixed_g, out_full)
        before_h = current_h + attn_h + out_bias[layer, 0]
        before_g = current_g + attn_g + out_bias[layer, 0]
        normed_h = norm_rows(before_h, norm_gain[layer, 0], norm_shift[layer, 0])
        normed_g = norm_rows(before_g, norm_gain[layer, 0], norm_shift[layer, 0])
        fed_h, fed_g = share_rows(normed_h.astype(jnp.bfloat16), normed_g.astype(jnp.bfloat16))
        inner_h = matmul(fed_h, up_full) + up_bias[layer]
        inner_g = matmul(fed_g, up_full) + up_bias[layer]
        act_h = smooth(inner_h).astype(jnp.bfloat16)
        act_g = smooth(inner_g).astype(jnp.bfloat16)
        ffn_h, ffn_g = sum_forward(act_h, down_full, act_g, down_full)
        ffn_kept = (up_full, down_full)
        after_h = normed_h + ffn_h + out_bias[layer, 1]
        after_g = normed_g + ffn_g + out_bias[layer, 1]
        kept.append(
            (
                sent_h,
                sent_g,
                query_h,
                query_g,
                keys,
                values,
                bias,
                logsum_h,
                logsum_g,
                mixed_h,
                mixed_g,
                before_h,
                before_g,
                fed_h,
                fed_g,
                inner_h,
                inner_g,
                act_h,
                act_g,
                after_h,
                after_g,
                ffn_kept,
            )
        )
        current_h = norm_rows(after_h, norm_gain[layer, 1], norm_shift[layer, 1])
        current_g = norm_rows(after_g, norm_gain[layer, 1], norm_shift[layer, 1])
    grad_h = h_cot.astype(jnp.float32)
    grad_g = g_cot.astype(jnp.float32)
    layer_grads = [None] * LAYERS
    small_grads = [None] * LAYERS
    norm_grads = [None] * LAYERS
    for layer in range(LAYERS - 1, -1, -1):
        (
            sent_h,
            sent_g,
            query_h,
            query_g,
            keys,
            values,
            bias,
            logsum_h,
            logsum_g,
            mixed_h,
            mixed_g,
            before_h,
            before_g,
            fed_h,
            fed_g,
            inner_h,
            inner_g,
            act_h,
            act_g,
            after_h,
            after_g,
            ffn_kept,
        ) = kept[layer]
        weights = fetch_again(
            w_query[layer], w_key[layer], w_value[layer], w_up[layer], w_out[layer], w_down[layer]
        )
        query_full, key_full, value_full, up_full, out_full, down_full = weights
        back_h, gain_two_h, shift_two_h = norm_back(
            after_h, norm_gain[layer, 1], norm_shift[layer, 1], grad_h
        )
        back_g, gain_two_g, shift_two_g = norm_back(
            after_g, norm_gain[layer, 1], norm_shift[layer, 1], grad_g
        )
        down_in_h, down_in_g = share_grads(back_h.astype(jnp.bfloat16), back_g.astype(jnp.bfloat16))
        grad_inner_h = smooth_back(inner_h, over_cols(down_in_h, down_full)).astype(jnp.bfloat16)
        grad_inner_g = smooth_back(inner_g, over_cols(down_in_g, down_full)).astype(jnp.bfloat16)
        down_grad = over_rows(act_h, down_in_h) + over_rows(act_g, down_in_g)
        up_grad = over_rows(fed_h, grad_inner_h) + over_rows(fed_g, grad_inner_g)
        up_bias_grad = jnp.sum(grad_inner_h.astype(jnp.float32), axis=0) + jnp.sum(
            grad_inner_g.astype(jnp.float32), axis=0
        )
        part_h, part_g = sum_backward(grad_inner_h, up_full, grad_inner_g, up_full)
        middle_h = back_h + part_h
        middle_g = back_g + part_g
        first_h, gain_one_h, shift_one_h = norm_back(
            before_h, norm_gain[layer, 0], norm_shift[layer, 0], middle_h
        )
        first_g, gain_one_g, shift_one_g = norm_back(
            before_g, norm_gain[layer, 0], norm_shift[layer, 0], middle_g
        )
        mixed_in_h, mixed_in_g = share_grads(
            first_h.astype(jnp.bfloat16), first_g.astype(jnp.bfloat16)
        )
        grad_mixed_h = over_cols(mixed_in_h, out_full).astype(jnp.bfloat16)
        grad_mixed_g = over_cols(mixed_in_g, out_full).astype(jnp.bfloat16)
        out_grad = over_rows(mixed_h, mixed_in_h) + over_rows(mixed_g, mixed_in_g)

        def slot_backward(carry, items, bias=bias):
            (
                slot_qh,
                slot_qg,
                slot_keys,
                slot_values,
                content_mask,
                query_mask,
                slot_lh,
                slot_lg,
                slot_gh,
                slot_gg,
            ) = items
            query_one, keys_one, values_one, scores_one = attend_back(
                slot_qh, slot_keys, slot_values, content_mask, bias, slot_lh, slot_gh
            )
            query_two, keys_two, values_two, scores_two = attend_back(
                slot_qg, slot_keys, slot_values, query_mask, bias, slot_lg, slot_gg
            )
            carry = carry + scores_one.astype(jnp.float32) + scores_two.astype(jnp.float32)
            return (
                carry,
                (
                    query_one.astype(jnp.bfloat16),
                    query_two.astype(jnp.bfloat16),
                    (keys_one + keys_two).astype(jnp.bfloat16),
                    (values_one + values_two).astype(jnp.bfloat16),
                ),
            )

        start_table = jnp.zeros((heads_local, SEQ, SEQ), jnp.float32)
        table_sums, (grad_qh, grad_qg, grad_keys, grad_values) = lax.scan(
            slot_backward,
            start_table,
            (
                to_heads(query_h),
                to_heads(query_g),
                to_heads(keys),
                to_heads(values),
                content_masks,
                query_masks,
                logsum_h,
                logsum_g,
                to_heads(grad_mixed_h),
                to_heads(grad_mixed_g),
            ),
        )
        grad_qh = grad_qh.reshape(-1, width_local)
        grad_qg = grad_qg.reshape(-1, width_local)
        grad_keys = grad_keys.reshape(-1, width_local)
        grad_values = grad_values.reshape(-1, width_local)
        table_grad = jnp.einsum("hij,bij->hb", table_sums, onehot, precision=highest)
        q_bias_grad = jnp.sum(grad_qh.astype(jnp.float32), axis=0) + jnp.sum(
            grad_qg.astype(jnp.float32), axis=0
        )
        v_bias_grad = jnp.sum(grad_values.astype(jnp.float32), axis=0)
        query_grad = over_rows(sent_h, grad_qh) + over_rows(sent_g, grad_qg)
        key_grad = over_rows(sent_h, grad_keys)
        value_grad = over_rows(sent_h, grad_values)
        part_h, part_g = sum_backward(
            jnp.concatenate([grad_qh, grad_keys, grad_values], axis=1),
            jnp.concatenate([query_full, key_full, value_full], axis=1),
            grad_qg,
            query_full,
        )
        grad_h = first_h + part_h
        grad_g = first_g + part_g
        layer_grads[layer] = (
            lax.psum_scatter(query_grad, "dp", scatter_dimension=0, tiled=True),
            lax.psum_scatter(key_grad, "dp", scatter_dimension=0, tiled=True),
            lax.psum_scatter(value_grad, "dp", scatter_dimension=0, tiled=True),
            lax.psum_scatter(up_grad, "dp", scatter_dimension=0, tiled=True),
            lax.psum_scatter(out_grad, "dp", scatter_dimension=1, tiled=True),
            lax.psum_scatter(down_grad, "dp", scatter_dimension=1, tiled=True),
        )
        small_grads[layer] = (q_bias_grad, v_bias_grad, up_bias_grad, table_grad)
        norm_grads[layer] = (
            jnp.stack([gain_one_h + gain_one_g, gain_two_h + gain_two_g]),
            jnp.stack([shift_one_h + shift_one_g, shift_two_h + shift_two_g]),
            jnp.stack([jnp.sum(first_h + first_g, axis=0), jnp.sum(back_h + back_g, axis=0)]),
        )
    stacked = tuple(
        (jnp.stack([layer_grads[layer][index] for layer in range(LAYERS)]) for index in range(6))
    )
    smalls = tuple(
        (jnp.stack([small_grads[layer][index] for layer in range(LAYERS)]) for index in range(4))
    )
    bias_sums = lax.psum((smalls[0], smalls[1], smalls[2], smalls[3]), "dp")
    norms = tuple(
        (jnp.stack([norm_grads[layer][index] for layer in range(LAYERS)]) for index in range(3))
    )
    norm_sums = lax.psum((norms[0], norms[1], norms[2]), ("dp", "tensor"))
    return (
        current_h.astype(jnp.bfloat16),
        current_g.astype(jnp.bfloat16),
        grad_h.astype(jnp.bfloat16),
        grad_g.astype(jnp.bfloat16),
        stacked[0],
        stacked[1],
        stacked[2],
        stacked[4],
        stacked[3],
        stacked[5],
        bias_sums[0],
        bias_sums[1],
        bias_sums[2],
        bias_sums[3],
        norm_sums[0],
        norm_sums[1],
        norm_sums[2],
    )


def solution(mesh):
    return jax.shard_map(
        local,
        mesh=mesh,
        in_specs=(
            P(("dp", "tensor"), None),
            P(("dp", "tensor"), None),
            P("dp", None),
            P("dp", None),
            P("dp", None),
            P(None, "dp", "tensor"),
            P(None, "dp", "tensor"),
            P(None, "dp", "tensor"),
            P(None, "tensor", "dp"),
            P(None, "dp", "tensor"),
            P(None, "tensor", "dp"),
            P(None, "tensor"),
            P(None, "tensor"),
            P(None, "tensor"),
            P(None, "tensor", None),
            P(),
            P(),
            P(),
            P(("dp", "tensor"), None),
            P(("dp", "tensor"), None),
        ),
        out_specs=(
            P(("dp", "tensor"), None),
            P(("dp", "tensor"), None),
            P(("dp", "tensor"), None),
            P(("dp", "tensor"), None),
            P(None, "dp", "tensor"),
            P(None, "dp", "tensor"),
            P(None, "dp", "tensor"),
            P(None, "tensor", "dp"),
            P(None, "dp", "tensor"),
            P(None, "tensor", "dp"),
            P(None, "tensor"),
            P(None, "tensor"),
            P(None, "tensor"),
            P(None, "tensor", None),
            P(),
            P(),
            P(),
        ),
        check_vma=False,
    )
```

profile of v0, /device:TPU:0, one launch (start us, length us, event | category | flops | bytes accessed | tf_op | source)
XLA Modules:
  0.0 2111.7 jit_solution(14181788264237914744)
XLA Ops:
  17.7 34.9 %all-gather.1 = bf16[1,768,192]{2,1,0:T(8,128)(2,1)} all-gather(bf16[1,96,192]{2,1,0:T(8,128)(2,1)S(1)} %get-tuple-element.1103), channel_id=3, replica_groups=mesh['dp'=8,'tensor'=4] {'dp'}, dimensions={1}, use_global_device_ids=true | all-gather | bytes 331776 | tf_op jit(solution)/shard_map/all_gather | solution.py:113
  52.6 33.1 %all-gather = bf16[1,768,192]{2,1,0:T(8,128)(2,1)} all-gather(bf16[1,96,192]{2,1,0:T(8,128)(2,1)S(1)} %get-tuple-element.1105), channel_id=2, replica_groups=mesh['dp'=8,'tensor'=4] {'dp'}, dimensions={1}, use_global_device_ids=true | all-gather | bytes 331776 | tf_op jit(solution)/shard_map/all_gather | solution.py:115
  85.7 31.8 %all-gather.3 = bf16[1,192,768]{1,0,2:T(2,128)(2,1)S(1)} all-gather(bf16[1,192,96]{1,0,2:T(2,128)(2,1)S(1)} %copy.419), channel_id=5, replica_groups=mesh['dp'=8,'tensor'=4] {'dp'}, dimensions={2}, use_global_device_ids=true | all-gather | bytes 331776 | tf_op jit(solution)/shard_map/all_gather | solution.py:117
  134.8 31.5 %all-gather.2 = bf16[1,768,192]{2,1,0:T(8,128)(2,1)S(1)} all-gather(bf16[1,96,192]{2,1,0:T(8,128)(2,1)S(1)} %get-tuple-element.1101), channel_id=4, replica_groups=mesh['dp'=8,'tensor'=4] {'dp'}, dimensions={1}, use_global_device_ids=true | all-gather | bytes 331776 | tf_op jit(solution)/shard_map/all_gather | solution.py:114
  201.6 16.7 while.70
  229.7 34.9 %reduce-scatter.37.cloned.1.call-done = bf16[256,1536]{0,1:T(8,128)(2,1)} async-done(((bf16[1024,1536]{0,1:T(8,128)(2,1)}), bf16[256,1536]{0,1:T(8,128)(2,1)}) %reduce-scatter.37.cloned.1.call-update) | async-done | bytes 786448 | tf_op jit(solution)/shard_map/reduce_scatter | solution.py:154
  271.5 20.3 all-gather.39.cloned.1.call-done
  296.5 17.0 all-gather.37.cloned.1.call-done
  318.0 40.1 %all-gather.67.cloned.1.call-done = bf16[1,768,768]{1,2,0:T(8,128)(2,1)} async-done(((bf16[1,768,96]{1,2,0:T(8,128)(2,1)}), bf16[1,768,768]{1,2,0:T(8,128)(2,1)}) %all-gather.67.cloned.1.call-update) | async-done | bytes 1179664 | tf_op jit(solution)/shard_map/all_gather | solution.py:118
  365.8 36.3 %reduce-scatter.39.cloned.1.call-done = bf16[256,1536]{0,1:T(8,128)(2,1)} async-done(((bf16[1024,1536]{0,1:T(8,128)(2,1)}), bf16[256,1536]{0,1:T(8,128)(2,1)}) %reduce-scatter.39.cloned.1.call-update) | async-done | bytes 786448 | tf_op jit(solution)/shard_map/reduce_scatter | solution.py:154
  406.9 32.2 %all-gather.9 = bf16[1,192,768]{1,0,2:T(2,128)(2,1)S(1)} all-gather(bf16[1,192,96]{1,0,2:T(2,128)(2,1)S(1)} %copy.420), channel_id=11, replica_groups=mesh['dp'=8,'tensor'=4] {'dp'}, dimensions={2}, use_global_device_ids=true | all-gather | bytes 331776 | tf_op jit(solution)/shard_map/all_gather | solution.py:117
  440.8 12.7 fusion.225
  456.9 33.1 %all-gather.7 = bf16[1,768,192]{2,1,0:T(8,128)(2,1)} all-gather(bf16[1,96,192]{2,1,0:T(8,128)(2,1)S(1)} %copy-done.129), channel_id=9, replica_groups=mesh['dp'=8,'tensor'=4] {'dp'}, dimensions={1}, use_global_device_ids=true | all-gather | bytes 331776 | tf_op jit(solution)/shard_map/all_gather | solution.py:113
  490.0 31.3 %all-gather.6 = bf16[1,768,192]{2,1,0:T(8,128)(2,1)S(1)} all-gather(bf16[1,96,192]{2,1,0:T(8,128)(2,1)} %get-tuple-element.1104), channel_id=8, replica_groups=mesh['dp'=8,'tensor'=4] {'dp'}, dimensions={1}, use_global_device_ids=true | all-gather | bytes 331776 | tf_op jit(solution)/shard_map/all_gather | solution.py:115
  521.3 33.3 %all-gather.8 = bf16[1,768,192]{2,1,0:T(8,128)(2,1)} all-gather(bf16[1,96,192]{2,1,0:T(8,128)(2,1)} %get-tuple-element.1100), channel_id=10, replica_groups=mesh['dp'=8,'tensor'=4] {'dp'}, dimensions={1}, use_global_device_ids=true | all-gather | bytes 331776 | tf_op jit(solution)/shard_map/all_gather | solution.py:114
  578.7 16.7 while.71
  602.6 37.6 %reduce-scatter.41.cloned.1.call-done = bf16[256,1536]{0,1:T(8,128)(2,1)} async-done(((bf16[1024,1536]{0,1:T(8,128)(2,1)}), bf16[256,1536]{0,1:T(8,128)(2,1)}) %reduce-scatter.41.cloned.1.call-update) | async-done | bytes 786448 | tf_op jit(solution)/shard_map/reduce_scatter | solution.py:154
  647.2 37.4 %all-gather.69.cloned.1.call-done = bf16[1,768,768]{2,1,0:T(8,128)(2,1)} async-done(((bf16[1,96,768]{2,1,0:T(8,128)(2,1)}), bf16[1,768,768]{2,1,0:T(8,128)(2,1)}) %all-gather.69.cloned.1.call-update) | async-done | bytes 1179664 | tf_op jit(solution)/shard_map/all_gather | solution.py:116
  684.6 20.3 all-gather.47.cloned.1.call-done
  709.7 16.9 all-gather.45.cloned.1.call-done
  731.5 39.7 %all-gather.71.cloned.1.call-done = bf16[1,768,768]{1,2,0:T(8,128)(2,1)} async-done(((bf16[1,768,96]{1,2,0:T(8,128)(2,1)}), bf16[1,768,768]{1,2,0:T(8,128)(2,1)}) %all-gather.71.cloned.1.call-update) | async-done | bytes 1179664 | tf_op jit(solution)/shard_map/all_gather | solution.py:118
  782.6 32.7 %reduce-scatter.43.cloned.1.call-done = bf16[256,1536]{0,1:T(8,128)(2,1)} async-done(((bf16[1024,1536]{0,1:T(8,128)(2,1)}), bf16[256,1536]{0,1:T(8,128)(2,1)}) %reduce-scatter.43.cloned.1.call-update) | async-done | bytes 786448 | tf_op jit(solution)/shard_map/reduce_scatter | solution.py:154
  822.6 18.8 all-gather.51.cloned.1.call-done
  849.1 13.7 all-gather.49.cloned.1.call-done
  874.5 38.0 %reduce-scatter.45.cloned.1.call-done = bf16[256,1536]{0,1:T(8,128)(2,1)} async-done(((bf16[1024,1536]{0,1:T(8,128)(2,1)}), bf16[256,1536]{0,1:T(8,128)(2,1)}) %reduce-scatter.45.cloned.1.call-update) | async-done | bytes 786448 | tf_op jit(solution)/shard_map/reduce_scatter | solution.py:165
  927.3 16.4 all-gather.53.cloned.1.call-done
  950.4 14.8 all-gather.55.cloned.1.call-done
  974.9 41.6 %while.72 = (s32[]{:T(128)}, f32[3,512,512]{1,2,0:T(8,128)}, bf16[2,512,3,64]{1,3,2,0:T(8,128)(2,1)}, bf16[2,512,3,64]{1,3,2,0:T(8,128)(2,1)}, bf16[2,512,3,64]{...) while((s32[]{:T(128)}, f32[3,512,512]{1,2,0:T(8,128)}, ...), condition=%wide.region_47.48_spmd.clone, body=%wide.region_44.47_spmd.clone.sunk | while | flops 1028748288 | bytes 112140976 | solution.py:383
  1025.3 37.6 %reduce-scatter.47.cloned.1.call-done = bf16[256,1536]{0,1:T(8,128)(2,1)} async-done(((bf16[1024,1536]{0,1:T(8,128)(2,1)}), bf16[256,1536]{0,1:T(8,128)(2,1)}) %reduce-scatter.47.cloned.1.call-update) | async-done | bytes 786448 | tf_op jit(solution)/shard_map/reduce_scatter | solution.py:165
  1070.3 18.2 all-gather.57.cloned.1.call-done
  1095.7 14.6 all-gather.59.cloned.1.call-done
  1122.3 38.0 %reduce-scatter.49.cloned.1.call-done = bf16[256,1536]{0,1:T(8,128)(2,1)} async-done(((bf16[1024,1536]{0,1:T(8,128)(2,1)}), bf16[256,1536]{0,1:T(8,128)(2,1)}) %reduce-scatter.49.cloned.1.call-update) | async-done | bytes 786448 | tf_op jit(solution)/shard_map/reduce_scatter | solution.py:165
  1225.6 41.6 %while.73 = (s32[]{:T(128)}, f32[3,512,512]{1,2,0:T(8,128)}, bf16[2,512,3,64]{1,3,2,0:T(8,128)(2,1)}, bf16[2,512,3,64]{1,3,2,0:T(8,128)(2,1)}, bf16[2,512,3,64]{...) while((s32[]{:T(128)}, f32[3,512,512]{1,2,0:T(8,128)}, ...), condition=%wide.region_61.62_spmd.clone, body=%wide.region_58.61_spmd.clone.sunk | while | flops 1028748288 | bytes 112140976 | solution.py:383
  1303.5 18.3 fusion.278
  1323.6 15.5 reduce-scatter.67.cloned.1.call-done
  1340.7 63.5 %reduce-scatter.71.cloned.1.call-done = f32[96,192]{1,0:T(8,128)} async-done(((f32[768,192]{1,0:T(8,128)}), f32[96,192]{1,0:T(8,128)}) %reduce-scatter.71.cloned.1.call-update) | async-done | bytes 73744
  1405.8 63.3 %reduce-scatter.63.cloned.1.call-done = f32[96,192]{1,0:T(8,128)} async-done(((f32[768,192]{1,0:T(8,128)}), f32[96,192]{1,0:T(8,128)}) %reduce-scatter.63.cloned.1.call-update) | async-done | bytes 73744
  1474.8 66.1 %reduce-scatter.59.cloned.1.call-done = f32[768,96]{0,1:T(8,128)} async-done(((f32[768,768]{0,1:T(8,128)}), f32[768,96]{0,1:T(8,128)}) %reduce-scatter.59.cloned.1.call-update) | async-done | bytes 294928 | tf_op jit(solution)/shard_map/reduce_scatter | solution.py:425
  1540.9 72.1 %reduce-scatter.57.cloned.1.call-done = f32[768,96]{0,1:T(8,128)} async-done(((f32[768,768]{0,1:T(8,128)}), f32[768,96]{0,1:T(8,128)}) %reduce-scatter.57.cloned.1.call-update) | async-done | bytes 294928 | tf_op jit(solution)/shard_map/reduce_scatter | solution.py:425
  1614.9 69.9 %reduce-scatter.55.cloned.1.call-done = f32[96,768]{1,0:T(8,128)} async-done(((f32[768,768]{1,0:T(8,128)}), f32[96,768]{1,0:T(8,128)}) %reduce-scatter.55.cloned.1.call-update) | async-done | bytes 294928 | tf_op jit(solution)/shard_map/reduce_scatter | solution.py:423
  1684.8 72.0 %reduce-scatter.53.cloned.1.call-done = f32[96,768]{1,0:T(8,128)} async-done(((f32[768,768]{1,0:T(8,128)}), f32[96,768]{1,0:T(8,128)}) %reduce-scatter.53.cloned.1.call-update) | async-done | bytes 294928 | tf_op jit(solution)/shard_map/reduce_scatter | solution.py:423
  1769.7 17.9 fusion.277
  1787.6 35.0 %all-reduce.2 = (f32[2,192]{1,0:T(2,128)}, f32[2,192]{1,0:T(2,128)}, f32[2,768]{1,0:T(2,128)}, f32[2,3,32]{2,1,0:T(4,128)S(1)}) all-reduce(f32[2,192]{1,0:T(2,128)S(1)} %pad_maximum_fusion.19, f32[2,192]{1,0:T(2,128)S(1)} %pad_maximum_fusion.20, f32[2,768]{1,0:T(2,128)S(1)} %copy-done.175, ...), channel_id=1, replica_groups=mesh['dp'=8,'tensor'=4] {'dp'}, use_global_device_ids=true, to_apply=%region_79.80 | all-reduce | flops 2496 | bytes 19968 | tf_op jit(solution)/shard_map/psum | solution.py:439
  1824.2 62.7 %reduce-scatter.65.cloned.1.call-done = f32[96,192]{1,0:T(8,128)} async-done(((f32[768,192]{1,0:T(8,128)}), f32[96,192]{1,0:T(8,128)}) %reduce-scatter.65.cloned.1.call-update) | async-done | bytes 73744
  1888.8 63.5 %reduce-scatter.69.cloned.1.call-done = f32[96,192]{1,0:T(8,128)} async-done(((f32[768,192]{1,0:T(8,128)}), f32[96,192]{1,0:T(8,128)}) %reduce-scatter.69.cloned.1.call-update) | async-done | bytes 73744
  1954.1 63.0 %reduce-scatter.61.cloned.1.call-done = f32[96,192]{1,0:T(8,128)} async-done(((f32[768,192]{1,0:T(8,128)}), f32[96,192]{1,0:T(8,128)}) %reduce-scatter.61.cloned.1.call-update) | async-done | bytes 73744
  2019.6 36.9 %reduce-scatter.51.cloned.1.call-done = bf16[256,1536]{0,1:T(8,128)(2,1)} async-done(((bf16[1024,1536]{0,1:T(8,128)(2,1)}), bf16[256,1536]{0,1:T(8,128)(2,1)}) %reduce-scatter.51.cloned.1.call-update) | async-done | bytes 786448 | tf_op jit(solution)/shard_map/reduce_scatter | solution.py:165
  2063.6 40.5 %all-reduce.1 = (f32[2,2,768]{2,1,0:T(2,128)}, f32[2,2,768]{2,1,0:T(2,128)}, f32[2,2,768]{2,1,0:T(2,128)}) all-reduce(f32[2,2,768]{2,1,0:T(2,128)S(1)} %pad_maximum_fusion.14, f32[2,2,768]{2,1,0:T(2,128)} %pad_maximum_fusion.15, f32[2,2,768]{2,1,0:T(2,128)S(1)} %pad_maximum_fusion.16), channel_id=1, replica_groups=mesh['dp'=8,'tensor'=4] {'dp','tensor'}, use_global_device_ids=true, to_apply=%region_97.98 | all-reduce | flops 9216 | bytes 73728 | tf_op jit(solution)/shard_map/psum | solution.py:443
  (1072 shorter events, 513.9 us)
Async XLA Ops:
  8.0 165.3 %all-gather.33.cloned.1.call-start = ((), (), s32[]{:S(2)}) async-start(), calls=%async_computation.20 | async-start | bytes 1966080 | tf_op jit(solution)/shard_map/all_gather | solution.py:135
  8.8 183.9 %all-gather.35.cloned.1.call-start = ((), (), s32[]{:S(2)}) async-start(), calls=%async_computation.21 | async-start | bytes 1966080 | tf_op jit(solution)/shard_map/all_gather | solution.py:136
  9.5 255.1 %reduce-scatter.37.cloned.1.call-start = ((), (), s32[]{:S(2)}) async-start(), calls=%async_computation.22 | async-start | bytes 3932160 | tf_op jit(solution)/shard_map/reduce_scatter | solution.py:154
  225.1 46.3 %all-gather.65.cloned.1.call-start = ((), (), s32[]{:S(2)}) async-start(), calls=%async_computation.48 | async-start | bytes 1327104 | tf_op jit(solution)/shard_map/all_gather | solution.py:116
  226.8 64.9 %all-gather.39.cloned.1.call-start = ((), (), s32[]{:S(2)}) async-start(), calls=%async_computation.24 | async-start | bytes 1966080 | tf_op jit(solution)/shard_map/all_gather | solution.py:136
  229.7 175.2 %copy-start.143 = (f32[768]{0:T(1024)}, f32[768]{0:T(1024)S(1)}, u32[]{:S(2)}) copy-start(f32[768]{0:T(1024)S(1)} %get-tuple-element.862) | copy-start | bytes 9220
  269.2 44.3 %all-gather.37.cloned.1.call-start = ((), (), s32[]{:S(2)}) async-start(), calls=%async_computation.23 | async-start | bytes 1966080 | tf_op jit(solution)/shard_map/all_gather | solution.py:135
  269.7 88.3 %all-gather.67.cloned.1.call-start = ((), (), s32[]{:S(2)}) async-start(), calls=%async_computation.49 | async-start | bytes 1327104 | tf_op jit(solution)/shard_map/all_gather | solution.py:118
  270.6 131.5 %reduce-scatter.39.cloned.1.call-start = ((), (), s32[]{:S(2)}) async-start(), calls=%async_computation.25 | async-start | bytes 3932160 | tf_op jit(solution)/shard_map/reduce_scatter | solution.py:154
  365.7 188.9 %all-gather.41.cloned.1.call-start = ((), (), s32[]{:S(2)}) async-start(), calls=%async_computation.26 | async-start | bytes 1966080 | tf_op jit(solution)/shard_map/all_gather | solution.py:135
  406.1 163.9 %all-gather.43.cloned.1.call-start = ((), (), s32[]{:S(2)}) async-start(), calls=%async_computation.27 | async-start | bytes 1966080 | tf_op jit(solution)/shard_map/all_gather | solution.py:136
  406.7 233.5 %reduce-scatter.41.cloned.1.call-start = ((), (), s32[]{:S(2)}) async-start(), calls=%async_computation.28 | async-start | bytes 3932160 | tf_op jit(solution)/shard_map/reduce_scatter | solution.py:154
  601.9 82.7 %all-gather.69.cloned.1.call-start = ((), (), s32[]{:S(2)}) async-start(), calls=%async_computation.50 | async-start | bytes 1327104 | tf_op jit(solution)/shard_map/all_gather | solution.py:116
  602.5 102.3 %all-gather.47.cloned.1.call-start = ((), (), s32[]{:S(2)}) async-start(), calls=%async_computation.30 | async-start | bytes 1966080 | tf_op jit(solution)/shard_map/all_gather | solution.py:136
  645.6 81.0 %all-gather.45.cloned.1.call-start = ((), (), s32[]{:S(2)}) async-start(), calls=%async_computation.29 | async-start | bytes 1966080 | tf_op jit(solution)/shard_map/all_gather | solution.py:135
  646.2 125.0 %all-gather.71.cloned.1.call-start = ((), (), s32[]{:S(2)}) async-start(), calls=%async_computation.51 | async-start | bytes 1327104 | tf_op jit(solution)/shard_map/all_gather | solution.py:118
  646.9 168.4 %reduce-scatter.43.cloned.1.call-start = ((), (), s32[]{:S(2)}) async-start(), calls=%async_computation.31 | async-start | bytes 3932160 | tf_op jit(solution)/shard_map/reduce_scatter | solution.py:154
  778.7 62.7 %all-gather.51.cloned.1.call-start = ((), (), s32[]{:S(2)}) async-start(), calls=%async_computation.33 | async-start | bytes 1966080 | tf_op jit(solution)/shard_map/all_gather | solution.py:143
  821.4 41.4 %all-gather.49.cloned.1.call-start = ((), (), s32[]{:S(2)}) async-start(), calls=%async_computation.32 | async-start | bytes 1966080 | tf_op jit(solution)/shard_map/all_gather | solution.py:142
  822.1 90.4 %reduce-scatter.45.cloned.1.call-start = ((), (), s32[]{:S(2)}) async-start(), calls=%async_computation.34 | async-start | bytes 3932160 | tf_op jit(solution)/shard_map/reduce_scatter | solution.py:165
  874.4 69.4 %all-gather.53.cloned.1.call-start = ((), (), s32[]{:S(2)}) async-start(), calls=%async_computation.35 | async-start | bytes 1966080 | tf_op jit(solution)/shard_map/all_gather | solution.py:142
  924.0 41.1 %all-gather.55.cloned.1.call-start = ((), (), s32[]{:S(2)}) async-start(), calls=%async_computation.36 | async-start | bytes 1966080 | tf_op jit(solution)/shard_map/all_gather | solution.py:143
  927.3 135.7 %reduce-scatter.47.cloned.1.call-start = ((), (), s32[]{:S(2)}) async-start(), calls=%async_computation.37 | async-start | bytes 3932160 | tf_op jit(solution)/shard_map/reduce_scatter | solution.py:165
  1024.9 63.6 %all-gather.57.cloned.1.call-start = ((), (), s32[]{:S(2)}) async-start(), calls=%async_computation.38 | async-start | bytes 1966080 | tf_op jit(solution)/shard_map/all_gather | solution.py:142
  1068.7 41.7 %all-gather.59.cloned.1.call-start = ((), (), s32[]{:S(2)}) async-start(), calls=%async_computation.39 | async-start | bytes 1966080 | tf_op jit(solution)/shard_map/all_gather | solution.py:143
  1070.2 90.1 %reduce-scatter.49.cloned.1.call-start = ((), (), s32[]{:S(2)}) async-start(), calls=%async_computation.40 | async-start | bytes 3932160 | tf_op jit(solution)/shard_map/reduce_scatter | solution.py:165
  1122.3 88.1 %all-gather.61.cloned.1.call-start = ((), (), s32[]{:S(2)}) async-start(), calls=%async_computation.41 | async-start | bytes 1966080 | tf_op jit(solution)/shard_map/all_gather | solution.py:142
  1166.6 46.8 %all-gather.63.cloned.1.call-start = ((), (), s32[]{:S(2)}) async-start(), calls=%async_computation.42 | async-start | bytes 1966080 | tf_op jit(solution)/shard_map/all_gather | solution.py:143
  1168.7 153.1 %reduce-scatter.75.cloned.1.call-start = ((), (), s32[]{:S(2)}) async-start(), calls=%async_computation.59 | async-start | bytes 884736
  1175.5 163.6 %reduce-scatter.67.cloned.1.call-start = ((), (), s32[]{:S(2)}) async-start(), calls=%async_computation.55 | async-start | bytes 884736
  1178.1 226.1 %reduce-scatter.71.cloned.1.call-start = ((), (), s32[]{:S(2)}) async-start(), calls=%async_computation.57 | async-start | bytes 884736
  1179.9 289.2 %reduce-scatter.63.cloned.1.call-start = ((), (), s32[]{:S(2)}) async-start(), calls=%async_computation.53 | async-start | bytes 884736
  1183.5 357.4 %reduce-scatter.59.cloned.1.call-start = ((), (), s32[]{:S(2)}) async-start(), calls=%async_computation.47 | async-start | bytes 2654208 | tf_op jit(solution)/shard_map/reduce_scatter | solution.py:425
  1190.8 422.2 %reduce-scatter.57.cloned.1.call-start = ((), (), s32[]{:S(2)}) async-start(), calls=%async_computation.46 | async-start | bytes 2654208 | tf_op jit(solution)/shard_map/reduce_scatter | solution.py:425
  1198.1 486.7 %reduce-scatter.55.cloned.1.call-start = ((), (), s32[]{:S(2)}) async-start(), calls=%async_computation.45 | async-start | bytes 2654208 | tf_op jit(solution)/shard_map/reduce_scatter | solution.py:423
  1204.0 552.9 %reduce-scatter.53.cloned.1.call-start = ((), (), s32[]{:S(2)}) async-start(), calls=%async_computation.44 | async-start | bytes 2654208 | tf_op jit(solution)/shard_map/reduce_scatter | solution.py:423
  1210.3 612.9 %reduce-scatter.73.cloned.1.call-start = ((), (), s32[]{:S(2)}) async-start(), calls=%async_computation.58 | async-start | bytes 884736
  1222.0 664.9 %reduce-scatter.65.cloned.1.call-start = ((), (), s32[]{:S(2)}) async-start(), calls=%async_computation.54 | async-start | bytes 884736
  1272.1 680.2 %reduce-scatter.69.cloned.1.call-start = ((), (), s32[]{:S(2)}) async-start(), calls=%async_computation.56 | async-start | bytes 884736
  1274.3 742.7 %reduce-scatter.61.cloned.1.call-start = ((), (), s32[]{:S(2)}) async-start(), calls=%async_computation.52 | async-start | bytes 884736
  1278.9 777.7 %reduce-scatter.51.cloned.1.call-start = ((), (), s32[]{:S(2)}) async-start(), calls=%async_computation.43 | async-start | bytes 3932160 | tf_op jit(solution)/shard_map/reduce_scatter | solution.py:165
  1303.5 459.9 %copy-start.69 = (bf16[2,512,3,64]{1,3,2,0:T(8,128)(2,1)S(1)}, bf16[2,512,3,64]{1,3,2,0:T(8,128)(2,1)}, u32[]{:S(2)}) copy-start(bf16[2,512,3,64]{1,3,2,0:T(8,128)(2,1)} %get-tuple-element.343) | copy-start | bytes 1179652
  1321.8 444.2 %copy-start.8 = (f32[3,512,512]{1,2,0:T(8,128)S(1)}, f32[3,512,512]{1,2,0:T(8,128)}, u32[]{:S(2)}) copy-start(f32[3,512,512]{1,2,0:T(8,128)} %get-tuple-element.345) | copy-start | bytes 9437188
  1769.7 183.6 %copy-start.119 = (f32[96,192]{0,1:T(8,128)S(1)}, f32[96,192]{0,1:T(8,128)}, u32[]{:S(2)}) copy-start(f32[96,192]{0,1:T(8,128)} %copy.412) | copy-start | bytes 221188
  1769.7 248.4 %copy-start.118 = (f32[96,192]{0,1:T(8,128)S(1)}, f32[96,192]{0,1:T(8,128)}, u32[]{:S(2)}) copy-start(f32[96,192]{0,1:T(8,128)} %copy.404) | copy-start | bytes 221188
  1787.6 231.3 %copy-start.117 = (f32[192,96]{1,0:T(8,128)S(1)}, f32[192,96]{1,0:T(8,128)}, u32[]{:S(2)}) copy-start(f32[192,96]{1,0:T(8,128)} %copy.416) | copy-start | bytes 221188
  1787.6 270.2 %copy-start.57 = (f32[256,768]{0,1:T(8,128)S(1)}, f32[256,768]{0,1:T(8,128)}, u32[]{:S(2)}) copy-start(f32[256,768]{0,1:T(8,128)} %copy-done.56) | copy-start | bytes 2359300
  1787.6 270.2 %copy-start.59 = (f32[256,768]{0,1:T(8,128)S(1)}, f32[256,768]{0,1:T(8,128)}, u32[]{:S(2)}) copy-start(f32[256,768]{0,1:T(8,128)} %copy-done.58) | copy-start | bytes 2359300
  (286 other events, 4118.5 us)
Sparse Core Ops, SparseCore 0:
  10.4 22.3 all-gather.32
  34.4 19.6 all-gather.34
  225.3 39.2 reduce-scatter.36
  406.2 19.8 all-gather.40
  428.1 19.8 all-gather.42
  778.8 36.4 reduce-scatter.42
  821.5 19.8 all-gather.50
  842.9 19.8 all-gather.48
  874.5 37.9 reduce-scatter.44
  1025.0 37.9 reduce-scatter.46
  1122.4 37.9 reduce-scatter.48
Sparse Core Ops, SparseCore 1:
  228.6 42.8 all-gather.64
  273.5 18.1 all-gather.38
  293.8 19.6 all-gather.36
  316.5 41.5 all-gather.66
  365.8 36.3 reduce-scatter.38
  602.0 38.1 reduce-scatter.40
  643.0 41.5 all-gather.68
  686.7 18.1 all-gather.46
  706.9 19.6 all-gather.44
  729.7 41.5 all-gather.70
  924.1 19.6 all-gather.52
  945.4 19.6 all-gather.54
  1068.8 19.7 all-gather.56
  1090.6 19.6 all-gather.58
  1166.7 19.6 all-gather.60
  1188.0 19.6 all-gather.62
  1211.4 62.6 reduce-scatter.74
  1277.3 61.7 reduce-scatter.66
  1342.6 61.5 reduce-scatter.70
  1407.5 61.6 reduce-scatter.62
  1472.9 67.9 reduce-scatter.58
  1544.7 68.3 reduce-scatter.56
  1616.8 68.0 reduce-scatter.54
  1688.8 68.0 reduce-scatter.52
  1760.4 61.6 reduce-scatter.72
  1825.3 61.5 reduce-scatter.64
  1890.6 61.6 reduce-scatter.68
  1955.4 61.6 reduce-scatter.60
  2019.6 36.8 reduce-scatter.50
where the time goes:
time: 2120 us; the launch traced here: 2110 us
  waiting for transfers between devices  1200 us (57%)
  blocking collectives  337 us (16%)
  matrix products  268 us (13%)
  local copies, waits for them, and re-layouts  163 us (8%)
  other arithmetic  122 us (6%)
    unnamed x48, waiting for transfers between devices  337 us
    reduce_scatter x4, waiting for transfers between devices, sum_backward(): lax.psum_scatter(row_term(left_h, right_h, left_g, right_g, contract_cols...  151 us
    reduce_scatter x2, waiting for transfers between devices, local(): lax.psum_scatter(up_grad, 'dp', scatter_dimension=0, tiled=True)  142 us
    reduce_scatter x4, waiting for transfers between devices, sum_forward(): lax.psum_scatter(row_term(left_h, right_h, left_g, right_g, contract_plai...  142 us
    reduce_scatter x2, waiting for transfers between devices, local(): lax.psum_scatter(down_grad, 'dp', scatter_dimension=1, tiled=True)  138 us
    all_gather x2, waiting for transfers between devices, fetch_weights(): lax.all_gather(down_w, 'dp', axis=1, tiled=True)  79.8 us
    all_gather x2, blocking collectives, fetch_weights(): lax.all_gather(query_w, 'dp', axis=0, tiled=True)  68 us
    all_gather x2, blocking collectives, fetch_weights(): lax.all_gather(key_w, 'dp', axis=0, tiled=True)  64.8 us
  transfers between devices with their start and end apart: 40, of which 32 were waited for; matrix products, arithmetic and copies ran while one was open for 16% of the time, Pallas kernels for 0%

commit v1 on v0

v1 whole, which is shorter than its diff:
```python
import jax
import jax.numpy as jnp
from jax import lax
from jax.sharding import Mesh, PartitionSpec as P

HEAD = 64
BUCKETS = 32
LAYERS = 2
SEQ = 512

epsilon = 1e-05
limits = (12, 16, 23, 32, 46, 64, 91)
highest = lax.Precision.HIGHEST
f32 = jnp.float32
bf16 = jnp.bfloat16
SWAP = [(0, 1), (1, 0)]


def dot(left, right, numbers):
    return lax.dot_general(left, right, (numbers, ((), ())), preferred_element_type=f32)


def nn(left, right):
    return dot(left, right, ((1,), (0,)))


def nt(left, right):
    return dot(left, right, ((1,), (1,)))


def tn(left, right):
    return dot(left, right, ((0,), (0,)))


def bucket_of(offset):
    distance = jnp.abs(offset)
    farther = 8 + sum(((distance >= border).astype(jnp.int32) for border in limits))
    return jnp.where(distance < 8, distance, farther) + 16 * (offset > 0).astype(jnp.int32)


def slot_masks(piece_lengths, ranks, chosen):
    places = jnp.arange(SEQ, dtype=jnp.int32)
    first = piece_lengths[0]
    second = first + piece_lengths[1]
    third = second + piece_lengths[2]
    segment = (
        (places >= first).astype(jnp.int32)
        + (places >= second).astype(jnp.int32)
        + (places >= third).astype(jnp.int32)
    )
    leading = jnp.where(
        segment == 0,
        0,
        jnp.where(segment == 1, first, jnp.where(segment == 2, second, third)),
    )
    same_doc = segment[:, None] == segment[None, :]
    visible = chosen[None, :] == 0
    content_mask = same_doc & (visible | (ranks[None, :] <= ranks[:, None]))
    query_mask = same_doc & (
        (places[None, :] == leading[:, None])
        | visible & (places[None, :] != places[:, None])
        | (ranks[None, :] < ranks[:, None])
    )
    return (content_mask, query_mask)


class Links:
    def __init__(self, mesh):
        dp = mesh.shape["dp"]
        self.routed = dp == 8
        self.ny = 2
        self.nz = dp // 2
        self.nx = mesh.shape["tensor"] // 2
        self.mesh = Mesh(
            mesh.devices.reshape(self.nz, self.ny, self.nx, 2), ("z", "y", "x", "core")
        )
        self.ring = [(i, (i + 1) % self.nz) for i in range(self.nz)]

    def px(self, v):
        return lax.ppermute(v, "x", SWAP)

    def py(self, v):
        return lax.ppermute(v, "y", SWAP)

    def pz(self, v):
        return lax.ppermute(v, "z", self.ring)

    def pc(self, v):
        return lax.ppermute(v, "core", SWAP)

    def feature_order(self, width):
        count = self.nz * self.ny
        depth = width // count
        place = jnp.arange(width, dtype=jnp.int32)
        if not self.routed:
            return place
        block, rest = place // depth, place % depth
        ky, kz = block // self.nz, block % self.nz
        z = lax.rem(lax.axis_index("z") - kz + self.nz, self.nz)
        y = jnp.bitwise_xor(lax.axis_index("y"), ky)
        return (z * self.ny + y) * depth + rest

    def gather(self, block, route):
        if not self.routed:
            rows = lax.all_gather(block, ("z", "y"), axis=0, tiled=True)
            return lax.all_gather(rows, "x", axis=0)
        if route == "xzy":
            held = [jnp.stack([block, self.px(block)])]
            for _ in range(self.nz - 1):
                held.append(self.pz(held[-1]))
            return jnp.concatenate(held + [self.py(h) for h in held], axis=1)
        if route == "yzx":
            held = [jnp.concatenate([block, self.py(block)])]
            depth = block.shape[0]
            for _ in range(self.nz - 1):
                held.append(self.pz(held[-1]))
            other = [self.px(h) for h in held]
            return jnp.stack(
                [
                    jnp.concatenate([h[:depth] for h in s] + [h[depth:] for h in s])
                    for s in (held, other)
                ]
            )
        held = [block]
        for _ in range(self.nz - 1):
            held.append(self.pz(held[-1]))
        held = [jnp.stack([h, self.px(h)]) for h in held]
        return jnp.concatenate(held + [self.py(h) for h in held], axis=1)

    def scatter(self, grad, route):
        if not self.routed:
            mine = lax.psum_scatter(grad, "x", scatter_dimension=0, tiled=False)
            return lax.psum_scatter(
                mine, ("z", "y"), scatter_dimension=0, tiled=True
            ).astype(f32)
        depth = grad.shape[1] // (self.ny * self.nz)
        g = grad.reshape(2, self.ny, self.nz, depth, grad.shape[2])

        def ring(parts):
            acc = parts(1).astype(bf16)
            for k in range(2, self.nz):
                acc = (parts(k) + self.pz(acc).astype(f32)).astype(bf16)
            return parts(0) + self.pz(acc).astype(f32)

        def both(a, b):
            return a.astype(f32) + b.astype(f32)

        if route == "yzx":
            got = self.py(g[:, 1])
            done = ring(lambda k: both(g[:, 0, k], got[:, k]))
            return done[0] + self.px(done[1].astype(bf16)).astype(f32)
        if route == "xzy":
            got = self.px(g[1])
            done = ring(lambda k: both(g[0, :, k], got[:, k]))
            return done[0] + self.py(done[1].astype(bf16)).astype(f32)
        got = self.py(g[:, 1])
        more = self.px(both(g[1, 0], got[1]).astype(bf16))
        return ring(lambda k: both(g[0, 0, k], got[0, k]) + more[k].astype(f32))

    def pair(self, v):
        if not self.routed:
            return lax.all_gather(v, "x", axis=0)
        return jnp.stack([v, self.px(v)])

    def total(self, split, whole):
        if not self.routed:
            mine = lax.psum_scatter(split, "x", scatter_dimension=0, tiled=False)
            return lax.psum(mine, ("z", "y")), lax.psum(whole, ("z", "y", "x"))
        n = split.shape[1]
        count = n + whole.shape[0]
        filler = jnp.zeros((-count % 128,), f32)
        sent = jnp.concatenate([split[1], whole, filler]).reshape(-1, 128)
        kept = jnp.concatenate([split[0], whole, filler]).reshape(-1, 128)
        v = kept + self.px(sent)
        v = v + self.py(v)
        step = 1
        while step < self.nz:
            v = v + lax.ppermute(v, "z", [(i, i ^ step) for i in range(self.nz)])
            step *= 2
        v = v.reshape(-1)
        return v[:n], v[n:count]

    def both_rows(self, v):
        other = self.pc(v)
        first = lax.axis_index("core") == 0
        return jnp.concatenate([jnp.where(first, v, other), jnp.where(first, other, v)])


def norm_rows(rows, gain, shift):
    center = rows - jnp.mean(rows, axis=-1, keepdims=True)
    spread = jnp.mean(center * center, axis=-1, keepdims=True)
    return center * lax.rsqrt(spread + epsilon) * gain + shift


def norm_back(rows, gain, shift, grad):
    unused, pull = jax.vjp(norm_rows, rows, gain, shift)
    return pull(grad)


def smooth(inner):
    return jax.nn.gelu(inner, approximate=True)


def smooth_back(inner, grad):
    unused, pull = jax.vjp(smooth, inner)
    return pull(grad)[0]


def masked_scores(queries, keys, allowed, bias):
    scores = jnp.einsum("hqe,hke->hqk", queries, keys, preferred_element_type=f32) * 0.125 + bias
    return jnp.where(allowed[None], scores, -1e30)


def attend(queries, keys, values, allowed, bias):
    scores = masked_scores(queries, keys, allowed, bias)
    maxima = jnp.max(scores, axis=-1, keepdims=True)
    raised = jnp.exp(scores - maxima)
    total = jnp.sum(raised, axis=-1, keepdims=True)
    probs = (raised / total).astype(bf16)
    result = jnp.einsum("hqk,hke->hqe", probs, values, preferred_element_type=f32)
    return (result.astype(bf16), (maxima + jnp.log(total))[..., 0])


def attend_back(queries, keys, values, allowed, bias, logsum, grad_out):
    scores = masked_scores(queries, keys, allowed, bias)
    probs = jnp.where(allowed[None], jnp.exp(scores - logsum[..., None]), 0.0)
    grad_probs = jnp.einsum("hqe,hke->hqk", grad_out, values, preferred_element_type=f32)
    inner = jnp.sum(probs * grad_probs, axis=-1, keepdims=True)
    grad_scores = (probs * (grad_probs - inner)).astype(bf16)
    grad_query = jnp.einsum("hqk,hke->hqe", grad_scores, keys, preferred_element_type=f32) * 0.125
    grad_keys = jnp.einsum("hqk,hqe->hke", grad_scores, queries, preferred_element_type=f32) * 0.125
    grad_values = jnp.einsum(
        "hqk,hqe->hke", probs.astype(bf16), grad_out, preferred_element_type=f32
    )
    return (grad_query, grad_keys, grad_values, grad_scores)


def heads_of(block):
    rows, width = block.shape
    return block.reshape(rows, width // HEAD, HEAD).transpose(1, 0, 2)


def rows_of(block):
    heads, rows, head = block.shape
    return block.transpose(1, 0, 2).reshape(rows, heads * head)


def local(links, *arguments):
    (
        h_in,
        g_in,
        lengths,
        order,
        predicted,
        w_query,
        w_key,
        w_value,
        w_out,
        w_up,
        w_down,
        q_bias,
        v_bias,
        up_bias,
        rel_table,
        norm_gain,
        norm_shift,
        out_bias,
        h_cot,
        g_cot,
    ) = arguments
    rows_own, model = h_in.shape
    part = w_query.shape[2]
    units = w_up.shape[2]
    table_size = rel_table.shape[1] * BUCKETS
    slot = lax.axis_index("x")
    core = lax.axis_index("core")

    routes = (("zxy", "xzy", "yzx"), ("zxy", "xzy", "yzx"))
    blocks = []
    for layer in range(LAYERS):
        attn = jnp.concatenate(
            [w_query[layer], w_key[layer], w_value[layer], w_out[layer].T], axis=1
        )
        blocks.append((attn, w_up[layer], w_down[layer].T))
    gathered = [
        [links.gather(b, r) for b, r in zip(blocks[layer], routes[layer])]
        for layer in range(LAYERS)
    ]

    def pick(v):
        return lax.dynamic_index_in_dim(v, slot, 0, keepdims=False)

    content_mask, query_mask = slot_masks(pick(lengths), pick(order), pick(predicted))
    places = jnp.arange(SEQ, dtype=jnp.int32)
    buckets = bucket_of(places[None, :] - places[:, None])
    onehot = (jnp.arange(BUCKETS, dtype=jnp.int32)[:, None, None] == buckets[None]).astype(f32)

    small = links.pair(
        jnp.concatenate(
            [q_bias, v_bias, up_bias, rel_table.reshape(LAYERS, table_size)], axis=1
        )
    )
    features = links.feature_order(model)
    swapper = (jnp.arange(model, dtype=jnp.int32)[:, None] == features[None, :]).astype(bf16)
    swapper32 = swapper.astype(f32)

    entering = links.both_rows(jnp.concatenate([h_in, g_in], axis=1))
    leaving = links.both_rows(jnp.concatenate([h_cot, g_cot], axis=1))

    def ordered(rows):
        return nn(rows, swapper)

    params = jnp.dot(
        jnp.concatenate([norm_gain, norm_shift, out_bias], axis=1).reshape(-1, model),
        swapper32,
        precision=highest,
    ).reshape(LAYERS, 3, 2, model)

    current_h = ordered(entering[:, :model])
    current_g = ordered(entering[:, model:])
    kept = []
    for layer in range(LAYERS):
        attn, up, down = gathered[layer]
        own = small[:, layer]
        bias_q = own[:, :part].reshape(-1)
        bias_v = own[:, part : 2 * part].reshape(-1)
        bias_up = own[:, 2 * part : 2 * part + units].reshape(-1)
        table = own[:, 2 * part + units :].reshape(-1, BUCKETS)
        wq, wk, wv, wo = (
            jnp.concatenate([attn[i, :, part * n : part * (n + 1)] for i in range(2)], axis=1)
            for n in range(4)
        )
        wu = jnp.concatenate([up[0], up[1]], axis=1)
        wd = jnp.concatenate([down[0], down[1]], axis=1)
        gains, shifts, biases = params[layer]
        hs, gs = current_h.astype(bf16), current_g.astype(bf16)
        query_h = heads_of((nn(hs, wq) + bias_q).astype(bf16))
        query_g = heads_of((nn(gs, wq) + bias_q).astype(bf16))
        keys = heads_of(nn(hs, wk).astype(bf16))
        values = heads_of((nn(hs, wv) + bias_v).astype(bf16))
        bias = jnp.einsum("bij,hb->hij", onehot, table, precision=highest)
        mixed_h, logsum_h = attend(query_h, keys, values, content_mask, bias)
        mixed_g, logsum_g = attend(query_g, keys, values, query_mask, bias)
        mixed_h, mixed_g = rows_of(mixed_h), rows_of(mixed_g)
        part_h, part_g = nt(mixed_h, wo).astype(bf16), nt(mixed_g, wo).astype(bf16)
        before_h = current_h + part_h + links.pc(part_h).astype(f32) + biases[0]
        before_g = current_g + part_g + links.pc(part_g).astype(f32) + biases[0]
        normed_h = norm_rows(before_h, gains[0], shifts[0])
        normed_g = norm_rows(before_g, gains[0], shifts[0])
        fed_h, fed_g = normed_h.astype(bf16), normed_g.astype(bf16)
        inner_h, inner_g = nn(fed_h, wu) + bias_up, nn(fed_g, wu) + bias_up
        act_h, act_g = smooth(inner_h).astype(bf16), smooth(inner_g).astype(bf16)
        part_h, part_g = nt(act_h, wd).astype(bf16), nt(act_g, wd).astype(bf16)
        after_h = normed_h + part_h + links.pc(part_h).astype(f32) + biases[1]
        after_g = normed_g + part_g + links.pc(part_g).astype(f32) + biases[1]
        kept.append(
            (
                (hs, gs, query_h, query_g, keys, values, bias, logsum_h, logsum_g),
                (mixed_h, mixed_g, before_h, before_g, fed_h, fed_g, inner_h, inner_g),
                (act_h, act_g, after_h, after_g, wq, wk, wv, wo, wu, wd, gains, shifts),
            )
        )
        current_h = norm_rows(after_h, gains[1], shifts[1])
        current_g = norm_rows(after_g, gains[1], shifts[1])
    grad_h = ordered(leaving[:, :model])
    grad_g = ordered(leaving[:, model:])
    owned = [None] * LAYERS
    splits = [None] * LAYERS
    wholes = [None] * LAYERS
    for layer in range(LAYERS - 1, -1, -1):
        hs, gs, query_h, query_g, keys, values, bias, logsum_h, logsum_g = kept[layer][0]
        mixed_h, mixed_g, before_h, before_g, fed_h, fed_g, inner_h, inner_g = kept[layer][1]
        act_h, act_g, after_h, after_g, wq, wk, wv, wo, wu, wd, gains, shifts = kept[layer][2]
        back_h, gain2_h, shift2_h = norm_back(after_h, gains[1], shifts[1], grad_h)
        back_g, gain2_g, shift2_g = norm_back(after_g, gains[1], shifts[1], grad_g)
        dz_h, dz_g = back_h.astype(bf16), back_g.astype(bf16)
        du_h = smooth_back(inner_h, nn(dz_h, wd)).astype(bf16)
        du_g = smooth_back(inner_g, nn(dz_g, wd)).astype(bf16)
        down_grad = tn(dz_h, act_h) + tn(dz_g, act_g)
        up_grad = tn(fed_h, du_h) + tn(fed_g, du_g)
        up_bias_grad = jnp.sum(du_h.astype(f32), axis=0) + jnp.sum(du_g.astype(f32), axis=0)
        part_h, part_g = nt(du_h, wu).astype(bf16), nt(du_g, wu).astype(bf16)
        middle_h = back_h + part_h + links.pc(part_h).astype(f32)
        middle_g = back_g + part_g + links.pc(part_g).astype(f32)
        first_h, gain1_h, shift1_h = norm_back(before_h, gains[0], shifts[0], middle_h)
        first_g, gain1_g, shift1_g = norm_back(before_g, gains[0], shifts[0], middle_g)
        dy_h, dy_g = first_h.astype(bf16), first_g.astype(bf16)
        do_h = heads_of(nn(dy_h, wo).astype(bf16))
        do_g = heads_of(nn(dy_g, wo).astype(bf16))
        out_grad = tn(dy_h, mixed_h) + tn(dy_g, mixed_g)
        dq_h, dk_h, dv_h, ds_h = attend_back(
            query_h, keys, values, content_mask, bias, logsum_h, do_h
        )
        dq_g, dk_g, dv_g, ds_g = attend_back(
            query_g, keys, values, query_mask, bias, logsum_g, do_g
        )
        table_grad = jnp.einsum(
            "hij,bij->hb", ds_h.astype(f32) + ds_g.astype(f32), onehot, precision=highest
        )
        dq_h, dq_g = rows_of(dq_h).astype(bf16), rows_of(dq_g).astype(bf16)
        dk = rows_of(dk_h + dk_g).astype(bf16)
        dv = rows_of(dv_h + dv_g).astype(bf16)
        q_bias_grad = jnp.sum(dq_h.astype(f32), axis=0) + jnp.sum(dq_g.astype(f32), axis=0)
        v_bias_grad = jnp.sum(dv.astype(f32), axis=0)
        query_grad = tn(hs, dq_h) + tn(gs, dq_g)
        key_grad, value_grad = tn(hs, dk), tn(hs, dv)
        part_h = (nt(dq_h, wq) + nt(dk, wk) + nt(dv, wv)).astype(bf16)
        part_g = nt(dq_g, wq).astype(bf16)
        grad_h = first_h + part_h + links.pc(part_h).astype(f32)
        grad_g = first_g + part_g + links.pc(part_g).astype(f32)

        def by_x(v):
            return v.reshape(v.shape[0], 2, -1).transpose(1, 0, 2)

        attn_grad = jnp.concatenate(
            [by_x(query_grad), by_x(key_grad), by_x(value_grad), by_x(out_grad)], axis=2
        )
        owned[layer] = [
            links.scatter(g.astype(bf16), r)
            for g, r in zip((attn_grad, by_x(up_grad), by_x(down_grad)), routes[layer])
        ]
        splits[layer] = jnp.concatenate(
            [
                q_bias_grad.reshape(2, -1),
                v_bias_grad.reshape(2, -1),
                up_bias_grad.reshape(2, -1),
                table_grad.reshape(2, -1),
            ],
            axis=1,
        )
        wholes[layer] = jnp.stack(
            [
                gain1_h + gain1_g,
                gain2_h + gain2_g,
                shift1_h + shift1_g,
                shift2_h + shift2_g,
                jnp.sum(first_h + first_g, axis=0),
                jnp.sum(back_h + back_g, axis=0),
            ]
        )
    whole = jnp.dot(jnp.concatenate(wholes), swapper32.T, precision=highest)
    split_sum, whole_sum = links.total(jnp.concatenate(splits, axis=1), whole.reshape(-1))
    split_sum = split_sum.reshape(LAYERS, -1)
    whole_sum = whole_sum.reshape(LAYERS, 3, 2, model)

    def returned(rows):
        mine = lax.dynamic_slice_in_dim(rows.astype(bf16), core * rows_own, rows_own, 0)
        return nt(mine, swapper).astype(bf16)

    attn_sum = jnp.stack([owned[layer][0] for layer in range(LAYERS)])
    up_sum = jnp.stack([owned[layer][1] for layer in range(LAYERS)])
    down_sum = jnp.stack([owned[layer][2] for layer in range(LAYERS)])
    return (
        returned(current_h),
        returned(current_g),
        returned(grad_h),
        returned(grad_g),
        attn_sum[:, :, :part],
        attn_sum[:, :, part : 2 * part],
        attn_sum[:, :, 2 * part : 3 * part],
        attn_sum[:, :, 3 * part :].transpose(0, 2, 1),
        up_sum,
        down_sum.transpose(0, 2, 1),
        split_sum[:, :part],
        split_sum[:, part : 2 * part],
        split_sum[:, 2 * part : 2 * part + units],
        split_sum[:, 2 * part + units :].reshape(LAYERS, -1, BUCKETS),
        whole_sum[:, 0],
        whole_sum[:, 1],
        whole_sum[:, 2],
    )


def solution(mesh):
    links = Links(mesh)
    rows = P(("z", "y", "x", "core"), None)
    by_dp = P(("z", "y"), None)
    wide = P(None, ("z", "y"), ("x", "core"))
    tall = P(None, ("x", "core"), ("z", "y"))
    by_tensor = P(None, ("x", "core"))
    table = P(None, ("x", "core"), None)
    weights = (wide, wide, wide, tall, wide, tall)
    owned = (by_tensor, by_tensor, by_tensor, table, P(), P(), P())
    inner = jax.shard_map(
        lambda *arguments: local(links, *arguments),
        mesh=links.mesh,
        in_specs=(rows, rows, by_dp, by_dp, by_dp) + weights + owned + (rows, rows),
        out_specs=(rows, rows, rows, rows) + weights + owned,
        check_vma=False,
    )
    return inner
```

time: 2120 us -> 875 us (0.41)
  waiting for transfers between devices: 1200 us -> 201 us
  blocking collectives: 337 us -> 0 us
  starting transfers between devices: 3.89 us -> 76.4 us
  local copies, waits for them, and re-layouts: 163 us -> 214 us
    reduce_scatter x12 -> x0, waiting for transfers between devices: 572 us -> none  [the longest x4 151 us: sum_backward(): lax.psum_scatter(row_term(left_h, right_h, left_g, right_g, contract_cols...]
    unnamed x48 -> x0, waiting for transfers between devices: 337 us -> none
    all_gather x20 -> x0, waiting for transfers between devices: 288 us -> none  [the longest x2 79.8 us: fetch_weights(): lax.all_gather(down_w, 'dp', axis=1, tiled=True)]
    all_gather x8 -> x0, blocking collectives: 261 us -> none  [the longest x2 68 us: fetch_weights(): lax.all_gather(query_w, 'dp', axis=0, tiled=True)]
    ppermute x0 -> x107, waiting for transfers between devices: none -> 201 us  [the longest x36 115 us: pz(): return lax.ppermute(v, 'z', self.ring)]
    ppermute x0 -> x107, starting transfers between devices: none -> 76.4 us  [the longest x26 26.1 us: px(): return lax.ppermute(v, 'x', SWAP)]
    psum x2 -> x0, blocking collectives: 75.6 us -> none  [the longest x1 40.5 us: local(): norm_sums = lax.psum((norms[0], norms[1], norms[2]), ('dp', 'tensor'))]
    while x216 -> x0, local copies, waits for them, and re-layouts: 54.3 us -> none  [the longest x14 24.9 us: local(): lax.map(slot_forward, (to_heads(query_h), to_heads(query_g), to_heads(key...]
  transfers between devices with their start and end apart: 40 -> 107, of which waited for: 32 -> 41; matrix products, arithmetic and copies ran while one was open for 16% -> 60% of each run, Pallas kernels for 0% -> 0%
where the time goes in v1:
time: 875 us; the launch traced here: 866 us
  matrix products  253 us (29%)
  local copies, waits for them, and re-layouts  214 us (24%)
  waiting for transfers between devices  201 us (23%)
  other arithmetic  114 us (13%)
  starting transfers between devices  76.4 us (9%)
    dot_general x68, matrix products, dot(): lax.dot_general(left, right, (numbers, ((), ())), preferred_element_type=...  133 us
    ppermute x36, waiting for transfers between devices, pz(): return lax.ppermute(v, 'z', self.ring)  115 us
    unnamed x609, local copies, waits for them, and re-layouts  78.8 us
    ppermute x26, waiting for transfers between devices, px(): return lax.ppermute(v, 'x', SWAP)  51.8 us
    dot_general x2, matrix products, local(): jnp.einsum('hij,bij->hb', ds_h.astype(f32) + ds_g.astype(f32), onehot, pr...  36.9 us
    ppermute x25, waiting for transfers between devices, py(): return lax.ppermute(v, 'y', SWAP)  29.6 us
    concatenate x10, local copies, waits for them, and re-layouts, local(): jnp.concatenate([by_x(query_grad), by_x(key_grad), by_x(value_grad), by_x...  27.6 us
    ppermute x26, starting transfers between devices, px(): return lax.ppermute(v, 'x', SWAP)  26.1 us
  transfers between devices with their start and end apart: 107, of which 41 were waited for; matrix products, arithmetic and copies ran while one was open for 60% of the time, Pallas kernels for 0%

profile of v1, /device:TPU:0, one launch (start us, length us, event | category | flops | bytes accessed | tf_op | source)
XLA Modules:
  0.0 865.5 jit_solution(16528715623646435871)
XLA Ops:
  30.5 12.4 %fusion.2 = f32[6,512,512]{2,0,1:T(8,128)} fusion(f32[6,32,1]{1,0,2:T(8,128)S(1)} %reshape.1155, s32[512,512]{1,0:T(8,128)S(1)} %fusion.140), kind=kOutput, calls=%fused_computation.3 | convolution fusion | flops 612368384 | bytes 7340800 | tf_op jit(solution)/shard_map/bij,hb->hij/dot_general | solution.py:341
  42.9 12.3 %fusion.3 = f32[6,512,512]{2,0,1:T(8,128)} fusion(f32[6,32,1]{1,0,2:T(8,128)S(1)} %reshape.1154, s32[512,512]{1,0:T(8,128)S(1)} %fusion.140), kind=kOutput, calls=%fused_computation.4 | convolution fusion | flops 612368384 | bytes 7340800 | tf_op jit(solution)/shard_map/bij,hb->hij/dot_general | solution.py:341
  55.6 9.1 %copy.145 = f32[6,512,512]{1,2,0:T(8,128)} copy(f32[6,512,512]{2,0,1:T(8,128)} %fusion.2) | data formatting | bytes 12582912 | tf_op jit(solution)/shard_map/bij,hb->hij/dot_general | solution.py:341
  64.7 9.1 %copy.140 = f32[6,512,512]{1,2,0:T(8,128)} copy(f32[6,512,512]{2,0,1:T(8,128)} %fusion.3) | data formatting | bytes 12582912 | tf_op jit(solution)/shard_map/bij,hb->hij/dot_general | solution.py:341
  89.3 8.6 collective-permute-done.33
  101.3 6.8 collective-permute-done.3
  113.0 6.7 collective-permute-done.23
  120.5 9.8 %collective-permute-done.34 = bf16[96,768]{0,1:T(8,128)(2,1)S(1)} collective-permute-done((bf16[96,768]{0,1:T(8,128)(2,1)}, bf16[96,768]{0,1:T(8,128)(2,1)S(1)}, u32[]{:S(2)}, u32[]{:S(2)}) %collective-permute-start.34) | collective-permute-done | bytes 147488 | tf_op jit(solution)/shard_map/ppermute | solution.py:86
  136.8 4.2 collective-permute-done.35
  143.2 5.5 collective-permute-done.36
  157.8 9.2 %collective-permute-done.7 = bf16[96,768]{0,1:T(8,128)(2,1)S(1)} collective-permute-done((bf16[96,768]{0,1:T(8,128)(2,1)S(1)}, bf16[96,768]{0,1:T(8,128)(2,1)S(1)}, u32[]{:S(2)}, u32[]{:S(2)}) %collective-permute-start.7) | collective-permute-done | bytes 147488 | tf_op jit(solution)/shard_map/ppermute | solution.py:80
  167.9 4.9 collective-permute-done.56
  173.6 11.4 %collective-permute-done.45 = bf16[2,96,768]{2,1,0:T(8,128)(2,1)S(1)} collective-permute-done((bf16[2,96,768]{2,1,0:T(8,128)(2,1)}, bf16[2,96,768]{2,1,0:T(8,128)(2,1)S(1)}, u32[]{:S(2)}, u32[]{:S(2)}) %collective-permute-start.45) | collective-permute-done | bytes 294944 | tf_op jit(solution)/shard_map/ppermute | solution.py:86
  192.5 6.4 collective-permute-done.53
  214.7 4.9 collective-permute-done.10
  220.1 7.9 collective-permute-done.11
  229.2 5.5 concatenate.131
  255.0 5.6 concatenate.145
  267.0 4.3 collective-permute-start.46
  296.0 7.2 collective-permute-done.29
  304.3 7.1 collective-permute-done.21
  385.1 4.8 convert_reduce_fusion
  394.9 5.0 add_convert_fusion
  421.7 4.6 multiply_reduce_fusion.2
  426.9 4.7 multiply_reduce_fusion.3
  431.6 8.7 %convert_add_fusion = (f32[6,512,512]{1,2,0:T(8,128)}, bf16[6,512,512]{1,2,0:T(8,128)(2,1)}, bf16[6,512,512]{1,2,0:T(8,128)(2,1)}) fusion(f32[6,512,512]{1,2,0:T(8,128)} %get-tuple-element.307, f32[6,512]{1,0:T(8,128)S(1)} %get-tuple-element.306, f32[6,512,512]{1,2,0:T(8,128)S(1)} %bitcast.726, f32[6,512]{1,0:T(8,128)S(1)} %log_add_fusion.2, ...), kind=kLoop, calls=%fused_computation.9 | loop fusion | flops 20447232 | bytes 38322176 | tf_op jit(solution)/shard_map/add | solution.py:398
  440.4 4.0 fusion.351
  483.4 9.6 %copy.215 = f32[6,512,512]{2,0,1:T(8,128)} copy(f32[6,512,512]{1,2,0:T(8,128)} %get-tuple-element.116) | data formatting | bytes 12582912 | tf_op jit(solution)/shard_map/add | solution.py:398
  495.2 18.5 %fusion.139 = f32[6,32]{1,0:T(8,128)S(1)} fusion(f32[6,512,512]{2,0,1:T(8,128)} %copy.215, s32[512,512]{1,0:T(8,128)} %copy-done.35), kind=kOutput, calls=%fused_computation.310 | convolution fusion | flops 612368384 | bytes 7340800 | tf_op jit(solution)/shard_map/hij,bij->hb/dot_general | solution.py:397
  548.5 4.6 fusion.314
  563.6 4.5 add_convert_fusion.3
  596.7 7.9 collective-permute-done.91
  628.2 4.7 multiply_reduce_fusion
  633.6 4.7 multiply_reduce_fusion.1
  638.3 8.8 %convert_add_fusion.1 = (f32[6,512,512]{1,2,0:T(8,128)}, bf16[6,512,512]{1,2,0:T(8,128)(2,1)S(1)}, bf16[6,512,512]{1,2,0:T(8,128)(2,1)}) fusion(f32[6,512,512]{1,2,0:T(8,128)} %get-tuple-element.311, f32[6,512]{1,0:T(8,128)S(1)} %get-tuple-element.310, f32[6,512,512]{1,2,0:T(8,128)S(1)} %bitcast.722, f32[6,512]{1,0:T(8,128)S(1)} %copy-done.202, ...), kind=kLoop, calls=%fused_computation.10 | loop fusion | flops 20447232 | bytes 38322176 | tf_op jit(solution)/shard_map/add | solution.py:398
  647.1 4.0 fusion.352
  658.2 5.1 convert_reduce_fusion.7
  691.4 9.7 %copy.214 = f32[6,512,512]{2,0,1:T(8,128)} copy(f32[6,512,512]{1,2,0:T(8,128)} %get-tuple-element.119) | data formatting | bytes 12582912 | tf_op jit(solution)/shard_map/add | solution.py:398
  701.1 18.5 %fusion.138 = f32[6,32]{1,0:T(8,128)S(1)} fusion(f32[6,512,512]{2,0,1:T(8,128)} %copy.214, s32[512,512]{1,0:T(8,128)S(1)} %copy-done.36), kind=kOutput, calls=%fused_computation.309 | convolution fusion | flops 612368384 | bytes 7340800 | tf_op jit(solution)/shard_map/hij,bij->hb/dot_general | solution.py:397
  759.1 4.1 collective-permute-done.80
  766.5 6.9 collective-permute-done.81
  775.7 11.1 %collective-permute-done.82 = bf16[96,768]{0,1:T(8,128)(2,1)S(1)} collective-permute-done((bf16[96,768]{0,1:T(8,128)(2,1)S(1)}, bf16[96,768]{0,1:T(8,128)(2,1)S(1)}, u32[]{:S(2)}, u32[]{:S(2)}) %collective-permute-start.82) | collective-permute-done | bytes 147488 | tf_op jit(solution)/shard_map/ppermute | solution.py:86
  789.0 9.5 %collective-permute-done.84 = bf16[2,96,768]{2,1,0:T(8,128)(2,1)S(1)} collective-permute-done((bf16[2,96,768]{2,1,0:T(8,128)(2,1)S(1)}, bf16[2,96,768]{2,1,0:T(8,128)(2,1)S(1)}, u32[]{:S(2)}, u32[]{:S(2)}) %collective-permute-start.84) | collective-permute-done | bytes 294944 | tf_op jit(solution)/shard_map/ppermute | solution.py:86
  806.7 4.2 collective-permute-done.85
  831.8 3.9 collective-permute-done.74
  838.7 7.1 collective-permute-done.75
  849.0 5.4 collective-permute-done.76
  856.5 5.6 collective-permute-done.77
  (1129 shorter events, 509.6 us)
Async XLA Ops:
  5.2 75.3 %collective-permute-start.31 = (bf16[96,768]{0,1:T(8,128)(2,1)}, bf16[96,768]{0,1:T(8,128)(2,1)}, u32[]{:S(2)}, u32[]{:S(2)}) collective-permute-start(bf16[96,768]{0,1:T(8,128)(2,1)} %get-tuple-element.244), channel_id=1, source_target_pairs={{0,2},{2,0},{1,3},{3,1},{4,6},{6,4},{5,7},{7,5},{8,10},{10,8},{9,1... | collective-permute-start | bytes 442376 | tf_op jit(solution)/shard_map/ppermute | solution.py:80
  8.1 75.7 %collective-permute-start.32 = (bf16[96,768]{0,1:T(8,128)(2,1)}, bf16[96,768]{0,1:T(8,128)(2,1)}, u32[]{:S(2)}, u32[]{:S(2)}) collective-permute-start(bf16[96,768]{0,1:T(8,128)(2,1)} %get-tuple-element.244), channel_id=1, source_target_pairs={{0,8},{8,16},{16,24},{24,0},{1,9},{9,17},{17,25},{25,1},{2,10},{10... | collective-permute-start | bytes 442376 | tf_op jit(solution)/shard_map/ppermute | solution.py:86
  9.9 18.9 %collective-permute-start.12 = (f32[2,1248]{1,0:T(2,128)S(1)}, f32[2,1248]{1,0:T(2,128)S(1)}, u32[]{:S(2)}, u32[]{:S(2)}) collective-permute-start(f32[2,1248]{1,0:T(2,128)S(1)} %concatenate.133), channel_id=1, source_target_pairs={{0,2},{2,0},{1,3},{3,1},{4,6},{6,4},{5,7},{7,5},{8,10},{10,8},{9,1... | collective-permute-start | bytes 29960 | tf_op jit(solution)/shard_map/ppermute | solution.py:80
  11.6 74.6 %collective-permute-start.1 = (bf16[96,768]{0,1:T(8,128)(2,1)}, bf16[96,768]{0,1:T(8,128)(2,1)}, u32[]{:S(2)}, u32[]{:S(2)}) collective-permute-start(bf16[96,768]{0,1:T(8,128)(2,1)} %get-tuple-element.246), channel_id=1, source_target_pairs={{0,2},{2,0},{1,3},{3,1},{4,6},{6,4},{5,7},{7,5},{8,10},{10,8},{9,1... | collective-permute-start | bytes 442376 | tf_op jit(solution)/shard_map/ppermute | solution.py:80
  13.9 63.4 %collective-permute-start.14 = (bf16[96,768]{1,0:T(8,128)(2,1)}, bf16[96,768]{1,0:T(8,128)(2,1)}, u32[]{:S(2)}, u32[]{:S(2)}) collective-permute-start(bf16[96,768]{1,0:T(8,128)(2,1)} %get-tuple-element.234), channel_id=1, source_target_pairs={{0,2},{2,0},{1,3},{3,1},{4,6},{6,4},{5,7},{7,5},{8,10},{10,8},{9,1... | collective-permute-start | bytes 442376 | tf_op jit(solution)/shard_map/ppermute | solution.py:80
  28.8 45.0 %collective-permute-start.43 = (bf16[96,768]{1,0:T(8,128)(2,1)}, bf16[96,768]{1,0:T(8,128)(2,1)}, u32[]{:S(2)}, u32[]{:S(2)}) collective-permute-start(bf16[96,768]{1,0:T(8,128)(2,1)} %get-tuple-element.235), channel_id=1, source_target_pairs={{0,2},{2,0},{1,3},{3,1},{4,6},{6,4},{5,7},{7,5},{8,10},{10,8},{9,1... | collective-permute-start | bytes 442376 | tf_op jit(solution)/shard_map/ppermute | solution.py:80
  83.8 120.6 %collective-permute-start.64 = (bf16[256,1536]{1,0:T(8,128)(2,1)}, bf16[256,1536]{1,0:T(8,128)(2,1)S(1)}, u32[]{:S(2)}, u32[]{:S(2)}) collective-permute-start(bf16[256,1536]{1,0:T(8,128)(2,1)} %constant_dynamic-update-slice_fusion.22), channel_id=1, source_target_pairs={{0,1},{1,0},{2,3},{3,2},{4,5},{5,4},{6,7},{7,6},{8,9},{9,8},{10,11... | collective-permute-start | bytes 2359304 | tf_op jit(solution)/shard_map/ppermute | solution.py:89
  83.8 27.0 %collective-permute-start.55 = (bf16[192,768]{1,0:T(8,128)(2,1)S(1)}, bf16[192,768]{1,0:T(8,128)(2,1)S(1)}, u32[]{:S(2)}, u32[]{:S(2)}) collective-permute-start(bf16[192,768]{1,0:T(8,128)(2,1)S(1)} %pad_maximum_fusion.36), channel_id=1, source_target_pairs={{0,2},{2,0},{1,3},{3,1},{4,6},{6,4},{5,7},{7,5},{8,10},{10,8},{9,1... | collective-permute-start | bytes 884744 | tf_op jit(solution)/shard_map/ppermute | solution.py:80
  86.2 23.6 %collective-permute-start.26 = (bf16[192,768]{1,0:T(8,128)(2,1)S(1)}, bf16[192,768]{1,0:T(8,128)(2,1)S(1)}, u32[]{:S(2)}, u32[]{:S(2)}) collective-permute-start(bf16[192,768]{1,0:T(8,128)(2,1)S(1)} %pad_maximum_fusion.34), channel_id=1, source_target_pairs={{0,2},{2,0},{1,3},{3,1},{4,6},{6,4},{5,7},{7,5},{8,10},{10,8},{9,1... | collective-permute-start | bytes 884744 | tf_op jit(solution)/shard_map/ppermute | solution.py:80
  87.7 20.3 %collective-permute-start.3 = (bf16[96,768]{0,1:T(8,128)(2,1)S(1)}, bf16[96,768]{0,1:T(8,128)(2,1)S(1)}, u32[]{:S(2)}, u32[]{:S(2)}) collective-permute-start(bf16[96,768]{0,1:T(8,128)(2,1)S(1)} %collective-permute-done.2), channel_id=1, source_target_pairs={{0,2},{2,0},{1,3},{3,1},{4,6},{6,4},{5,7},{7,5},{8,10},{10,8},{9,1... | collective-permute-start | bytes 442376 | tf_op jit(solution)/shard_map/ppermute | solution.py:80
  97.9 36.8 %collective-permute-start.52 = (bf16[192,768]{1,0:T(8,128)(2,1)S(1)}, bf16[192,768]{1,0:T(8,128)(2,1)S(1)}, u32[]{:S(2)}, u32[]{:S(2)}) collective-permute-start(bf16[192,768]{1,0:T(8,128)(2,1)S(1)} %pad_maximum_fusion.36), channel_id=1, source_target_pairs={{0,8},{8,16},{16,24},{24,0},{1,9},{9,17},{17,25},{25,1},{2,10},{10... | collective-permute-start | bytes 884744 | tf_op jit(solution)/shard_map/ppermute | solution.py:86
  109.8 38.9 %collective-permute-start.44 = (bf16[2,96,768]{2,1,0:T(8,128)(2,1)S(1)}, bf16[2,96,768]{2,1,0:T(8,128)(2,1)}, u32[]{:S(2)}, u32[]{:S(2)}) collective-permute-start(bf16[2,96,768]{2,1,0:T(8,128)(2,1)S(1)} %get-tuple-element.241), channel_id=1, source_target_pairs={{0,8},{8,16},{16,24},{24,0},{1,9},{9,17},{17,25},{25,1},{2,10},{10... | collective-permute-start | bytes 884744 | tf_op jit(solution)/shard_map/ppermute | solution.py:86
  110.8 19.5 %collective-permute-start.34 = (bf16[96,768]{0,1:T(8,128)(2,1)}, bf16[96,768]{0,1:T(8,128)(2,1)S(1)}, u32[]{:S(2)}, u32[]{:S(2)}) collective-permute-start(bf16[96,768]{0,1:T(8,128)(2,1)} %collective-permute-done.32), channel_id=1, source_target_pairs={{0,8},{8,16},{16,24},{24,0},{1,9},{9,17},{17,25},{25,1},{2,10},{10... | collective-permute-start | bytes 442376 | tf_op jit(solution)/shard_map/ppermute | solution.py:86
  130.3 22.2 %collective-permute-start.15 = (bf16[2,96,768]{2,1,0:T(8,128)(2,1)S(1)}, bf16[2,96,768]{2,1,0:T(8,128)(2,1)S(1)}, u32[]{:S(2)}, u32[]{:S(2)}) collective-permute-start(bf16[2,96,768]{2,1,0:T(8,128)(2,1)S(1)} %get-tuple-element.231), channel_id=1, source_target_pairs={{0,8},{8,16},{16,24},{24,0},{1,9},{9,17},{17,25},{25,1},{2,10},{10... | collective-permute-start | bytes 884744 | tf_op jit(solution)/shard_map/ppermute | solution.py:86
  148.7 52.3 %collective-permute-start = (bf16[256,1536]{1,0:T(8,128)(2,1)S(1)}, bf16[256,1536]{1,0:T(8,128)(2,1)S(1)}, u32[]{:S(2)}, u32[]{:S(2)}) collective-permute-start(bf16[256,1536]{1,0:T(8,128)(2,1)S(1)} %constant_dynamic-update-slice_fusion), channel_id=1, source_target_pairs={{0,1},{1,0},{2,3},{3,2},{4,5},{5,4},{6,7},{7,6},{8,9},{9,8},{10,11... | collective-permute-start | bytes 2359304 | tf_op jit(solution)/shard_map/ppermute | solution.py:89
  167.0 23.5 %collective-permute-start.24 = (bf16[192,768]{1,0:T(8,128)(2,1)S(1)}, bf16[192,768]{1,0:T(8,128)(2,1)}, u32[]{:S(2)}, u32[]{:S(2)}) collective-permute-start(bf16[192,768]{1,0:T(8,128)(2,1)S(1)} %collective-permute-done.23), channel_id=1, source_target_pairs={{0,8},{8,16},{16,24},{24,0},{1,9},{9,17},{17,25},{25,1},{2,10},{10... | collective-permute-start | bytes 884744 | tf_op jit(solution)/shard_map/ppermute | solution.py:86
  185.0 27.6 %collective-permute-start.8 = (bf16[2,96,768]{1,2,0:T(8,128)(2,1)S(1)}, bf16[2,96,768]{1,2,0:T(8,128)(2,1)S(1)}, u32[]{:S(2)}, u32[]{:S(2)}) collective-permute-start(bf16[2,96,768]{1,2,0:T(8,128)(2,1)S(1)} %pad_maximum_fusion.17), channel_id=1, source_target_pairs={{0,4},{4,0},{1,5},{5,1},{2,6},{6,2},{3,7},{7,3},{8,12},{12,8},{9,1... | collective-permute-start | bytes 884744 | tf_op jit(solution)/shard_map/ppermute | solution.py:83
  190.4 61.4 %collective-permute-start.38 = (bf16[2,96,768]{1,2,0:T(8,128)(2,1)}, bf16[2,96,768]{1,2,0:T(8,128)(2,1)}, u32[]{:S(2)}, u32[]{:S(2)}) collective-permute-start(bf16[2,96,768]{1,2,0:T(8,128)(2,1)} %pad_maximum_fusion.21), channel_id=1, source_target_pairs={{0,4},{4,0},{1,5},{5,1},{2,6},{6,2},{3,7},{7,3},{8,12},{12,8},{9,1... | collective-permute-start | bytes 884744 | tf_op jit(solution)/shard_map/ppermute | solution.py:83
  201.0 18.5 %collective-permute-start.10 = (bf16[2,96,768]{1,2,0:T(8,128)(2,1)S(1)}, bf16[2,96,768]{1,2,0:T(8,128)(2,1)S(1)}, u32[]{:S(2)}, u32[]{:S(2)}) collective-permute-start(bf16[2,96,768]{1,2,0:T(8,128)(2,1)S(1)} %pad_maximum_fusion.19), channel_id=1, source_target_pairs={{0,4},{4,0},{1,5},{5,1},{2,6},{6,2},{3,7},{7,3},{8,12},{12,8},{9,1... | collective-permute-start | bytes 884744 | tf_op jit(solution)/shard_map/ppermute | solution.py:83
  204.4 23.6 %collective-permute-start.11 = (bf16[2,96,768]{1,2,0:T(8,128)(2,1)S(1)}, bf16[2,96,768]{1,2,0:T(8,128)(2,1)S(1)}, u32[]{:S(2)}, u32[]{:S(2)}) collective-permute-start(bf16[2,96,768]{1,2,0:T(8,128)(2,1)S(1)} %pad_maximum_fusion.20), channel_id=1, source_target_pairs={{0,4},{4,0},{1,5},{5,1},{2,6},{6,2},{3,7},{7,3},{8,12},{12,8},{9,1... | collective-permute-start | bytes 884744 | tf_op jit(solution)/shard_map/ppermute | solution.py:83
  212.6 39.8 %collective-permute-start.39 = (bf16[2,96,768]{1,2,0:T(8,128)(2,1)}, bf16[2,96,768]{1,2,0:T(8,128)(2,1)}, u32[]{:S(2)}, u32[]{:S(2)}) collective-permute-start(bf16[2,96,768]{1,2,0:T(8,128)(2,1)} %pad_maximum_fusion.22), channel_id=1, source_target_pairs={{0,4},{4,0},{1,5},{5,1},{2,6},{6,2},{3,7},{7,3},{8,12},{12,8},{9,1... | collective-permute-start | bytes 884744 | tf_op jit(solution)/shard_map/ppermute | solution.py:83
  214.2 39.7 %collective-permute-start.40 = (bf16[2,96,768]{1,2,0:T(8,128)(2,1)}, bf16[2,96,768]{1,2,0:T(8,128)(2,1)}, u32[]{:S(2)}, u32[]{:S(2)}) collective-permute-start(bf16[2,96,768]{1,2,0:T(8,128)(2,1)} %pad_maximum_fusion.23), channel_id=1, source_target_pairs={{0,4},{4,0},{1,5},{5,1},{2,6},{6,2},{3,7},{7,3},{8,12},{12,8},{9,1... | collective-permute-start | bytes 884744 | tf_op jit(solution)/shard_map/ppermute | solution.py:83
  219.5 34.9 %collective-permute-start.41 = (bf16[2,96,768]{1,2,0:T(8,128)(2,1)}, bf16[2,96,768]{1,2,0:T(8,128)(2,1)}, u32[]{:S(2)}, u32[]{:S(2)}) collective-permute-start(bf16[2,96,768]{1,2,0:T(8,128)(2,1)} %pad_maximum_fusion.24), channel_id=1, source_target_pairs={{0,4},{4,0},{1,5},{5,1},{2,6},{6,2},{3,7},{7,3},{8,12},{12,8},{9,1... | collective-permute-start | bytes 884744 | tf_op jit(solution)/shard_map/ppermute | solution.py:83
  228.7 34.0 %collective-permute-start.25 = (bf16[192,768]{1,0:T(8,128)(2,1)}, bf16[192,768]{1,0:T(8,128)(2,1)}, u32[]{:S(2)}, u32[]{:S(2)}) collective-permute-start(bf16[192,768]{1,0:T(8,128)(2,1)} %collective-permute-done.24), channel_id=1, source_target_pairs={{0,8},{8,16},{16,24},{24,0},{1,9},{9,17},{17,25},{25,1},{2,10},{10... | collective-permute-start | bytes 884744 | tf_op jit(solution)/shard_map/ppermute | solution.py:86
  251.8 29.2 %collective-permute-start.47 = (bf16[2,96,768]{2,1,0:T(8,128)(2,1)S(1)}, bf16[2,96,768]{2,1,0:T(8,128)(2,1)}, u32[]{:S(2)}, u32[]{:S(2)}) collective-permute-start(bf16[2,96,768]{2,1,0:T(8,128)(2,1)S(1)} %copy-done.182), channel_id=1, source_target_pairs={{0,4},{4,0},{1,5},{5,1},{2,6},{6,2},{3,7},{7,3},{8,12},{12,8},{9,1... | collective-permute-start | bytes 884744 | tf_op jit(solution)/shard_map/ppermute | solution.py:83
  252.4 35.5 %collective-permute-start.18 = (bf16[2,96,768]{2,1,0:T(8,128)(2,1)S(1)}, bf16[2,96,768]{2,1,0:T(8,128)(2,1)}, u32[]{:S(2)}, u32[]{:S(2)}) collective-permute-start(bf16[2,96,768]{2,1,0:T(8,128)(2,1)S(1)} %copy-done.180), channel_id=1, source_target_pairs={{0,4},{4,0},{1,5},{5,1},{2,6},{6,2},{3,7},{7,3},{8,12},{12,8},{9,1... | collective-permute-start | bytes 884744 | tf_op jit(solution)/shard_map/ppermute | solution.py:83
  253.9 29.4 %collective-permute-start.48 = (bf16[2,96,768]{2,1,0:T(8,128)(2,1)}, bf16[2,96,768]{2,1,0:T(8,128)(2,1)}, u32[]{:S(2)}, u32[]{:S(2)}) collective-permute-start(bf16[2,96,768]{2,1,0:T(8,128)(2,1)} %collective-permute-done.44), channel_id=1, source_target_pairs={{0,4},{4,0},{1,5},{5,1},{2,6},{6,2},{3,7},{7,3},{8,12},{12,8},{9,1... | collective-permute-start | bytes 884744 | tf_op jit(solution)/shard_map/ppermute | solution.py:83
  283.3 46.8 %collective-permute-start.49 = (bf16[2,96,768]{2,1,0:T(8,128)(2,1)S(1)}, bf16[2,96,768]{2,1,0:T(8,128)(2,1)S(1)}, u32[]{:S(2)}, u32[]{:S(2)}) collective-permute-start(bf16[2,96,768]{2,1,0:T(8,128)(2,1)S(1)} %copy-done.190), channel_id=1, source_target_pairs={{0,4},{4,0},{1,5},{5,1},{2,6},{6,2},{3,7},{7,3},{8,12},{12,8},{9,1... | collective-permute-start | bytes 884744 | tf_op jit(solution)/shard_map/ppermute | solution.py:83
  287.9 28.0 %collective-permute-start.13 = (bf16[512,768]{1,0:T(8,128)(2,1)}, bf16[512,768]{1,0:T(8,128)(2,1)S(1)}, u32[]{:S(2)}, u32[]{:S(2)}) collective-permute-start(bf16[512,768]{1,0:T(8,128)(2,1)} %convolution_convert_fusion.13), channel_id=1, source_target_pairs={{0,1},{1,0},{2,3},{3,2},{4,5},{5,4},{6,7},{7,6},{8,9},{9,8},{10,11... | collective-permute-start | bytes 2359304 | tf_op jit(solution)/shard_map/ppermute | solution.py:89
  289.6 26.3 %collective-permute-start.60 = (bf16[512,768]{1,0:T(8,128)(2,1)}, bf16[512,768]{1,0:T(8,128)(2,1)S(1)}, u32[]{:S(2)}, u32[]{:S(2)}) collective-permute-start(bf16[512,768]{1,0:T(8,128)(2,1)} %convolution_convert_fusion.11), channel_id=1, source_target_pairs={{0,1},{1,0},{2,3},{3,2},{4,5},{5,4},{6,7},{7,6},{8,9},{9,8},{10,11... | collective-permute-start | bytes 2359304 | tf_op jit(solution)/shard_map/ppermute | solution.py:89
  295.3 35.5 %collective-permute-start.58 = (bf16[192,768]{1,0:T(8,128)(2,1)}, bf16[192,768]{1,0:T(8,128)(2,1)S(1)}, u32[]{:S(2)}, u32[]{:S(2)}) collective-permute-start(bf16[192,768]{1,0:T(8,128)(2,1)} %collective-permute-done.54), channel_id=1, source_target_pairs={{0,2},{2,0},{1,3},{3,1},{4,6},{6,4},{5,7},{7,5},{8,10},{10,8},{9,1... | collective-permute-start | bytes 884744 | tf_op jit(solution)/shard_map/ppermute | solution.py:80
  311.5 38.5 %collective-permute-start.50 = (bf16[2,96,768]{2,1,0:T(8,128)(2,1)S(1)}, bf16[2,96,768]{2,1,0:T(8,128)(2,1)S(1)}, u32[]{:S(2)}, u32[]{:S(2)}) collective-permute-start(bf16[2,96,768]{2,1,0:T(8,128)(2,1)S(1)} %collective-permute-done.46), channel_id=1, source_target_pairs={{0,4},{4,0},{1,5},{5,1},{2,6},{6,2},{3,7},{7,3},{8,12},{12,8},{9,1... | collective-permute-start | bytes 884744 | tf_op jit(solution)/shard_map/ppermute | solution.py:83
  402.5 111.1 %collective-permute-start.98 = (bf16[2,4,96,768]{3,2,0,1:T(8,128)(2,1)}, bf16[2,4,96,768]{3,2,0,1:T(8,128)(2,1)}, u32[]{:S(2)}, u32[]{:S(2)}) collective-permute-start(bf16[2,4,96,768]{3,2,0,1:T(8,128)(2,1)} %copy_bitcast_fusion.4), channel_id=1, source_target_pairs={{0,4},{4,0},{1,5},{5,1},{2,6},{6,2},{3,7},{7,3},{8,12},{12,8},{9,1... | collective-permute-start | bytes 3538952 | tf_op jit(solution)/shard_map/ppermute | solution.py:83
  406.7 109.2 %collective-permute-start.88 = (bf16[2,4,96,768]{3,2,0,1:T(8,128)(2,1)}, bf16[2,4,96,768]{3,2,0,1:T(8,128)(2,1)}, u32[]{:S(2)}, u32[]{:S(2)}) collective-permute-start(bf16[2,4,96,768]{3,2,0,1:T(8,128)(2,1)} %copy.199), channel_id=1, source_target_pairs={{0,2},{2,0},{1,3},{3,1},{4,6},{6,4},{5,7},{7,5},{8,10},{10,8},{9,1... | collective-permute-start | bytes 3538952 | tf_op jit(solution)/shard_map/ppermute | solution.py:80
  473.4 61.6 %collective-permute-start.69 = (bf16[512,768]{1,0:T(8,128)(2,1)}, bf16[512,768]{1,0:T(8,128)(2,1)}, u32[]{:S(2)}, u32[]{:S(2)}) collective-permute-start(bf16[512,768]{1,0:T(8,128)(2,1)} %convolution_convert_fusion.9), channel_id=1, source_target_pairs={{0,1},{1,0},{2,3},{3,2},{4,5},{5,4},{6,7},{7,6},{8,9},{9,8},{10,11... | collective-permute-start | bytes 2359304 | tf_op jit(solution)/shard_map/ppermute | solution.py:89
  477.0 58.0 %collective-permute-start.67 = (bf16[512,768]{1,0:T(8,128)(2,1)}, bf16[512,768]{1,0:T(8,128)(2,1)}, u32[]{:S(2)}, u32[]{:S(2)}) collective-permute-start(bf16[512,768]{1,0:T(8,128)(2,1)} %add_convert_fusion.5), channel_id=1, source_target_pairs={{0,1},{1,0},{2,3},{3,2},{4,5},{5,4},{6,7},{7,6},{8,9},{9,8},{10,11... | collective-permute-start | bytes 2359304 | tf_op jit(solution)/shard_map/ppermute | solution.py:89
  526.3 49.9 %collective-permute-start.78 = (bf16[2,4,96,768]{3,2,1,0:T(8,128)(2,1)}, bf16[2,4,96,768]{3,2,1,0:T(8,128)(2,1)}, u32[]{:S(2)}, u32[]{:S(2)}) collective-permute-start(bf16[2,4,96,768]{3,2,1,0:T(8,128)(2,1)} %copy.181), channel_id=1, source_target_pairs={{0,4},{4,0},{1,5},{5,1},{2,6},{6,2},{3,7},{7,3},{8,12},{12,8},{9,1... | collective-permute-start | bytes 3538952 | tf_op jit(solution)/shard_map/ppermute | solution.py:83
  529.4 40.7 %collective-permute-start.100 = (bf16[2,96,768]{2,1,0:T(8,128)(2,1)}, bf16[2,96,768]{2,1,0:T(8,128)(2,1)}, u32[]{:S(2)}, u32[]{:S(2)}) collective-permute-start(bf16[2,96,768]{2,1,0:T(8,128)(2,1)} %fusion.173), channel_id=1, source_target_pairs={{0,8},{8,16},{16,24},{24,0},{1,9},{9,17},{17,25},{25,1},{2,10},{10... | collective-permute-start | bytes 884744 | tf_op jit(solution)/shard_map/ppermute | solution.py:86
  535.0 38.2 %collective-permute-start.90 = (bf16[2,96,768]{2,1,0:T(8,128)(2,1)}, bf16[2,96,768]{2,1,0:T(8,128)(2,1)}, u32[]{:S(2)}, u32[]{:S(2)}) collective-permute-start(bf16[2,96,768]{2,1,0:T(8,128)(2,1)} %fusion.185), channel_id=1, source_target_pairs={{0,8},{8,16},{16,24},{24,0},{1,9},{9,17},{17,25},{25,1},{2,10},{10... | collective-permute-start | bytes 884744 | tf_op jit(solution)/shard_map/ppermute | solution.py:86
  558.5 58.0 %collective-permute-start.70 = (bf16[512,768]{1,0:T(8,128)(2,1)}, bf16[512,768]{1,0:T(8,128)(2,1)}, u32[]{:S(2)}, u32[]{:S(2)}) collective-permute-start(bf16[512,768]{1,0:T(8,128)(2,1)} %convolution_convert_fusion), channel_id=1, source_target_pairs={{0,1},{1,0},{2,3},{3,2},{4,5},{5,4},{6,7},{7,6},{8,9},{9,8},{10,11... | collective-permute-start | bytes 2359304 | tf_op jit(solution)/shard_map/ppermute | solution.py:89
  563.1 53.5 %collective-permute-start.68 = (bf16[512,768]{1,0:T(8,128)(2,1)}, bf16[512,768]{1,0:T(8,128)(2,1)}, u32[]{:S(2)}, u32[]{:S(2)}) collective-permute-start(bf16[512,768]{1,0:T(8,128)(2,1)} %convolution_convert_fusion.1), channel_id=1, source_target_pairs={{0,1},{1,0},{2,3},{3,2},{4,5},{5,4},{6,7},{7,6},{8,9},{9,8},{10,11... | collective-permute-start | bytes 2359304 | tf_op jit(solution)/shard_map/ppermute | solution.py:89
  570.2 195.1 %collective-permute-start.93 = (bf16[2,4,96,768]{3,2,0,1:T(8,128)(2,1)}, bf16[2,4,96,768]{3,2,0,1:T(8,128)(2,1)}, u32[]{:S(2)}, u32[]{:S(2)}) collective-permute-start(bf16[2,4,96,768]{3,2,0,1:T(8,128)(2,1)} %copy_bitcast_fusion.5), channel_id=1, source_target_pairs={{0,4},{4,0},{1,5},{5,1},{2,6},{6,2},{3,7},{7,3},{8,12},{12,8},{9,1... | collective-permute-start | bytes 3538952 | tf_op jit(solution)/shard_map/ppermute | solution.py:83
  573.1 201.3 %collective-permute-start.83 = (bf16[2,4,96,768]{3,2,0,1:T(8,128)(2,1)}, bf16[2,4,96,768]{3,2,0,1:T(8,128)(2,1)}, u32[]{:S(2)}, u32[]{:S(2)}) collective-permute-start(bf16[2,4,96,768]{3,2,0,1:T(8,128)(2,1)} %copy.194), channel_id=1, source_target_pairs={{0,2},{2,0},{1,3},{3,1},{4,6},{6,4},{5,7},{7,5},{8,10},{10,8},{9,1... | collective-permute-start | bytes 3538952 | tf_op jit(solution)/shard_map/ppermute | solution.py:80
  614.9 134.1 %collective-permute-start.79 = (bf16[4,96,768]{2,1,0:T(8,128)(2,1)}, bf16[4,96,768]{2,1,0:T(8,128)(2,1)}, u32[]{:S(2)}, u32[]{:S(2)}) collective-permute-start(bf16[4,96,768]{2,1,0:T(8,128)(2,1)} %copy.184), channel_id=1, source_target_pairs={{0,2},{2,0},{1,3},{3,1},{4,6},{6,4},{5,7},{7,5},{8,10},{10,8},{9,1... | collective-permute-start | bytes 1769480 | tf_op jit(solution)/shard_map/ppermute | solution.py:80
  691.4 108.4 %collective-permute-start.72 = (bf16[512,768]{1,0:T(8,128)(2,1)}, bf16[512,768]{1,0:T(8,128)(2,1)}, u32[]{:S(2)}, u32[]{:S(2)}) collective-permute-start(bf16[512,768]{1,0:T(8,128)(2,1)} %convolution_convert_fusion.8), channel_id=1, source_target_pairs={{0,1},{1,0},{2,3},{3,2},{4,5},{5,4},{6,7},{7,6},{8,9},{9,8},{10,11... | collective-permute-start | bytes 2359304 | tf_op jit(solution)/shard_map/ppermute | solution.py:89
  746.8 55.6 %collective-permute-start.71 = (bf16[512,768]{1,0:T(8,128)(2,1)S(1)}, bf16[512,768]{1,0:T(8,128)(2,1)}, u32[]{:S(2)}, u32[]{:S(2)}) collective-permute-start(bf16[512,768]{1,0:T(8,128)(2,1)S(1)} %copy-done.137), channel_id=1, source_target_pairs={{0,1},{1,0},{2,3},{3,2},{4,5},{5,4},{6,7},{7,6},{8,9},{9,8},{10,11... | collective-permute-start | bytes 2359304 | tf_op jit(solution)/shard_map/ppermute | solution.py:89
  763.3 49.5 %collective-permute-start.73 = (bf16[2,4,96,768]{3,2,1,0:T(8,128)(2,1)}, bf16[2,4,96,768]{3,2,1,0:T(8,128)(2,1)S(1)}, u32[]{:S(2)}, u32[]{:S(2)}) collective-permute-start(bf16[2,4,96,768]{3,2,1,0:T(8,128)(2,1)} %copy.164), channel_id=1, source_target_pairs={{0,4},{4,0},{1,5},{5,1},{2,6},{6,2},{3,7},{7,3},{8,12},{12,8},{9,1... | collective-permute-start | bytes 3538952 | tf_op jit(solution)/shard_map/ppermute | solution.py:83
  806.7 19.7 %collective-permute-start.96 = (bf16[2,96,768]{2,1,0:T(8,128)(2,1)}, bf16[2,96,768]{2,1,0:T(8,128)(2,1)}, u32[]{:S(2)}, u32[]{:S(2)}) collective-permute-start(bf16[2,96,768]{2,1,0:T(8,128)(2,1)} %fusion.181), channel_id=1, source_target_pairs={{0,8},{8,16},{16,24},{24,0},{1,9},{9,17},{17,25},{25,1},{2,10},{10... | collective-permute-start | bytes 884744 | tf_op jit(solution)/shard_map/ppermute | solution.py:86
  (325 other events, 3840.9 us)

commit v2 on v1

v2 whole, which is shorter than its diff:
```python
import functools

import jax
import jax.numpy as jnp
from jax import lax
from jax.experimental import pallas as pl
from jax.experimental.pallas import tpu as pltpu
from jax.sharding import Mesh, PartitionSpec as P

HEAD = 64
BUCKETS = 32
LAYERS = 2
SEQ = 512
TILE = 128
NEAR = 5

epsilon = 1e-05
limits = (12, 16, 23, 32, 46, 64, 91)
highest = lax.Precision.HIGHEST
f32 = jnp.float32
bf16 = jnp.bfloat16
SWAP = [(0, 1), (1, 0)]
GATHER = (("zxy", "xzy", "yzx"), ("zyx", "xzy", "yzx"))
SCATTER = ("xyz", "yxz")
ANY = pl.BlockSpec(memory_space=pl.ANY)
VMEM = pl.BlockSpec(memory_space=pltpu.VMEM)


def dot(left, right, numbers):
    return lax.dot_general(left, right, (numbers, ((), ())), preferred_element_type=f32)


def nn(left, right):
    return dot(left, right, ((1,), (0,)))


def nt(left, right):
    return dot(left, right, ((1,), (1,)))


def tn(left, right):
    return dot(left, right, ((0,), (0,)))


def bucket_of(offset):
    distance = jnp.abs(offset)
    farther = 8 + sum(((distance >= border).astype(jnp.int32) for border in limits))
    return jnp.where(distance < 8, distance, farther) + 16 * (offset > 0).astype(jnp.int32)


def slot_masks(piece_lengths, ranks, chosen):
    places = jnp.arange(SEQ, dtype=jnp.int32)
    first = piece_lengths[0]
    second = first + piece_lengths[1]
    third = second + piece_lengths[2]
    segment = (
        (places >= first).astype(jnp.int32)
        + (places >= second).astype(jnp.int32)
        + (places >= third).astype(jnp.int32)
    )
    leading = jnp.where(
        segment == 0,
        0,
        jnp.where(segment == 1, first, jnp.where(segment == 2, second, third)),
    )
    same_doc = segment[:, None] == segment[None, :]
    visible = chosen[:, None] == 0
    content = same_doc & (visible | (ranks[:, None] <= ranks[None, :]))
    query = same_doc & (
        (places[:, None] == leading[None, :])
        | visible & (places[:, None] != places[None, :])
        | (ranks[:, None] < ranks[None, :])
    )
    return jnp.where(jnp.stack([content, query]), 0.0, -1e30).astype(f32)


def tile_buckets():
    near = jnp.arange(NEAR, dtype=jnp.int32)[:, None, None] - NEAR // 2
    key = jnp.arange(TILE, dtype=jnp.int32)[None, :, None]
    query = jnp.arange(TILE, dtype=jnp.int32)[None, None, :]
    return bucket_of(near * TILE + key - query)


class Links:
    def __init__(self, mesh):
        dp = mesh.shape["dp"]
        self.routed = dp == 8
        self.ny = 2
        self.nz = dp // 2
        self.nx = mesh.shape["tensor"] // 2
        self.mesh = Mesh(
            mesh.devices.reshape(self.nz, self.ny, self.nx, 2), ("z", "y", "x", "core")
        )
        self.ring = [(i, (i + 1) % self.nz) for i in range(self.nz)]

    def swap(self, v, axis):
        return lax.ppermute(v, axis, SWAP)

    def pz(self, v):
        return lax.ppermute(v, "z", self.ring)

    def pc(self, v):
        return lax.ppermute(v, "core", SWAP)

    def feature_order(self, width):
        count = self.nz * self.ny
        depth = width // count
        place = jnp.arange(width, dtype=jnp.int32)
        if not self.routed:
            return place
        block, rest = place // depth, place % depth
        ky, kz = block // self.nz, block % self.nz
        z = lax.rem(lax.axis_index("z") - kz + self.nz, self.nz)
        y = jnp.bitwise_xor(lax.axis_index("y"), ky)
        return (z * self.ny + y) * depth + rest

    def gather(self, block, route):
        if not self.routed:
            rows = lax.all_gather(block, ("z", "y"), axis=0, tiled=True)
            return Weight([lax.all_gather(rows, "x", axis=0)], (((0, 0), (1, 0)),))
        depth = block.shape[0]
        a, b = route.replace("z", "")
        held = [block if route[0] == "z" else jnp.stack([block, self.swap(block, a)])]
        for _ in range(self.nz - 1):
            held.append(self.pz(held[-1]))
        if route[0] == "z":
            held = [jnp.stack([h, self.swap(h, a)]) for h in held]
        pieces = held + [self.swap(h, b) for h in held]
        spots = []
        for other in range(2):
            for k in range(self.nz):
                pair = []
                for j in range(2):
                    x, y = (j, other) if a == "x" else (other, j)
                    pair.append((x, (y * self.nz + k) * depth))
                spots.append(tuple(pair))
        return Weight(pieces, tuple(spots))

    def scatter(self, keep, send, route):
        whole = jnp.concatenate([keep, send], axis=1)
        if route[0] == "x":
            whole = jnp.stack([keep.reshape(-1, keep.shape[2]), send.reshape(-1, send.shape[2])])
        mine = lax.psum_scatter(whole, "x", scatter_dimension=0, tiled=False)
        return lax.psum_scatter(mine, ("z", "y"), scatter_dimension=0, tiled=True).astype(f32)

    def pair(self, v):
        if not self.routed:
            return lax.all_gather(v, "x", axis=0)
        return jnp.stack([v, self.swap(v, "x")])

    def total(self, split, whole):
        if not self.routed:
            mine = lax.psum_scatter(split, "x", scatter_dimension=0, tiled=False)
            return lax.psum(mine, ("z", "y")), lax.psum(whole, ("z", "y", "x"))
        n = split.shape[1]
        count = n + whole.shape[0]
        filler = jnp.zeros((-count % 128,), f32)
        sent = jnp.concatenate([split[1], whole, filler]).reshape(-1, 128)
        kept = jnp.concatenate([split[0], whole, filler]).reshape(-1, 128)
        v = kept + self.swap(sent, "x")
        v = v + self.swap(v, "y")
        step = 1
        while step < self.nz:
            v = v + lax.ppermute(v, "z", [(i, i ^ step) for i in range(self.nz)])
            step *= 2
        v = v.reshape(-1)
        return v[:n], v[n:count]

    def both_rows(self, v):
        other = self.pc(v)
        first = lax.axis_index("core") == 0
        return jnp.concatenate([jnp.where(first, v, other), jnp.where(first, other, v)])


class Chain:
    last = ()

    def call(self, body, inputs, in_specs, outs, out_specs, flops, grid=(), scratch=(), after=()):
        waits = [*self.last, *after]
        count = len(inputs)

        def rest(*refs):
            body(*refs[:count], *refs[count + len(waits) :])

        made = pl.pallas_call(
            rest,
            out_shape=[jax.ShapeDtypeStruct(*o) for o in outs],
            grid=grid,
            in_specs=[*in_specs, *[ANY] * len(waits)],
            out_specs=out_specs,
            scratch_shapes=list(scratch),
            compiler_params=pltpu.CompilerParams(vmem_limit_bytes=48 << 20),
            cost_estimate=pl.CostEstimate(
                flops=4 * flops, bytes_accessed=0, transcendentals=0
            ),
        )(*inputs, *waits)
        self.last = (min(made, key=lambda v: v.size),)
        return made


class Weight:
    def __init__(self, arrays, spots):
        self.arrays = arrays
        self.spots = spots
        self.width = arrays[0].shape[2]

    def specs(self, grid):
        return [fixed(*v.shape) if grid else VMEM for v in self.arrays]

    def join(self, refs, target):
        for piece, places in zip(refs, self.spots):
            rows = piece.shape[1]
            for j, (x, row) in enumerate(places):
                target[x, row : row + rows] = piece[j]


def fold_sums(chain, arrays, wanted):
    inputs = [v for group in arrays for v in group]
    first = [sum(len(group) for group in arrays[:n]) for n in range(len(arrays))]
    outs = []
    for rows, dtype in wanted:
        which, index = rows[0]
        shape = jax.eval_shape(lambda v: v[index], arrays[which][0]).shape
        outs.append((shape if len(rows) == 1 else (len(rows), *shape), dtype))

    def body(*refs):
        for out, (rows, dtype) in zip(refs[len(inputs) :], wanted):
            for n, (which, index) in enumerate(rows):
                group = refs[first[which] : first[which] + len(arrays[which])]
                total = sum(ref[index].astype(f32) for ref in group).astype(dtype)
                if len(rows) == 1:
                    out[...] = total
                else:
                    out[n] = total

    return chain.call(
        body,
        inputs,
        [VMEM] * len(inputs),
        outs,
        [VMEM] * len(outs),
        flops=sum(v.size for v in inputs),
    )


class Scatter:
    def __init__(self, chain, links, parts):
        self.chain = chain
        self.links = links
        self.routes = [route for _, _, route in parts]
        self.depth = parts[0][0].shape[1] // links.nz
        if links.routed:
            self.sums = [[keep, links.swap(send, route[0])] for keep, send, route in parts]
        else:
            self.sums = [links.scatter(*part) for part in parts]

    def second(self):
        if not self.links.routed:
            return
        wanted = [([(n, (i,))], bf16 if i else f32) for n in range(len(self.routes)) for i in range(2)]
        made = fold_sums(self.chain, self.sums, wanted)
        self.sums = [
            [made[2 * n], self.links.swap(made[2 * n + 1], route[1])]
            for n, route in enumerate(self.routes)
        ]

    def third(self):
        links = self.links
        if not links.routed:
            return
        wanted = []
        for k in range(links.nz):
            at = (slice(k * self.depth, (k + 1) * self.depth),)
            wanted.append(([(n, at) for n in range(len(self.routes))], bf16 if k else f32))
        made = fold_sums(self.chain, self.sums, wanted)
        self.sums = [made[0]]
        for k in range(1, links.nz):
            to = [(i, (i - k) % links.nz) for i in range(links.nz)]
            self.sums.append(lax.ppermute(made[k], "z", to))

    def finish(self):
        if not self.links.routed:
            return self.sums
        wanted = [([(0, (n,))], f32) for n in range(len(self.routes))]
        return fold_sums(self.chain, [self.sums], wanted)


def centered(rows):
    center = rows - jnp.mean(rows, axis=-1, keepdims=True)
    scale = lax.rsqrt(jnp.mean(center * center, axis=-1, keepdims=True) + epsilon)
    return center * scale, scale


def norm_back(rows, gain, grad):
    unit, scale = centered(rows)
    inner = grad * gain
    first = jnp.mean(inner, axis=-1, keepdims=True)
    second = jnp.mean(inner * unit, axis=-1, keepdims=True)
    back = scale * (inner - first - unit * second)
    return back, jnp.sum(grad * unit, axis=0, keepdims=True), jnp.sum(grad, axis=0, keepdims=True)


def gelu_pair(u):
    root = 0.7978845608028654
    square = u * u
    t = jnp.tanh(root * u * (1.0 + 0.044715 * square))
    half = 0.5 * (1.0 + t)
    slope = half + (0.5 * root) * u * (1.0 - t * t) * (1.0 + (3 * 0.044715) * square)
    return u * half, slope


def bias_block(tiles, head, half):
    rows = []
    for key in range(SEQ // TILE):
        row = []
        for query in range(2 * half, 2 * half + 2):
            row.append(tiles[head, min(max(key - query, -2), 2) + 2])
        rows.append(jnp.concatenate(row, axis=1))
    return jnp.concatenate(rows, axis=0)


def split_heads(block, count):
    return [block[:, HEAD * n : HEAD * (n + 1)] for n in range(count)]


def attn_forward(weight, later, refs):
    n = len(weight.arrays)
    refs = list(refs)
    if later:
        h1_ref, own_ref, other_ref, prm_ref = refs[:4]
        refs = refs[4:]
    else:
        x_ref = refs.pop(0)
    pieces, refs = refs[:n], refs[n:]
    qv_ref, tiles_ref, mask_ref = refs[:3]
    refs = refs[3:]
    if later:
        h_ref, x_ref = refs[:2]
        refs = refs[2:]
    part_ref, q_ref, k_ref, v_ref, o_ref, lse_ref, w_ref, mixed_ref = refs
    rows = 2 * SEQ
    if later:
        gain, shift, bias = prm_ref[3:4], prm_ref[4:5], prm_ref[5:6]

        def norm(i, carry):
            at = pl.ds(pl.multiple_of(i * 128, 128), 128)
            value = h1_ref[at] + own_ref[at].astype(f32) + other_ref[at].astype(f32) + bias
            unit, scale = centered(value)
            result = unit * gain + shift
            h_ref[at] = result
            x_ref[at] = result.astype(bf16)
            return carry

        lax.fori_loop(0, rows // 128, norm, 0)
    weight.join(pieces, w_ref)
    heads = k_ref.shape[0]
    per = heads // 2
    part = per * HEAD
    for x in range(2):
        for stream in range(2):
            block = x_ref[stream * SEQ : (stream + 1) * SEQ]
            width = w_ref.shape[2] if stream == 0 else 256
            result = nn(block, w_ref[x, :, :width])
            query = (result[:, :part] + qv_ref[x, 0:1, :part]).astype(bf16).astype(f32) * 0.125
            for j, one in enumerate(split_heads(query.astype(bf16), per)):
                q_ref[stream * heads + x * per + j] = one
            if stream == 0:
                key = result[:, part : 2 * part].astype(bf16)
                value = (result[:, 2 * part : 3 * part] + qv_ref[x, 1:2, :part]).astype(bf16)
                for j, one in enumerate(split_heads(key, per)):
                    k_ref[x * per + j] = one
                for j, one in enumerate(split_heads(value, per)):
                    v_ref[x * per + j] = one

    def one_head(head, carry):
        key, value = k_ref[head], v_ref[head]
        for half in range(2):
            at = slice(half * 256, half * 256 + 256)
            bias = bias_block(tiles_ref, head, half)
            for stream in range(2):
                query = q_ref[stream * heads + head, at]
                score = nt(key, query) + (bias + mask_ref[stream, :, at])
                top = jnp.max(score, axis=0, keepdims=True)
                raised = jnp.exp(score - top)
                total = jnp.sum(raised, axis=0, keepdims=True)
                mixed = tn(value, raised.astype(bf16)) * (1.0 / total)
                mixed_ref[stream * heads + head, at] = mixed.T.astype(bf16)
                lse_ref[stream * heads + head, :, at] = top + jnp.log(total)
        return carry

    lax.fori_loop(0, heads, one_head, 0)
    for stream in range(2):
        total = None
        for x in range(2):
            blocks = [jnp.zeros((SEQ, HEAD), bf16)]
            blocks += [mixed_ref[stream * heads + x * per + j] for j in range(per)]
            block = jnp.concatenate(blocks, axis=1)
            o_ref[x, stream * SEQ : (stream + 1) * SEQ] = block
            term = nt(block, w_ref[x, :, 512:768])
            total = term if total is None else total + term
        part_ref[stream * SEQ : (stream + 1) * SEQ] = total.astype(bf16)


def run_attn_forward(chain, entering, weight, qv, tiles, mask, after):
    later = len(entering) == 4
    heads = tiles.shape[0]
    width = entering[0].shape[1]
    rows = entering[0].shape[0]
    columns = weight.width
    inputs = [*entering, *weight.arrays, qv, tiles, mask]
    specs = [VMEM] * len(entering) + weight.specs(False) + [VMEM] * 3
    outs = [((rows, width), f32), ((rows, width), bf16)] if later else []
    outs += [
        ((rows, width), bf16),
        ((2 * heads, SEQ, HEAD), bf16),
        ((heads, SEQ, HEAD), bf16),
        ((heads, SEQ, HEAD), bf16),
        ((2, rows, 256), bf16),
        ((2 * heads, 1, SEQ), f32),
    ]
    return chain.call(
        lambda *refs: attn_forward(weight, later, refs),
        inputs,
        specs,
        outs,
        [VMEM] * len(outs),
        flops=14 * 10**9,
        scratch=[
            pltpu.VMEM((2, width, weight.width), bf16),
            pltpu.VMEM((2 * heads, SEQ, HEAD), bf16),
        ],
        after=after,
    )


def ffn_forward(up, down, refs):
    h_ref, own_ref, other_ref, prm_ref, bias_ref = refs[:5]
    refs = refs[5:]
    up_pieces, refs = refs[: len(up.arrays)], refs[len(up.arrays) :]
    down_pieces, refs = refs[: len(down.arrays)], refs[len(down.arrays) :]
    ah_ref, h1_ref, fed_ref, act_ref, slope_ref, part_ref = refs[:6]
    up_ref, down_ref = refs[6:]

    @pl.when(pl.program_id(0) == 0)
    def _():
        up.join(up_pieces, up_ref)
        down.join(down_pieces, down_ref)

    gain, shift, bias = prm_ref[0:1], prm_ref[1:2], prm_ref[2:3]
    before = h_ref[...].astype(f32) + own_ref[...].astype(f32) + other_ref[...].astype(f32) + bias
    ah_ref[...] = before
    unit, scale = centered(before)
    normed = unit * gain + shift
    h1_ref[...] = normed
    fed = normed.astype(bf16)
    fed_ref[...] = fed

    total = None
    for x in range(2):
        inner = nn(fed, up_ref[x]) + bias_ref[x]
        act, slope = gelu_pair(inner)
        act = act.astype(bf16)
        act_ref[x] = act
        slope_ref[x] = slope.astype(bf16)
        term = nt(act, down_ref[x])
        total = term if total is None else total + term
    part_ref[...] = total.astype(bf16)


def by_rows(rows, width):
    return pl.BlockSpec((rows, width), lambda i: (i, 0))


def by_rows_pair(rows, width):
    return pl.BlockSpec((2, rows, width), lambda i: (0, i, 0))


def fixed(*shape):
    return pl.BlockSpec(shape, lambda i: (0,) * len(shape))


def run_ffn_forward(chain, entering, params, bias, up, down):
    rows, width = entering[0].shape
    step = 256
    units = up.width
    inputs = [*entering, params, bias, *up.arrays, *down.arrays]
    specs = [by_rows(step, width)] * 3 + [fixed(8, width), fixed(2, 1, units)]
    specs += up.specs(True) + down.specs(True)
    outs = [
        ((rows, width), f32),
        ((rows, width), f32),
        ((rows, width), bf16),
        ((2, rows, units), bf16),
        ((2, rows, units), bf16),
        ((rows, width), bf16),
    ]
    out_specs = [by_rows(step, width)] * 3 + [by_rows_pair(step, units)] * 2
    out_specs += [by_rows(step, width)]
    return chain.call(
        lambda *refs: ffn_forward(up, down, refs),
        inputs,
        specs,
        outs,
        out_specs,
        flops=8 * rows * width * units,
        grid=(rows // step,),
        scratch=[
            pltpu.VMEM((2, width, units), bf16),
            pltpu.VMEM((2, width, units), bf16),
        ],
    )


def ffn_backward(up, down, grads, last, refs):
    grad_refs, refs = refs[:grads], refs[grads:]
    h1_ref, own_ref, other_ref, prm_ref, slope_ref = refs[:5]
    refs = refs[5:]
    up_pieces, refs = refs[: len(up.arrays)], refs[len(up.arrays) :]
    down_pieces, refs = refs[: len(down.arrays)], refs[len(down.arrays) :]
    dz_ref, dbh_ref, du_ref, part_ref, sums_ref, up_sums_ref = refs[:6]
    refs = refs[6:]
    if last:
        out_ref, refs = refs[0], refs[1:]
    up_ref, down_ref = refs

    @pl.when(pl.program_id(0) == 0)
    def _():
        up.join(up_pieces, up_ref)
        down.join(down_pieces, down_ref)
        sums_ref[...] = jnp.zeros_like(sums_ref)
        up_sums_ref[...] = jnp.zeros_like(up_sums_ref)

    gain, shift, bias = prm_ref[3:4], prm_ref[4:5], prm_ref[5:6]
    grad = sum(ref[...].astype(f32) for ref in grad_refs)
    after = h1_ref[...] + own_ref[...].astype(f32) + other_ref[...].astype(f32) + bias
    if last:
        unit, scale = centered(after)
        out_ref[...] = (unit * gain + shift).astype(bf16)
    back, gain_sum, shift_sum = norm_back(after, gain, grad)
    dbh_ref[...] = back
    sums_ref[0:1] += gain_sum
    sums_ref[1:2] += shift_sum
    sums_ref[2:3] += jnp.sum(back, axis=0, keepdims=True)
    dz = back.astype(bf16)
    dz_ref[...] = dz

    total = None
    for x in range(2):
        du = (nn(dz, down_ref[x]) * slope_ref[x].astype(f32)).astype(bf16)
        du_ref[x] = du
        up_sums_ref[x] += jnp.sum(du.astype(f32), axis=0, keepdims=True)
        term = nt(du, up_ref[x])
        total = term if total is None else total + term
    part_ref[...] = total.astype(bf16)


def run_ffn_backward(chain, grads, entering, params, slope, up, down, last):
    rows, width = entering[0].shape
    step = 256
    units = up.width
    inputs = [*grads, *entering, params, slope, *up.arrays, *down.arrays]
    specs = [by_rows(step, width)] * (len(grads) + 3)
    specs += [fixed(8, width), by_rows_pair(step, units)]
    specs += up.specs(True) + down.specs(True)
    outs = [
        ((rows, width), bf16),
        ((rows, width), f32),
        ((2, rows, units), bf16),
        ((rows, width), bf16),
        ((8, width), f32),
        ((2, 1, units), f32),
    ]
    out_specs = [by_rows(step, width)] * 2 + [by_rows_pair(step, units), by_rows(step, width)]
    out_specs += [fixed(8, width), fixed(2, 1, units)]
    if last:
        outs.append(((rows, width), bf16))
        out_specs.append(by_rows(step, width))
    return chain.call(
        lambda *refs: ffn_backward(up, down, len(grads), last, refs),
        inputs,
        specs,
        outs,
        out_specs,
        flops=8 * rows * width * units,
        grid=(rows // step,),
        scratch=[
            pltpu.VMEM((2, width, units), bf16),
            pltpu.VMEM((2, width, units), bf16),
        ],
    )


def fold(near):
    within = lax.broadcasted_iota(jnp.int32, (8, TILE), 0)
    lane = lax.broadcasted_iota(jnp.int32, (8, TILE), 1)
    zero = jnp.zeros((8, TILE), f32)

    def aligned(rows, at):
        rows = pltpu.roll(rows, (TILE - at) % TILE, 1)
        for bit in (1, 2, 4):
            rows = jnp.where((within & bit) != 0, pltpu.roll(rows, TILE - bit, 1), rows)
        return rows

    same = after = far_before = far_after = zero
    for at in range(0, TILE, 8):
        upper = within + lane < TILE - at
        one, two, three = (aligned(near[i][at : at + 8], at) for i in (1, 2, 3))
        same += jnp.where(upper, two, one)
        after += jnp.where(upper, three, two)
        far_before += near[0][at : at + 8] + jnp.where(upper, one, zero)
        far_after += near[4][at : at + 8] + jnp.where(upper, zero, three)
    sums = [jnp.sum(v, axis=0, keepdims=True) for v in (same, after, far_before, far_after)]
    return jnp.concatenate([*sums, jnp.zeros((4, TILE), f32)])


def attn_backward(weight, refs):
    n = len(weight.arrays)
    dbh_ref, own_ref, other_ref, ah_ref, prm_ref = refs[:5]
    pieces, refs = refs[5 : 5 + n], refs[5 + n :]
    q_ref, k_ref, v_ref, lse_ref, tiles_ref, mask_ref = refs[:6]
    refs = refs[6:]
    dah_ref, dy_ref, dcat_ref, dqg_ref, part_ref, near_ref, sums_ref, col_ref = refs[:8]
    w_ref, do_ref, dq_ref, dk_ref, dv_ref = refs[8:]
    rows = 2 * SEQ
    gain = prm_ref[0:1]
    sums_ref[...] = jnp.zeros_like(sums_ref)

    def norm(i, carry):
        at = pl.ds(pl.multiple_of(i * 128, 128), 128)
        grad = dbh_ref[at] + own_ref[at].astype(f32) + other_ref[at].astype(f32)
        back, gain_sum, shift_sum = norm_back(ah_ref[at], gain, grad)
        dah_ref[at] = back
        dy_ref[at] = back.astype(bf16)
        sums_ref[0:1] += gain_sum
        sums_ref[1:2] += shift_sum
        sums_ref[2:3] += jnp.sum(back, axis=0, keepdims=True)
        return carry

    lax.fori_loop(0, rows // 128, norm, 0)
    weight.join(pieces, w_ref)
    heads = k_ref.shape[0]
    per = heads // 2
    for stream in range(2):
        at = slice(stream * SEQ, (stream + 1) * SEQ)
        for x in range(2):
            block = nn(dy_ref[at], w_ref[x, :, 512:768]).astype(bf16)
            for j in range(per):
                do_ref[stream * heads + x * per + j] = block[:, HEAD * (1 + j) : HEAD * (2 + j)]

    def one_head(head, carry):
        key, value = k_ref[head], v_ref[head]
        grad_key = jnp.zeros((SEQ, HEAD), f32)
        grad_value = jnp.zeros((SEQ, HEAD), f32)
        near = [jnp.zeros((TILE, TILE), f32) for _ in range(NEAR)]
        for half in range(2):
            at = slice(half * 256, half * 256 + 256)
            bias = bias_block(tiles_ref, head, half)
            for stream in range(2):
                spot = stream * heads + head
                query, grad_out = q_ref[spot, at], do_ref[spot, at]
                score = nt(key, query) + (bias + mask_ref[stream, :, at])
                prob = jnp.exp(score - lse_ref[spot, :, at])
                both = prob * nt(value, grad_out)
                inner = jnp.sum(both, axis=0, keepdims=True)
                grad_score = (both - prob * inner).astype(bf16)
                grad_value += nn(prob.astype(bf16), grad_out)
                grad_key += nn(grad_score, query)
                dq_ref[spot, at] = (tn(key, grad_score) * 0.125).T.astype(bf16)
                wide = grad_score.astype(f32)
                for k in range(SEQ // TILE):
                    for q in range(2):
                        which = min(max(k - (2 * half + q), -2), 2) + 2
                        near[which] += wide[
                            k * TILE : (k + 1) * TILE, q * TILE : (q + 1) * TILE
                        ]
        near_ref[head] = fold(near)
        dk_ref[head] = grad_key.astype(bf16)
        dv_ref[head] = grad_value.astype(bf16)
        return carry

    lax.fori_loop(0, heads, one_head, 0)
    total_h = total_g = None
    for x in range(2):
        near = range(x * per, (x + 1) * per)
        blocks = [dq_ref[j] for j in near] + [dk_ref[j] for j in near] + [dv_ref[j] for j in near]
        blocks += [jnp.zeros((SEQ, HEAD), bf16)] * per
        block = jnp.concatenate(blocks, axis=1)
        dcat_ref[x] = block
        term = nt(block, w_ref[x])
        total_h = term if total_h is None else total_h + term
        col_ref[x, 0:1] = jnp.sum(block.astype(f32), axis=0, keepdims=True)
        blocks = [dq_ref[heads + j] for j in near] + [jnp.zeros((SEQ, HEAD), bf16)]
        block = jnp.concatenate(blocks, axis=1)
        dqg_ref[x] = block
        term = nt(block, w_ref[x, :, :256])
        total_g = term if total_g is None else total_g + term
        col_ref[x, 1:2, :256] = jnp.sum(block.astype(f32), axis=0, keepdims=True)
    part_ref[:SEQ] = total_h.astype(bf16)
    part_ref[SEQ:] = total_g.astype(bf16)


def run_attn_backward(chain, entering, params, weight, saved, tiles, mask):
    rows, width = entering[0].shape
    heads = tiles.shape[0]
    columns = weight.width
    q, k, v, _, lse = saved
    inputs = [*entering, params, *weight.arrays, q, k, v, lse, tiles, mask]
    specs = [VMEM] * 5 + weight.specs(False) + [VMEM] * 6
    outs = [
        ((rows, width), f32),
        ((rows, width), bf16),
        ((2, SEQ, columns), bf16),
        ((2, SEQ, 256), bf16),
        ((rows, width), bf16),
        ((heads, 8, TILE), f32),
        ((8, width), f32),
        ((2, 8, columns), f32),
    ]
    return chain.call(
        lambda *refs: attn_backward(weight, refs),
        inputs,
        specs,
        outs,
        [VMEM] * len(outs),
        flops=20 * 10**9,
        scratch=[
            pltpu.VMEM((2, width, weight.width), bf16),
            pltpu.VMEM((2 * heads, SEQ, HEAD), bf16),
            pltpu.VMEM((2 * heads, SEQ, HEAD), bf16),
            pltpu.VMEM((heads, SEQ, HEAD), bf16),
            pltpu.VMEM((heads, SEQ, HEAD), bf16),
        ],
    )


def quarters(part, first):
    return [(part, x) for x in range(2)] if first == "y" else [(y, part) for y in range(2)]


def ffn_grads(chain, fed, du, dz, act, part, up_first, down_first):
    rows, width = fed.shape
    units = du.shape[2]
    half = width // 2

    def body(fed_ref, du_ref, dz_ref, act_ref, up_ref, down_ref):
        for left, right, out, first in (
            (fed_ref, du_ref, up_ref, up_first),
            (dz_ref, act_ref, down_ref, down_first),
        ):
            for n, (y, x) in enumerate(quarters(part, first)):
                out[n] = tn(left[:, y * half : (y + 1) * half], right[x]).astype(bf16)

    return chain.call(
        body,
        [fed, du, dz, act],
        [VMEM] * 4,
        [((2, half, units), bf16)] * 2,
        [VMEM] * 2,
        flops=8 * rows * half * units,
    )


def attn_grads(chain, x, dcat, dqg, dy, o, part, firsts):
    rows, width = x.shape
    half = width // 2
    columns = dcat.shape[2]
    span = columns // len(firsts)

    def body(x_ref, dcat_ref, dqg_ref, dy_ref, o_ref, *outs):
        for y in range(2):
            at = slice(y * half, (y + 1) * half)
            for n, first in enumerate(firsts):
                for place, (want, other) in enumerate(quarters(part, first)):
                    if want != y:
                        continue
                    low, high = n * span, (n + 1) * span
                    total = tn(x_ref[:SEQ, at], dcat_ref[other, :, low:high])
                    outs[n][place] = total.astype(bf16)
                    if n == 0:
                        query = total[:, :256] + tn(x_ref[SEQ:, at], dqg_ref[other])
                        outs[n][place, :, :256] = query.astype(bf16)
                    if n == len(firsts) - 1:
                        out = total[:, span - 256 :] + tn(dy_ref[:, at], o_ref[other])
                        outs[n][place, :, span - 256 :] = out.astype(bf16)

    return chain.call(
        body,
        [x, dcat, dqg, dy, o],
        [VMEM] * 5,
        [((2, half, span), bf16)] * len(firsts),
        [VMEM] * len(firsts),
        flops=6 * rows * half * columns,
    )


def local(links, *arguments):
    (
        h_in,
        g_in,
        lengths,
        order,
        predicted,
        w_query,
        w_key,
        w_value,
        w_out,
        w_up,
        w_down,
        q_bias,
        v_bias,
        up_bias,
        rel_table,
        norm_gain,
        norm_shift,
        out_bias,
        h_cot,
        g_cot,
    ) = arguments
    rows_own, model = h_in.shape
    part = w_query.shape[2]
    units = w_up.shape[2]
    heads = 2 * rel_table.shape[1]
    table_size = rel_table.shape[1] * BUCKETS
    slot = lax.axis_index("x")
    core = lax.axis_index("core")

    chain = Chain()
    gathered = []
    for layer in range(LAYERS):
        attn = jnp.concatenate(
            [w_query[layer], w_key[layer], w_value[layer], w_out[layer].T], axis=1
        )
        blocks = (attn, w_up[layer], w_down[layer].T)
        gathered.append([links.gather(b, r) for b, r in zip(blocks, GATHER[layer])])

    def pick(v):
        return lax.dynamic_index_in_dim(v, slot, 0, keepdims=False)

    mask = slot_masks(pick(lengths), pick(order), pick(predicted))
    onehot = (
        jnp.arange(BUCKETS, dtype=jnp.int32)[:, None] == tile_buckets().reshape(1, -1)
    ).astype(f32)

    lanes = jnp.arange(TILE, dtype=jnp.int32)
    edge = jnp.full_like(lanes, TILE)
    fold_buckets = bucket_of(jnp.concatenate([-lanes, TILE - lanes, -edge, edge]))
    fold_hot = (fold_buckets[:, None] == jnp.arange(BUCKETS, dtype=jnp.int32)[None, :]).astype(f32)

    small = links.pair(
        jnp.concatenate(
            [q_bias, v_bias, up_bias, rel_table.reshape(LAYERS, table_size)], axis=1
        )
    )
    tables = small[:, :, 2 * part + units :].transpose(1, 0, 2).reshape(LAYERS * heads, BUCKETS)
    tiles = jnp.dot(tables, onehot, precision=highest).reshape(LAYERS, heads, NEAR, TILE, TILE)
    qv = jnp.stack([small[:, :, :part], small[:, :, part : 2 * part]], axis=2)
    qv = jnp.pad(qv, ((0, 0), (0, 0), (0, 6), (0, 256 - part)))
    bias_up = small[:, :, None, 2 * part : 2 * part + units]

    features = links.feature_order(model)
    swapper = (jnp.arange(model, dtype=jnp.int32)[:, None] == features[None, :]).astype(bf16)
    swapper32 = swapper.astype(f32)
    params = jnp.dot(
        jnp.stack([norm_gain, norm_shift, out_bias], axis=2).reshape(-1, model),
        swapper32,
        precision=highest,
    ).reshape(LAYERS, 6, model)
    params = jnp.pad(params, ((0, 0), (0, 2), (0, 0)))

    def ordered(first, second):
        rows = links.both_rows(jnp.concatenate([first, second], axis=1))
        both = jnp.concatenate([rows[:, :model], rows[:, model:]], axis=0)
        return nn(both, swapper).astype(bf16)

    entering = ordered(h_in, g_in)
    kept = []
    for layer in range(LAYERS):
        attn, up, down = gathered[layer]
        if layer == 0:
            x = stream = entering
            before = (entering,)
            after = []
            if links.routed:
                after = [v for w in (up, down, *gathered[1]) for v in w.arrays]
        else:
            before = (h1, part_own, part_other, params[layer - 1])
            after = []
        made = run_attn_forward(chain, before, attn, qv[:, layer], tiles[layer], mask, after)
        if layer > 0:
            stream, x = made[:2]
            made = made[2:]
        mixed_own, q, k, v, o, lse = made
        ah, h1, fed, act, slope, part_own = run_ffn_forward(
            chain, (stream, mixed_own, links.pc(mixed_own)), params[layer], bias_up[:, layer], up, down
        )
        part_other = links.pc(part_own)
        kept.append((x, (q, k, v, o, lse), ah, (h1, part_own, part_other), fed, act, slope))
    grads = (ordered(h_cot, g_cot),)
    owned = [None] * LAYERS
    splits = [None] * LAYERS
    wholes = [None] * LAYERS
    for layer in range(LAYERS - 1, -1, -1):
        attn, up, down = gathered[layer]
        firsts = [r[0] for r in SCATTER]
        x, saved, ah, second, fed, act, slope = kept[layer]
        last = layer == LAYERS - 1
        made = run_ffn_backward(chain, grads, second, params[layer], slope, up, down, last)
        dz, dbh, du, part_own, sums_two, up_sums = made[:6]
        if last:
            result = made[6]
        part_other = links.pc(part_own)
        if not last:
            ffn_way.third()
            attn_way.second()
        sent = ffn_grads(chain, fed, du, dz, act, 1, *firsts)
        held = ffn_grads(chain, fed, du, dz, act, 0, *firsts)
        if not last:
            attn_way.third()
            done_ffn = ffn_way.finish()
            old_attn = attn_way
        ffn_way = Scatter(chain, links, list(zip(held, sent, SCATTER)))
        dah, dy, dcat, dqg, part_own, near, sums_one, cols = run_attn_backward(
            chain, (dbh, part_own, part_other, ah), params[layer], attn, saved, tiles[layer], mask
        )
        part_other = links.pc(part_own)
        ffn_way.second()
        sent = attn_grads(chain, x, dcat, dqg, dy, saved[3], 1, firsts)
        held = attn_grads(chain, x, dcat, dqg, dy, saved[3], 0, firsts)
        attn_way = Scatter(chain, links, list(zip(held, sent, SCATTER)))
        if not last:
            owned[layer + 1] = (old_attn.finish(), done_ffn)
            ffn_way.third()
            attn_way.second()
            attn_way.third()
            owned[layer] = (attn_way.finish(), ffn_way.finish())
        grads = (dah, part_own, part_other)
        table = jnp.dot(near[:, :4].reshape(heads, -1), fold_hot, precision=highest)
        splits[layer] = jnp.concatenate(
            [
                cols[:, 0, :part] + cols[:, 1, :part],
                cols[:, 0, 2 * part : 3 * part],
                up_sums[:, 0],
                table.reshape(2, table_size),
            ],
            axis=1,
        )
        wholes[layer] = jnp.stack(
            [sums_one[0], sums_two[0], sums_one[1], sums_two[1], sums_one[2], sums_two[2]]
        )
    whole = jnp.dot(jnp.concatenate(wholes), swapper32.T, precision=highest)
    split_sum, whole_sum = links.total(jnp.concatenate(splits, axis=1), whole.reshape(-1))
    split_sum = split_sum.reshape(LAYERS, -1)
    whole_sum = whole_sum.reshape(LAYERS, 3, 2, model)

    def returned(parts):
        mine = []
        for stream in range(2):
            at = stream * SEQ + core * rows_own
            rows = [lax.dynamic_slice_in_dim(p, at, rows_own, 0) for p in parts]
            mine.append(sum(r.astype(f32) for r in rows).astype(bf16))
        back = nt(jnp.concatenate(mine), swapper).astype(bf16)
        return back[:rows_own], back[rows_own:]

    h_out, g_out = returned((result,))
    h_grad, g_grad = returned(grads)
    attn_sum = jnp.stack([jnp.concatenate(owned[layer][0], axis=1) for layer in range(LAYERS)])
    up_sum = jnp.stack([owned[layer][1][0] for layer in range(LAYERS)])
    down_sum = jnp.stack([owned[layer][1][1] for layer in range(LAYERS)])
    return (
        h_out,
        g_out,
        h_grad,
        g_grad,
        attn_sum[:, :, :part],
        attn_sum[:, :, part : 2 * part],
        attn_sum[:, :, 2 * part : 3 * part],
        attn_sum[:, :, 3 * part :].transpose(0, 2, 1),
        up_sum,
        down_sum.transpose(0, 2, 1),
        split_sum[:, :part],
        split_sum[:, part : 2 * part],
        split_sum[:, 2 * part : 2 * part + units],
        split_sum[:, 2 * part + units :].reshape(LAYERS, -1, BUCKETS),
        whole_sum[:, 0],
        whole_sum[:, 1],
        whole_sum[:, 2],
    )


def solution(mesh):
    links = Links(mesh)
    rows = P(("z", "y", "x", "core"), None)
    by_dp = P(("z", "y"), None)
    wide = P(None, ("z", "y"), ("x", "core"))
    tall = P(None, ("x", "core"), ("z", "y"))
    by_tensor = P(None, ("x", "core"))
    table = P(None, ("x", "core"), None)
    weights = (wide, wide, wide, tall, wide, tall)
    owned = (by_tensor, by_tensor, by_tensor, table, P(), P(), P())
    return jax.shard_map(
        functools.partial(local, links),
        mesh=links.mesh,
        in_specs=(rows, rows, by_dp, by_dp, by_dp) + weights + owned + (rows, rows),
        out_specs=(rows, rows, rows, rows) + weights + owned,
        check_vma=False,
    )
```

time: 875 us -> 530 us (0.61)
  matrix products: 253 us -> 18.2 us
  Pallas kernels: 0 us -> 200 us
  local copies, waits for them, and re-layouts: 214 us -> 51.2 us
  other arithmetic: 114 us -> 24.5 us
  waiting for transfers between devices: 201 us -> 129 us
  starting transfers between devices: 76.4 us -> 94.5 us
    pallas_call x0 -> x28, Pallas kernels: none -> 200 us  [call(): pl.pallas_call(rest, out_shape=[jax.ShapeDtypeStruct(*o) for o in outs],...]
    dot_general x68 -> x4, matrix products: 133 us -> 8.93 us  [dot(): lax.dot_general(left, right, (numbers, ((), ())), preferred_element_type=...]
    dot_general x29 -> x4, matrix products: 119 us -> 6.83 us  [the longest x1 4.74 us: local(): jnp.dot(tables, onehot, precision=highest)]
    ppermute x36 -> x18, waiting for transfers between devices: 115 us -> 51.3 us  [pz(): return lax.ppermute(v, 'z', self.ring)]
    unnamed x609 -> x412, local copies, waits for them, and re-layouts: 78.8 us -> 27.9 us
    concatenate x20 -> x2, local copies, waits for them, and re-layouts: 44.9 us -> 1.64 us  [ordered(): rows = links.both_rows(jnp.concatenate([first, second], axis=1))]
    ppermute x51 -> x67, starting transfers between devices: 49 us -> 80.8 us  [the longest x55 61.8 us: swap(): return lax.ppermute(v, axis, SWAP)]
    reduce_sum x22 -> x0, other arithmetic: 30.8 us -> none  [the longest x8 15.7 us: norm_rows(): center = rows - jnp.mean(rows, axis=-1, keepdims=True)]
  transfers between devices with their start and end apart: 107 -> 97, of which waited for: 41 -> 39; matrix products, arithmetic and copies ran while one was open for 60% -> 13% of each run, Pallas kernels for 0% -> 23%
where the time goes in v2:
time: 530 us; the launch traced here: 523 us
  Pallas kernels  200 us (38%)
  waiting for transfers between devices  129 us (24%)
  starting transfers between devices  94.5 us (18%)
  local copies, waits for them, and re-layouts  51.2 us (10%)
  other arithmetic  24.5 us (5%)
  matrix products  18.2 us (3%)
    pallas_call x28, Pallas kernels, call(): pl.pallas_call(rest, out_shape=[jax.ShapeDtypeStruct(*o) for o in outs],...  200 us
    ppermute x55, starting transfers between devices, swap(): return lax.ppermute(v, axis, SWAP)  61.8 us
    ppermute x18, waiting for transfers between devices, pz(): return lax.ppermute(v, 'z', self.ring)  51.3 us
    ppermute x55, waiting for transfers between devices, swap(): return lax.ppermute(v, axis, SWAP)  38.9 us
    ppermute x12, waiting for transfers between devices, third(): self.sums.append(lax.ppermute(made[k], 'z', to))  31.2 us
    unnamed x412, local copies, waits for them, and re-layouts  27.9 us
    ppermute x12, starting transfers between devices, third(): self.sums.append(lax.ppermute(made[k], 'z', to))  19 us
    ppermute x18, starting transfers between devices, pz(): return lax.ppermute(v, 'z', self.ring)  12.4 us
  transfers between devices with their start and end apart: 97, of which 39 were waited for; matrix products, arithmetic and copies ran while one was open for 13% of the time, Pallas kernels for 23%

profile of v2, /device:TPU:0, one launch (start us, length us, event | category | flops | bytes accessed | tf_op | source)
XLA Modules:
  0.0 522.7 jit_solution(5215263648692964926)
XLA Ops:
  3.6 3.1 collective-permute-start.31
  48.0 3.1 collective-permute-done.7
  58.0 4.8 collective-permute-done.15.refs_13_.refs_6_.refs_9_
  62.8 6.3 %collective-permute-done.23.refs_21_.refs_14_.refs_17_ = bf16[2,96,768]{2,1,0:T(8,128)(2,1)S(1)} collective-permute-done((bf16[2,96,768]{2,1,0:T(8,128)(2,1)S(1)}, bf16[2,96,768]{2,1,0:T(8,128)(2,1)S(1)}, u32[]{:S(2)}, u32[]{:S(2)}) %collective-permute-start.23) | collective-permute-done | bytes 294944 | tf_op jit(solution)/shard_map/ppermute | solution.py:100
  69.1 3.3 collective-permute-done.42.refs_37_.refs_6_.refs_7_
  88.4 2.7 collective-permute-done.38.refs_33_.refs_9_.refs_10_
  91.6 2.6 collective-permute-done.39.refs_34_.refs_10_.refs_11_
  95.2 4.7 fusion
  99.9 6.2 %collective-permute-done.24.refs_22_.refs_15_.refs_18_ = bf16[2,96,768]{2,1,0:T(8,128)(2,1)S(1)} collective-permute-done((bf16[2,96,768]{2,1,0:T(8,128)(2,1)}, bf16[2,96,768]{2,1,0:T(8,128)(2,1)S(1)}, u32[]{:S(2)}, u32[]{:S(2)}) %collective-permute-start.24) | collective-permute-done | bytes 294944 | tf_op jit(solution)/shard_map/ppermute | solution.py:100
  106.2 6.0 %collective-permute-done.43.refs_38_.refs_7_.refs_8_ = bf16[2,96,768]{2,1,0:T(8,128)(2,1)S(1)} collective-permute-done((bf16[2,96,768]{2,1,0:T(8,128)(2,1)}, bf16[2,96,768]{2,1,0:T(8,128)(2,1)S(1)}, u32[]{:S(2)}, u32[]{:S(2)}) %collective-permute-start.43) | collective-permute-done | bytes 294944 | tf_op jit(solution)/shard_map/ppermute | solution.py:100
  124.1 2.9 collective-permute-done.54.refs_49_.refs_18_.refs_19_
  133.5 5.5 %collective-permute-done.17.refs_15_.refs_8_.refs_11_ = bf16[2,96,768]{2,1,0:T(8,128)(2,1)S(1)} collective-permute-done((bf16[2,96,768]{2,1,0:T(8,128)(2,1)}, bf16[2,96,768]{2,1,0:T(8,128)(2,1)S(1)}, u32[]{:S(2)}, u32[]{:S(2)}) %collective-permute-start.17) | collective-permute-done | bytes 294944 | tf_op jit(solution)/shard_map/ppermute | solution.py:100
  139.9 5.4 %collective-permute-done.25.refs_23_.refs_16_.refs_19_ = bf16[2,96,768]{2,1,0:T(8,128)(2,1)S(1)} collective-permute-done((bf16[2,96,768]{2,1,0:T(8,128)(2,1)S(1)}, bf16[2,96,768]{2,1,0:T(8,128)(2,1)S(1)}, u32[]{:S(2)}, u32[]{:S(2)}) %collective-permute-start.25) | collective-permute-done | bytes 294944 | tf_op jit(solution)/shard_map/ppermute | solution.py:100
  145.3 2.9 broadcast_select_fusion.1
  157.9 2.7 fusion.11.refs_0_
  161.1 3.2 collective-permute-done.29.refs_27_.refs_20_.refs_23_
  164.3 3.2 collective-permute-done.56.refs_51_.refs_20_.refs_21_
  168.3 19.0 %shard_map.323 = (bf16[1024,768]{1,0:T(8,128)(2,1)}, bf16[12,512,64]{2,1,0:T(8,128)(2,1)}, bf16[6,512,64]{2,1,0:T(8,128)(2,1)}, bf16[6,512,64]{2,1,0:T(8,128)(2,...) custom-call(bf16[1024,768]{1,0:T(8,128)(2,1)} %fusion.11.refs_0_, ...), custom_call_target="tpu_custom_call" | custom-call | flops 56000000000 | tf_op jit(solution)/shard_map/pallas_call | solution.py:185
  188.3 2.6 collective-permute-done.57.refs_2_
  193.0 12.8 %shard_map.324 = (f32[1024,768]{1,0:T(8,128)}, f32[1024,768]{1,0:T(8,128)}, bf16[1024,768]{1,0:T(8,128)(2,1)}, bf16[2,1024,768]{2,1,0:T(8,128)(2,1)}, bf16[2,102...) custom-call(bf16[1024,768]{1,0:T(8,128)(2,1)} %fusion.11.refs_0_, bf16[1024,768]{1,0:T(8,128)(2,1)} %get-tuple-element.128.refs_1_, ...), custom_call_target="tpu_custom_call" | custom-call | flops 19327352832 | tf_op jit(solution)/shard_map/pallas_call | solution.py:185
  210.9 22.7 %shard_map.325 = (f32[1024,768]{1,0:T(8,128)}, bf16[1024,768]{1,0:T(8,128)(2,1)}, bf16[1024,768]{1,0:T(8,128)(2,1)}, bf16[12,512,64]{2,1,0:T(8,128)(2,1)}, bf16[...) custom-call(f32[1024,768]{1,0:T(8,128)} %get-tuple-element.130.refs_, ...), custom_call_target="tpu_custom_call" | custom-call | flops 56000000000 | tf_op jit(solution)/shard_map/pallas_call | solution.py:185
  234.7 3.5 collective-permute-done.59.refs_2_
  239.4 13.1 %shard_map.326 = (f32[1024,768]{1,0:T(8,128)}, f32[1024,768]{1,0:T(8,128)}, bf16[1024,768]{1,0:T(8,128)(2,1)}, bf16[2,1024,768]{2,1,0:T(8,128)(2,1)}, bf16[2,102...) custom-call(f32[1024,768]{1,0:T(8,128)} %get-tuple-element.133.refs_0_, bf16[1024,768]{1,0:T(8,128)(2,1)} %get-tuple-element.134.refs_1_, ...), custom_call_target="tpu_custom_call" | custom-call | flops 19327352832 | tf_op jit(solution)/shard_map/pallas_call | solution.py:185
  254.4 2.6 fusion.10.refs_0_
  257.1 13.2 %shard_map.327 = (bf16[1024,768]{1,0:T(8,128)(2,1)}, f32[1024,768]{1,0:T(8,128)}, bf16[2,1024,768]{2,1,0:T(8,128)(2,1)}, bf16[1024,768]{1,0:T(8,128)(2,1)}, f32[...) custom-call(bf16[1024,768]{1,0:T(8,128)(2,1)} %fusion.10.refs_0_, ...), custom_call_target="tpu_custom_call" | custom-call | flops 19327352832 | tf_op jit(solution)/shard_map/pallas_call | solution.py:185
  272.1 5.6 %shard_map.328 = (bf16[2,384,768]{2,1,0:T(8,128)(2,1)S(1)}, bf16[2,384,768]{2,1,0:T(8,128)(2,1)S(1)}) custom-call(bf16[1024,768]{1,0:T(8,128)(2,1)S(1)} %copy-done.125, bf16[2,1024,768]{2,1,0:T(8,128)(2,1)} %get-tuple-element.147.refs_1_, bf16[1024,768]{1,0:T(8,128)(2,1)S(1)} %copy-done.126, bf16[2,1024,768]{2,1,0:T(8,128)(2,1)} %get-tuple-element.149.refs_3_, ...), custom_call_target="tpu_custom_call" | custom-call | flops 9663676416 | tf_op jit(solution)/shard_map/pallas_call | solution.py:185
  282.7 6.1 %shard_map.329 = (bf16[2,384,768]{2,1,0:T(8,128)(2,1)S(1)}, bf16[2,384,768]{2,1,0:T(8,128)(2,1)S(1)}) custom-call(bf16[1024,768]{1,0:T(8,128)(2,1)S(1)} %copy-done.125, bf16[2,1024,768]{2,1,0:T(8,128)(2,1)} %get-tuple-element.147.refs_1_, bf16[1024,768]{1,0:T(8,128)(2,1)} %get-tuple-element.148.refs_2_, bf16[2,1024,768]{2,1,0:T(8,128)(2,1)} %get-tuple-element.149.refs_3_, ...), custom_call_target="tpu_custom_call" | custom-call | flops 9663676416 | tf_op jit(solution)/shard_map/pallas_call | solution.py:185
  291.0 27.8 %shard_map.330 = (f32[1024,768]{1,0:T(8,128)}, bf16[1024,768]{1,0:T(8,128)(2,1)}, bf16[2,512,768]{2,1,0:T(8,128)(2,1)}, bf16[2,512,256]{2,1,0:T(8,128)(2,1)S(1)}...) custom-call(f32[1024,768]{1,0:T(8,128)} %get-tuple-element.141.refs_0_,, ...), custom_call_target="tpu_custom_call" | custom-call | flops 80000000000 | tf_op jit(solution)/shard_map/pallas_call | solution.py:185
  320.0 3.0 shard_map.331
  324.3 4.4 shard_map.332
  338.5 3.7 shard_map.333
  342.4 13.3 %shard_map.334 = (bf16[1024,768]{1,0:T(8,128)(2,1)}, f32[1024,768]{1,0:T(8,128)}, bf16[2,1024,768]{2,1,0:T(8,128)(2,1)}, bf16[1024,768]{1,0:T(8,128)(2,1)}, f32[...) custom-call(f32[1024,768]{1,0:T(8,128)} %get-tuple-element.153.refs_0_, bf16[1024,768]{1,0:T(8,128)(2,1)} %get-tuple-element.154.refs_1_, ...), custom_call_target="tpu_custom_call" | custom-call | flops 19327352832 | tf_op jit(solution)/shard_map/pallas_call | solution.py:185
  359.7 6.5 %shard_map.337 = (bf16[2,384,768]{2,1,0:T(8,128)(2,1)}, bf16[2,384,768]{2,1,0:T(8,128)(2,1)}) custom-call(bf16[1024,768]{1,0:T(8,128)(2,1)S(1)} %copy-done.123, bf16[2,1024,768]{2,1,0:T(8,128)(2,1)} %get-tuple-element.187.refs_1_, bf16[1024,768]{1,0:T(8,128)(2,1)S(1)} %copy-done.124, bf16[2,1024,768]{2,1,0:T(8,128)(2,1)} %get-tuple-element.189.refs_3_, ...), custom_call_target="tpu_custom_call" | custom-call | flops 9663676416 | tf_op jit(solution)/shard_map/pallas_call | solution.py:185
  368.0 5.9 %shard_map.338 = (bf16[2,384,768]{2,1,0:T(8,128)(2,1)S(1)}, bf16[2,384,768]{2,1,0:T(8,128)(2,1)S(1)}) custom-call(bf16[1024,768]{1,0:T(8,128)(2,1)S(1)} %copy-done.123, bf16[2,1024,768]{2,1,0:T(8,128)(2,1)} %get-tuple-element.187.refs_1_, bf16[1024,768]{1,0:T(8,128)(2,1)} %get-tuple-element.188.refs_2_, bf16[2,1024,768]{2,1,0:T(8,128)(2,1)} %get-tuple-element.189.refs_3_, ...), custom_call_target="tpu_custom_call" | custom-call | flops 9663676416 | tf_op jit(solution)/shard_map/pallas_call | solution.py:185
  378.8 5.5 %collective-permute-done.69.refs_2_ = bf16[2,96,768]{2,1,0:T(8,128)(2,1)S(1)} collective-permute-done((bf16[2,96,768]{2,1,0:T(8,128)(2,1)S(1)}, bf16[2,96,768]{2,1,0:T(8,128)(2,1)S(1)}, u32[]{:S(2)}, u32[]{:S(2)}) %collective-permute-start.69) | collective-permute-done | bytes 294944 | tf_op jit(solution)/shard_map/ppermute | solution.py:279
  384.6 28.1 %shard_map.341 = (f32[1024,768]{1,0:T(8,128)}, bf16[1024,768]{1,0:T(8,128)(2,1)}, bf16[2,512,768]{2,1,0:T(8,128)(2,1)}, bf16[2,512,256]{2,1,0:T(8,128)(2,1)S(1)}...) custom-call(f32[1024,768]{1,0:T(8,128)} %get-tuple-element.167.refs_0_,, ...), custom_call_target="tpu_custom_call" | custom-call | flops 80000000000 | tf_op jit(solution)/shard_map/pallas_call | solution.py:185
  415.0 2.5 fusion.2
  423.1 2.8 fusion.20
  438.8 3.7 shard_map.343
  443.2 3.1 collective-permute-done.83.refs_2_
  447.5 3.5 shard_map.344
  451.1 2.8 collective-permute-done.80.refs_1_
  454.7 4.1 collective-permute-done.81.refs_3_
  459.8 8.9 %collective-permute-done.78.refs_1_ = bf16[2,384,384]{2,1,0:T(8,128)(2,1)S(1)} collective-permute-done((bf16[2,384,384]{2,1,0:T(8,128)(2,1)S(1)}, bf16[2,384,384]{2,1,0:T(8,128)(2,1)S(1)}, u32[]{:S(2)}, u32[]{:S(2)}) %collective-permute-start.78) | collective-permute-done | bytes 589856 | tf_op jit(solution)/shard_map/ppermute | solution.py:97
  486.9 7.9 %collective-permute-done.88.refs_2_ = bf16[2,96,384]{2,1,0:T(8,128)(2,1)S(1)} collective-permute-done((bf16[2,96,384]{2,1,0:T(8,128)(2,1)S(1)}, bf16[2,96,384]{2,1,0:T(8,128)(2,1)S(1)}, u32[]{:S(2)}, u32[]{:S(2)}) %collective-permute-start.88) | collective-permute-done | bytes 147488 | tf_op jit(solution)/shard_map/ppermute | solution.py:279
  494.7 4.9 collective-permute-start.89
  501.6 6.2 %collective-permute-done.89.refs_3_ = bf16[2,96,384]{2,1,0:T(8,128)(2,1)S(1)} collective-permute-done((bf16[2,96,384]{2,1,0:T(8,128)(2,1)}, bf16[2,96,384]{2,1,0:T(8,128)(2,1)S(1)}, u32[]{:S(2)}, u32[]{:S(2)}) %collective-permute-start.89) | collective-permute-done | bytes 147488 | tf_op jit(solution)/shard_map/ppermute | solution.py:279
  509.6 7.2 %collective-permute-done.91.refs_2_ = bf16[2,96,768]{2,1,0:T(8,128)(2,1)S(1)} collective-permute-done((bf16[2,96,768]{2,1,0:T(8,128)(2,1)}, bf16[2,96,768]{2,1,0:T(8,128)(2,1)S(1)}, u32[]{:S(2)}, u32[]{:S(2)}) %collective-permute-start.91) | collective-permute-done | bytes 294944 | tf_op jit(solution)/shard_map/ppermute | solution.py:279
  (692 shorter events, 191.8 us)
Async XLA Ops:
  3.6 24.0 %collective-permute-start.31 = (bf16[96,768]{1,0:T(8,128)(2,1)S(1)}, bf16[96,768]{1,0:T(8,128)(2,1)S(1)}, u32[]{:S(2)}, u32[]{:S(2)}) collective-permute-start(bf16[96,768]{1,0:T(8,128)(2,1)S(1)} %pad_maximum_fusion.17), channel_id=1, source_target_pairs={{0,8},{8,16},{16,24},{24,0},{1,9},{9,17},{17,25},{25,1},{2,10},{10... | collective-permute-start | bytes 442376 | tf_op jit(solution)/shard_map/ppermute | solution.py:100
  6.7 22.0 %collective-permute-start.30 = (bf16[96,768]{1,0:T(8,128)(2,1)S(1)}, bf16[96,768]{1,0:T(8,128)(2,1)S(1)}, u32[]{:S(2)}, u32[]{:S(2)}) collective-permute-start(bf16[96,768]{1,0:T(8,128)(2,1)S(1)} %pad_maximum_fusion.17), channel_id=1, source_target_pairs={{0,4},{4,0},{1,5},{5,1},{2,6},{6,2},{3,7},{7,3},{8,12},{12,8},{9,1... | collective-permute-start | bytes 442376 | tf_op jit(solution)/shard_map/ppermute | solution.py:97
  9.1 19.1 %collective-permute-start.3 = (bf16[96,768]{1,0:T(8,128)(2,1)}, bf16[96,768]{1,0:T(8,128)(2,1)S(1)}, u32[]{:S(2)}, u32[]{:S(2)}) collective-permute-start(bf16[96,768]{1,0:T(8,128)(2,1)} %pad_maximum_fusion.16), channel_id=1, source_target_pairs={{0,8},{8,16},{16,24},{24,0},{1,9},{9,17},{17,25},{25,1},{2,10},{10... | collective-permute-start | bytes 442376 | tf_op jit(solution)/shard_map/ppermute | solution.py:100
  10.7 19.8 %collective-permute-start.2 = (bf16[96,768]{1,0:T(8,128)(2,1)}, bf16[96,768]{1,0:T(8,128)(2,1)S(1)}, u32[]{:S(2)}, u32[]{:S(2)}) collective-permute-start(bf16[96,768]{1,0:T(8,128)(2,1)} %pad_maximum_fusion.16), channel_id=1, source_target_pairs={{0,2},{2,0},{1,3},{3,1},{4,6},{6,4},{5,7},{7,5},{8,10},{10,8},{9,1... | collective-permute-start | bytes 442376 | tf_op jit(solution)/shard_map/ppermute | solution.py:97
  12.3 13.7 %collective-permute-start.13 = (f32[2,1248]{1,0:T(2,128)S(1)}, f32[2,1248]{1,0:T(2,128)S(1)}, u32[]{:S(2)}, u32[]{:S(2)}) collective-permute-start(f32[2,1248]{1,0:T(2,128)S(1)} %concatenate.68), channel_id=1, source_target_pairs={{0,2},{2,0},{1,3},{3,1},{4,6},{6,4},{5,7},{7,5},{8,10},{10,8},{9,1... | collective-permute-start | bytes 29960 | tf_op jit(solution)/shard_map/ppermute | solution.py:97
  37.0 15.8 %collective-permute-start.37 = (bf16[2,96,768]{2,1,0:T(8,128)(2,1)S(1)}, bf16[2,96,768]{2,1,0:T(8,128)(2,1)}, u32[]{:S(2)}, u32[]{:S(2)}) collective-permute-start(bf16[2,96,768]{2,1,0:T(8,128)(2,1)S(1)} %pad_maximum_fusion.9.refs_28_.refs_4_.refs_5_), channel_id=1, source_target_pairs={{0,2},{2,0},{1,3},{3,1},{4,6},{6,4},{5,7},{7,5},{8,10},{10,8},{9,1... | collective-permute-start | bytes 884744 | tf_op jit(solution)/shard_map/ppermute | solution.py:97
  51.1 18.0 %collective-permute-start.23 = (bf16[2,96,768]{2,1,0:T(8,128)(2,1)S(1)}, bf16[2,96,768]{2,1,0:T(8,128)(2,1)S(1)}, u32[]{:S(2)}, u32[]{:S(2)}) collective-permute-start(bf16[2,96,768]{2,1,0:T(8,128)(2,1)S(1)} %pad_maximum_fusion.8.refs_20_.refs_13_.refs_16_), channel_id=1, source_target_pairs={{0,8},{8,16},{16,24},{24,0},{1,9},{9,17},{17,25},{25,1},{2,10},{10... | collective-permute-start | bytes 884744 | tf_op jit(solution)/shard_map/ppermute | solution.py:100
  51.8 20.7 %collective-permute-start.42 = (bf16[2,96,768]{2,1,0:T(8,128)(2,1)S(1)}, bf16[2,96,768]{2,1,0:T(8,128)(2,1)S(1)}, u32[]{:S(2)}, u32[]{:S(2)}) collective-permute-start(bf16[2,96,768]{2,1,0:T(8,128)(2,1)S(1)} %pad_maximum_fusion.13.refs_36_.refs_5_.refs_6_), channel_id=1, source_target_pairs={{0,8},{8,16},{16,24},{24,0},{1,9},{9,17},{17,25},{25,1},{2,10},{10... | collective-permute-start | bytes 884744 | tf_op jit(solution)/shard_map/ppermute | solution.py:100
  52.8 24.1 %collective-permute-start.18 = (bf16[2,96,768]{2,1,0:T(8,128)(2,1)S(1)}, bf16[2,96,768]{2,1,0:T(8,128)(2,1)S(1)}, u32[]{:S(2)}, u32[]{:S(2)}) collective-permute-start(bf16[2,96,768]{2,1,0:T(8,128)(2,1)S(1)} %pad_maximum_fusion.7.refs_12_.refs_5_.refs_8_), channel_id=1, source_target_pairs={{0,4},{4,0},{1,5},{5,1},{2,6},{6,2},{3,7},{7,3},{8,12},{12,8},{9,1... | collective-permute-start | bytes 884744 | tf_op jit(solution)/shard_map/ppermute | solution.py:97
  54.3 21.4 %collective-permute-start.50 = (bf16[2,96,768]{2,1,0:T(8,128)(2,1)S(1)}, bf16[2,96,768]{2,1,0:T(8,128)(2,1)}, u32[]{:S(2)}, u32[]{:S(2)}) collective-permute-start(bf16[2,96,768]{2,1,0:T(8,128)(2,1)S(1)} %pad_maximum_fusion.14.refs_44_.refs_13_.refs_14_), channel_id=1, source_target_pairs={{0,8},{8,16},{16,24},{24,0},{1,9},{9,17},{17,25},{25,1},{2,10},{10... | collective-permute-start | bytes 884744 | tf_op jit(solution)/shard_map/ppermute | solution.py:100
  62.8 16.9 %collective-permute-start.26 = (bf16[2,96,768]{2,1,0:T(8,128)(2,1)S(1)}, bf16[2,96,768]{2,1,0:T(8,128)(2,1)S(1)}, u32[]{:S(2)}, u32[]{:S(2)}) collective-permute-start(bf16[2,96,768]{2,1,0:T(8,128)(2,1)S(1)} %pad_maximum_fusion.8.refs_20_.refs_13_.refs_16_), channel_id=1, source_target_pairs={{0,2},{2,0},{1,3},{3,1},{4,6},{6,4},{5,7},{7,5},{8,10},{10,8},{9,1... | collective-permute-start | bytes 884744 | tf_op jit(solution)/shard_map/ppermute | solution.py:97
  91.0 36.0 %collective-permute-start = (bf16[256,1536]{1,0:T(8,128)(2,1)}, bf16[256,1536]{1,0:T(8,128)(2,1)S(1)}, u32[]{:S(2)}, u32[]{:S(2)}) collective-permute-start(bf16[256,1536]{1,0:T(8,128)(2,1)} %constant_dynamic-update-slice_fusion), channel_id=1, source_target_pairs={{0,1},{1,0},{2,3},{3,2},{4,5},{5,4},{6,7},{7,6},{8,9},{9,8},{10,11... | collective-permute-start | bytes 2359304 | tf_op jit(solution)/shard_map/ppermute | solution.py:103
  91.1 25.8 %collective-permute-start.19 = (bf16[2,96,768]{2,1,0:T(8,128)(2,1)}, bf16[2,96,768]{2,1,0:T(8,128)(2,1)S(1)}, u32[]{:S(2)}, u32[]{:S(2)}) collective-permute-start(bf16[2,96,768]{2,1,0:T(8,128)(2,1)} %copy-done.38), channel_id=1, source_target_pairs={{0,4},{4,0},{1,5},{5,1},{2,6},{6,2},{3,7},{7,3},{8,12},{12,8},{9,1... | collective-permute-start | bytes 884744 | tf_op jit(solution)/shard_map/ppermute | solution.py:97
  94.2 18.0 %collective-permute-start.43 = (bf16[2,96,768]{2,1,0:T(8,128)(2,1)}, bf16[2,96,768]{2,1,0:T(8,128)(2,1)S(1)}, u32[]{:S(2)}, u32[]{:S(2)}) collective-permute-start(bf16[2,96,768]{2,1,0:T(8,128)(2,1)} %copy-done.59), channel_id=1, source_target_pairs={{0,8},{8,16},{16,24},{24,0},{1,9},{9,17},{17,25},{25,1},{2,10},{10... | collective-permute-start | bytes 884744 | tf_op jit(solution)/shard_map/ppermute | solution.py:100
  94.3 21.0 %collective-permute-start.51 = (bf16[2,96,768]{2,1,0:T(8,128)(2,1)}, bf16[2,96,768]{2,1,0:T(8,128)(2,1)S(1)}, u32[]{:S(2)}, u32[]{:S(2)}) collective-permute-start(bf16[2,96,768]{2,1,0:T(8,128)(2,1)} %collective-permute-done.50.refs_45_.refs_14_.refs_15_), channel_id=1, source_target_pairs={{0,8},{8,16},{16,24},{24,0},{1,9},{9,17},{17,25},{25,1},{2,10},{10... | collective-permute-start | bytes 884744 | tf_op jit(solution)/shard_map/ppermute | solution.py:100
  106.2 24.4 %collective-permute-start.1 = (bf16[256,1536]{1,0:T(8,128)(2,1)}, bf16[256,1536]{1,0:T(8,128)(2,1)S(1)}, u32[]{:S(2)}, u32[]{:S(2)}) collective-permute-start(bf16[256,1536]{1,0:T(8,128)(2,1)} %constant_dynamic-update-slice_fusion.2), channel_id=1, source_target_pairs={{0,1},{1,0},{2,3},{3,2},{4,5},{5,4},{6,7},{7,6},{8,9},{9,8},{10,11... | collective-permute-start | bytes 2359304 | tf_op jit(solution)/shard_map/ppermute | solution.py:103
  127.1 18.3 %collective-permute-start.25 = (bf16[2,96,768]{2,1,0:T(8,128)(2,1)S(1)}, bf16[2,96,768]{2,1,0:T(8,128)(2,1)S(1)}, u32[]{:S(2)}, u32[]{:S(2)}) collective-permute-start(bf16[2,96,768]{2,1,0:T(8,128)(2,1)S(1)} %collective-permute-done.24.refs_22_.refs_15_.refs_18_), channel_id=1, source_target_pairs={{0,8},{8,16},{16,24},{24,0},{1,9},{9,17},{17,25},{25,1},{2,10},{10... | collective-permute-start | bytes 884744 | tf_op jit(solution)/shard_map/ppermute | solution.py:100
  130.6 24.2 %collective-permute-start.20 = (bf16[2,96,768]{2,1,0:T(8,128)(2,1)}, bf16[2,96,768]{2,1,0:T(8,128)(2,1)S(1)}, u32[]{:S(2)}, u32[]{:S(2)}) collective-permute-start(bf16[2,96,768]{2,1,0:T(8,128)(2,1)} %collective-permute-done.16.refs_14_.refs_7_.refs_10_), channel_id=1, source_target_pairs={{0,4},{4,0},{1,5},{5,1},{2,6},{6,2},{3,7},{7,3},{8,12},{12,8},{9,1... | collective-permute-start | bytes 884744 | tf_op jit(solution)/shard_map/ppermute | solution.py:97
  131.7 24.7 %collective-permute-start.28 = (bf16[2,96,768]{2,1,0:T(8,128)(2,1)S(1)}, bf16[2,96,768]{2,1,0:T(8,128)(2,1)S(1)}, u32[]{:S(2)}, u32[]{:S(2)}) collective-permute-start(bf16[2,96,768]{2,1,0:T(8,128)(2,1)S(1)} %collective-permute-done.24.refs_22_.refs_15_.refs_18_), channel_id=1, source_target_pairs={{0,2},{2,0},{1,3},{3,1},{4,6},{6,4},{5,7},{7,5},{8,10},{10,8},{9,1... | collective-permute-start | bytes 884744 | tf_op jit(solution)/shard_map/ppermute | solution.py:97
  133.2 17.1 %collective-permute-start.44 = (bf16[2,96,768]{2,1,0:T(8,128)(2,1)S(1)}, bf16[2,96,768]{2,1,0:T(8,128)(2,1)S(1)}, u32[]{:S(2)}, u32[]{:S(2)}) collective-permute-start(bf16[2,96,768]{2,1,0:T(8,128)(2,1)S(1)} %collective-permute-done.43.refs_38_.refs_7_.refs_8_), channel_id=1, source_target_pairs={{0,8},{8,16},{16,24},{24,0},{1,9},{9,17},{17,25},{25,1},{2,10},{10... | collective-permute-start | bytes 884744 | tf_op jit(solution)/shard_map/ppermute | solution.py:100
  139.0 18.6 %collective-permute-start.47 = (bf16[2,96,768]{2,1,0:T(8,128)(2,1)S(1)}, bf16[2,96,768]{2,1,0:T(8,128)(2,1)S(1)}, u32[]{:S(2)}, u32[]{:S(2)}) collective-permute-start(bf16[2,96,768]{2,1,0:T(8,128)(2,1)S(1)} %collective-permute-done.43.refs_38_.refs_7_.refs_8_), channel_id=1, source_target_pairs={{0,4},{4,0},{1,5},{5,1},{2,6},{6,2},{3,7},{7,3},{8,12},{12,8},{9,1... | collective-permute-start | bytes 884744 | tf_op jit(solution)/shard_map/ppermute | solution.py:97
  270.3 19.4 %collective-permute-start.61 = (bf16[1024,768]{1,0:T(8,128)(2,1)}, bf16[1024,768]{1,0:T(8,128)(2,1)S(1)}, u32[]{:S(2)}, u32[]{:S(2)}) collective-permute-start(bf16[1024,768]{1,0:T(8,128)(2,1)} %get-tuple-element.142.refs_1_), channel_id=1, source_target_pairs={{0,1},{1,0},{2,3},{3,2},{4,5},{5,4},{6,7},{7,6},{8,9},{9,8},{10,11... | collective-permute-start | bytes 4718600 | tf_op jit(solution)/shard_map/ppermute | solution.py:103
  278.3 40.6 %collective-permute-start.63 = (bf16[2,384,768]{2,1,0:T(8,128)(2,1)S(1)}, bf16[2,384,768]{2,1,0:T(8,128)(2,1)S(1)}, u32[]{:S(2)}, u32[]{:S(2)}) collective-permute-start(bf16[2,384,768]{2,1,0:T(8,128)(2,1)S(1)} %get-tuple-element.151.refs_4_), channel_id=1, source_target_pairs={{0,2},{2,0},{1,3},{3,1},{4,6},{6,4},{5,7},{7,5},{8,10},{10,8},{9,1... | collective-permute-start | bytes 3538952 | tf_op jit(solution)/shard_map/ppermute | solution.py:97
  280.0 38.9 %collective-permute-start.64 = (bf16[2,384,768]{2,1,0:T(8,128)(2,1)S(1)}, bf16[2,384,768]{2,1,0:T(8,128)(2,1)S(1)}, u32[]{:S(2)}, u32[]{:S(2)}) collective-permute-start(bf16[2,384,768]{2,1,0:T(8,128)(2,1)S(1)} %get-tuple-element.162), channel_id=1, source_target_pairs={{0,4},{4,0},{1,5},{5,1},{2,6},{6,2},{3,7},{7,3},{8,12},{12,8},{9,1... | collective-permute-start | bytes 3538952 | tf_op jit(solution)/shard_map/ppermute | solution.py:97
  318.8 23.4 %collective-permute-start.62 = (bf16[1024,768]{1,0:T(8,128)(2,1)}, bf16[1024,768]{1,0:T(8,128)(2,1)}, u32[]{:S(2)}, u32[]{:S(2)}) collective-permute-start(bf16[1024,768]{1,0:T(8,128)(2,1)} %get-tuple-element.154.refs_1_), channel_id=1, source_target_pairs={{0,1},{1,0},{2,3},{3,2},{4,5},{5,4},{6,7},{7,6},{8,9},{9,8},{10,11... | collective-permute-start | bytes 4718600 | tf_op jit(solution)/shard_map/ppermute | solution.py:103
  323.1 32.6 %collective-permute-start.66 = (bf16[384,768]{1,0:T(8,128)(2,1)}, bf16[384,768]{1,0:T(8,128)(2,1)}, u32[]{:S(2)}, u32[]{:S(2)}) collective-permute-start(bf16[384,768]{1,0:T(8,128)(2,1)} %get-tuple-element.172), channel_id=1, source_target_pairs={{0,4},{4,0},{1,5},{5,1},{2,6},{6,2},{3,7},{7,3},{8,12},{12,8},{9,1... | collective-permute-start | bytes 1769480 | tf_op jit(solution)/shard_map/ppermute | solution.py:97
  324.0 31.8 %collective-permute-start.67 = (bf16[384,768]{1,0:T(8,128)(2,1)}, bf16[384,768]{1,0:T(8,128)(2,1)}, u32[]{:S(2)}, u32[]{:S(2)}) collective-permute-start(bf16[384,768]{1,0:T(8,128)(2,1)} %get-tuple-element.174), channel_id=1, source_target_pairs={{0,2},{2,0},{1,3},{3,1},{4,6},{6,4},{5,7},{7,5},{8,10},{10,8},{9,1... | collective-permute-start | bytes 1769480 | tf_op jit(solution)/shard_map/ppermute | solution.py:97
  328.7 28.8 %collective-permute-start.71 = (bf16[2,384,384]{2,1,0:T(8,128)(2,1)}, bf16[2,384,384]{2,1,0:T(8,128)(2,1)S(1)}, u32[]{:S(2)}, u32[]{:S(2)}) collective-permute-start(bf16[2,384,384]{2,1,0:T(8,128)(2,1)} %get-tuple-element.165.refs_5_), channel_id=1, source_target_pairs={{0,2},{2,0},{1,3},{3,1},{4,6},{6,4},{5,7},{7,5},{8,10},{10,8},{9,1... | collective-permute-start | bytes 1769480 | tf_op jit(solution)/shard_map/ppermute | solution.py:97
  330.4 27.1 %collective-permute-start.72 = (bf16[2,384,384]{2,1,0:T(8,128)(2,1)}, bf16[2,384,384]{2,1,0:T(8,128)(2,1)S(1)}, u32[]{:S(2)}, u32[]{:S(2)}) collective-permute-start(bf16[2,384,384]{2,1,0:T(8,128)(2,1)} %get-tuple-element.181), channel_id=1, source_target_pairs={{0,4},{4,0},{1,5},{5,1},{2,6},{6,2},{3,7},{7,3},{8,12},{12,8},{9,1... | collective-permute-start | bytes 1769480 | tf_op jit(solution)/shard_map/ppermute | solution.py:97
  358.7 16.9 %collective-permute-start.74 = (bf16[384,384]{1,0:T(8,128)(2,1)S(1)}, bf16[384,384]{1,0:T(8,128)(2,1)S(1)}, u32[]{:S(2)}, u32[]{:S(2)}) collective-permute-start(bf16[384,384]{1,0:T(8,128)(2,1)S(1)} %get-tuple-element.185), channel_id=1, source_target_pairs={{0,2},{2,0},{1,3},{3,1},{4,6},{6,4},{5,7},{7,5},{8,10},{10,8},{9,1... | collective-permute-start | bytes 884744 | tf_op jit(solution)/shard_map/ppermute | solution.py:97
  359.1 18.5 %collective-permute-start.68 = (bf16[2,96,768]{2,1,0:T(8,128)(2,1)S(1)}, bf16[2,96,768]{2,1,0:T(8,128)(2,1)S(1)}, u32[]{:S(2)}, u32[]{:S(2)}) collective-permute-start(bf16[2,96,768]{2,1,0:T(8,128)(2,1)S(1)} %get-tuple-element.177), channel_id=1, source_target_pairs={{0,24},{8,0},{16,8},{24,16},{1,25},{9,1},{17,9},{25,17},{2,26},{10... | collective-permute-start | bytes 884744 | tf_op jit(solution)/shard_map/ppermute | solution.py:279
  359.5 24.8 %collective-permute-start.69 = (bf16[2,96,768]{2,1,0:T(8,128)(2,1)S(1)}, bf16[2,96,768]{2,1,0:T(8,128)(2,1)S(1)}, u32[]{:S(2)}, u32[]{:S(2)}) collective-permute-start(bf16[2,96,768]{2,1,0:T(8,128)(2,1)S(1)} %get-tuple-element.178), channel_id=1, source_target_pairs={{0,16},{8,24},{16,0},{24,8},{1,17},{9,25},{17,1},{25,9},{2,18},{10... | collective-permute-start | bytes 884744 | tf_op jit(solution)/shard_map/ppermute | solution.py:279
  359.7 24.7 %collective-permute-start.65 = (bf16[1024,768]{1,0:T(8,128)(2,1)S(1)}, bf16[1024,768]{1,0:T(8,128)(2,1)}, u32[]{:S(2)}, u32[]{:S(2)}) collective-permute-start(bf16[1024,768]{1,0:T(8,128)(2,1)S(1)} %copy-done.193), channel_id=1, source_target_pairs={{0,1},{1,0},{2,3},{3,2},{4,5},{5,4},{6,7},{7,6},{8,9},{9,8},{10,11... | collective-permute-start | bytes 4718600 | tf_op jit(solution)/shard_map/ppermute | solution.py:103
  366.2 18.0 %collective-permute-start.70 = (bf16[2,96,768]{2,1,0:T(8,128)(2,1)S(1)}, bf16[2,96,768]{2,1,0:T(8,128)(2,1)S(1)}, u32[]{:S(2)}, u32[]{:S(2)}) collective-permute-start(bf16[2,96,768]{2,1,0:T(8,128)(2,1)S(1)} %get-tuple-element.179), channel_id=1, source_target_pairs={{0,8},{8,16},{16,24},{24,0},{1,9},{9,17},{17,25},{25,1},{2,10},{10... | collective-permute-start | bytes 884744 | tf_op jit(solution)/shard_map/ppermute | solution.py:279
  375.7 57.5 %collective-permute-start.76 = (bf16[2,384,768]{2,1,0:T(8,128)(2,1)}, bf16[2,384,768]{2,1,0:T(8,128)(2,1)S(1)}, u32[]{:S(2)}, u32[]{:S(2)}) collective-permute-start(bf16[2,384,768]{2,1,0:T(8,128)(2,1)} %get-tuple-element.190.refs_4_), channel_id=1, source_target_pairs={{0,2},{2,0},{1,3},{3,1},{4,6},{6,4},{5,7},{7,5},{8,10},{10,8},{9,1... | collective-permute-start | bytes 3538952 | tf_op jit(solution)/shard_map/ppermute | solution.py:97
  377.6 57.7 %collective-permute-start.77 = (bf16[2,384,768]{2,1,0:T(8,128)(2,1)}, bf16[2,384,768]{2,1,0:T(8,128)(2,1)}, u32[]{:S(2)}, u32[]{:S(2)}) collective-permute-start(bf16[2,384,768]{2,1,0:T(8,128)(2,1)} %get-tuple-element.201), channel_id=1, source_target_pairs={{0,4},{4,0},{1,5},{5,1},{2,6},{6,2},{3,7},{7,3},{8,12},{12,8},{9,1... | collective-permute-start | bytes 3538952 | tf_op jit(solution)/shard_map/ppermute | solution.py:97
  431.8 14.4 %collective-permute-start.83 = (bf16[2,96,384]{2,1,0:T(8,128)(2,1)S(1)}, bf16[2,96,384]{2,1,0:T(8,128)(2,1)S(1)}, u32[]{:S(2)}, u32[]{:S(2)}) collective-permute-start(bf16[2,96,384]{2,1,0:T(8,128)(2,1)S(1)} %copy-done.112), channel_id=1, source_target_pairs={{0,16},{8,24},{16,0},{24,8},{1,17},{9,25},{17,1},{25,9},{2,18},{10... | collective-permute-start | bytes 442376 | tf_op jit(solution)/shard_map/ppermute | solution.py:279
  433.2 13.9 %collective-permute-start.84 = (bf16[2,96,384]{2,1,0:T(8,128)(2,1)S(1)}, bf16[2,96,384]{2,1,0:T(8,128)(2,1)S(1)}, u32[]{:S(2)}, u32[]{:S(2)}) collective-permute-start(bf16[2,96,384]{2,1,0:T(8,128)(2,1)S(1)} %get-tuple-element.213), channel_id=1, source_target_pairs={{0,8},{8,16},{16,24},{24,0},{1,9},{9,17},{17,25},{25,1},{2,10},{10... | collective-permute-start | bytes 442376 | tf_op jit(solution)/shard_map/ppermute | solution.py:279
  437.6 16.3 %collective-permute-start.80 = (bf16[384,768]{1,0:T(8,128)(2,1)S(1)}, bf16[384,768]{1,0:T(8,128)(2,1)S(1)}, u32[]{:S(2)}, u32[]{:S(2)}) collective-permute-start(bf16[384,768]{1,0:T(8,128)(2,1)S(1)} %get-tuple-element.208), channel_id=1, source_target_pairs={{0,4},{4,0},{1,5},{5,1},{2,6},{6,2},{3,7},{7,3},{8,12},{12,8},{9,1... | collective-permute-start | bytes 1769480 | tf_op jit(solution)/shard_map/ppermute | solution.py:97
  442.5 16.3 %collective-permute-start.81 = (bf16[384,768]{1,0:T(8,128)(2,1)S(1)}, bf16[384,768]{1,0:T(8,128)(2,1)S(1)}, u32[]{:S(2)}, u32[]{:S(2)}) collective-permute-start(bf16[384,768]{1,0:T(8,128)(2,1)S(1)} %get-tuple-element.210), channel_id=1, source_target_pairs={{0,2},{2,0},{1,3},{3,1},{4,6},{6,4},{5,7},{7,5},{8,10},{10,8},{9,1... | collective-permute-start | bytes 1769480 | tf_op jit(solution)/shard_map/ppermute | solution.py:97
  446.2 22.5 %collective-permute-start.78 = (bf16[2,384,384]{2,1,0:T(8,128)(2,1)S(1)}, bf16[2,384,384]{2,1,0:T(8,128)(2,1)S(1)}, u32[]{:S(2)}, u32[]{:S(2)}) collective-permute-start(bf16[2,384,384]{2,1,0:T(8,128)(2,1)S(1)} %get-tuple-element.204.refs_5_), channel_id=1, source_target_pairs={{0,2},{2,0},{1,3},{3,1},{4,6},{6,4},{5,7},{7,5},{8,10},{10,8},{9,1... | collective-permute-start | bytes 1769480 | tf_op jit(solution)/shard_map/ppermute | solution.py:97
  447.1 21.6 %collective-permute-start.79 = (bf16[2,384,384]{2,1,0:T(8,128)(2,1)S(1)}, bf16[2,384,384]{2,1,0:T(8,128)(2,1)S(1)}, u32[]{:S(2)}, u32[]{:S(2)}) collective-permute-start(bf16[2,384,384]{2,1,0:T(8,128)(2,1)S(1)} %get-tuple-element.207), channel_id=1, source_target_pairs={{0,4},{4,0},{1,5},{5,1},{2,6},{6,2},{3,7},{7,3},{8,12},{12,8},{9,1... | collective-permute-start | bytes 1769480 | tf_op jit(solution)/shard_map/ppermute | solution.py:97
  447.5 71.1 %collective-permute-start.75 = (bf16[1024,768]{1,0:T(8,128)(2,1)}, bf16[1024,768]{1,0:T(8,128)(2,1)}, u32[]{:S(2)}, u32[]{:S(2)}) collective-permute-start(bf16[1024,768]{1,0:T(8,128)(2,1)} %get-tuple-element.195), channel_id=1, source_target_pairs={{0,1},{1,0},{2,3},{3,2},{4,5},{5,4},{6,7},{7,6},{8,9},{9,8},{10,11... | collective-permute-start | bytes 4718600 | tf_op jit(solution)/shard_map/ppermute | solution.py:103
  453.9 17.7 %collective-permute-start.96 = (f32[92,128]{1,0:T(8,128)S(1)}, f32[92,128]{1,0:T(8,128)S(1)}, u32[]{:S(2)}, u32[]{:S(2)}) collective-permute-start(f32[92,128]{1,0:T(8,128)S(1)} %add.326), channel_id=1, source_target_pairs={{0,16},{8,24},{16,0},{24,8},{1,17},{9,25},{17,1},{25,9},{2,18},{10... | collective-permute-start | bytes 141320 | tf_op jit(solution)/shard_map/ppermute | solution.py:164
  480.5 14.2 %collective-permute-start.88 = (bf16[2,96,384]{2,1,0:T(8,128)(2,1)S(1)}, bf16[2,96,384]{2,1,0:T(8,128)(2,1)S(1)}, u32[]{:S(2)}, u32[]{:S(2)}) collective-permute-start(bf16[2,96,384]{2,1,0:T(8,128)(2,1)S(1)} %get-tuple-element.222), channel_id=1, source_target_pairs={{0,16},{8,24},{16,0},{24,8},{1,17},{9,25},{17,1},{25,9},{2,18},{10... | collective-permute-start | bytes 442376 | tf_op jit(solution)/shard_map/ppermute | solution.py:279
  482.1 27.4 %collective-permute-start.90 = (bf16[2,96,768]{2,1,0:T(8,128)(2,1)}, bf16[2,96,768]{2,1,0:T(8,128)(2,1)S(1)}, u32[]{:S(2)}, u32[]{:S(2)}) collective-permute-start(bf16[2,96,768]{2,1,0:T(8,128)(2,1)} %get-tuple-element.227), channel_id=1, source_target_pairs={{0,24},{8,0},{16,8},{24,16},{1,25},{9,1},{17,9},{25,17},{2,26},{10... | collective-permute-start | bytes 884744 | tf_op jit(solution)/shard_map/ppermute | solution.py:279
  483.4 33.4 %collective-permute-start.91 = (bf16[2,96,768]{2,1,0:T(8,128)(2,1)}, bf16[2,96,768]{2,1,0:T(8,128)(2,1)S(1)}, u32[]{:S(2)}, u32[]{:S(2)}) collective-permute-start(bf16[2,96,768]{2,1,0:T(8,128)(2,1)} %get-tuple-element.228), channel_id=1, source_target_pairs={{0,16},{8,24},{16,0},{24,8},{1,17},{9,25},{17,1},{25,9},{2,18},{10... | collective-permute-start | bytes 884744 | tf_op jit(solution)/shard_map/ppermute | solution.py:279
  486.3 30.5 %collective-permute-start.92 = (bf16[2,96,768]{2,1,0:T(8,128)(2,1)S(1)}, bf16[2,96,768]{2,1,0:T(8,128)(2,1)S(1)}, u32[]{:S(2)}, u32[]{:S(2)}) collective-permute-start(bf16[2,96,768]{2,1,0:T(8,128)(2,1)S(1)} %get-tuple-element.229), channel_id=1, source_target_pairs={{0,8},{8,16},{16,24},{24,0},{1,9},{9,17},{17,25},{25,1},{2,10},{10... | collective-permute-start | bytes 884744 | tf_op jit(solution)/shard_map/ppermute | solution.py:279
  (248 other events, 3829.9 us)
